TPU v7x, 32 devices: a whole 2x2x4 slice. The times are simulated.
32 devices in a mesh: row: 8 (over y, x, core), col: 4 (over z).
Axes of the slice: x: 2, y: 2, z: 4, core: 2. Of those that a mesh axis runs over, the one named last changes fastest.
Arguments:
- kernel: float32 [1, 2048, 2, 1024], P(None, 'row', None, 'col'), may hold values from 0 to 1.5, as said below
Outputs:
- factored: float32 [1, 2048, 2, 1024], P(None, 'row', None, 'col')
Inputs may be any that keep to these rules, and one draw needn't show every extreme that they name: kernel is symmetric and positive definite with all eigenvalues at least about 0.5 (up to float32 rounding of the draw); its entries lie between 0 and 1.5.
All inputs are finite; a program needn't handle non-finite values.
Results may differ from a plain program's by a relative error of at most 0.0003.
Values sent between devices are 32-bit elements; how exact they have to be, the bound alone decides.
No kernel may reach another device: no remote copies, remote signals or barrier semaphores. Data moves between devices by JAX's collectives and lax.ppermute only.
A program may use at most 64 MiB of HBM per device.

v0:
```python
import jax
import jax.numpy as jnp
from jax import lax
from jax.sharding import PartitionSpec as P

PANELS = 3


def broadcast(value, axis, source):
    kept = jnp.where(lax.axis_index(axis) == source, value, 0).astype(value.dtype)
    return lax.psum(kept, axis)


def solve_rows(factor, blocks):
    count, height, width = blocks.shape
    flat = blocks.reshape(count * height, factor.shape[0])
    solved = lax.linalg.triangular_solve(
        factor, flat, left_side=False, lower=True, transpose_a=True
    )
    return solved.reshape(count, height, factor.shape[0])


def keep_after(blocks, block_ids, step):
    return jnp.where((block_ids > step)[:, None, None], blocks, jnp.float32(0.0))


def subtract(target, rows_here, cols_here):
    return target - jnp.einsum(
        "aik,bjk->aibj", rows_here, cols_here, precision=lax.Precision.HIGHEST
    )


def apply_update(matrix, rows_here, cols_here):
    return subtract(matrix, rows_here, cols_here)


def shards(kernel):
    blocks_r, width, blocks_c, _ = kernel.shape
    n_row = lax.axis_size("row")
    n_col = lax.axis_size("col")
    ratio = n_row // n_col
    row_pos = lax.axis_index("row")
    col_pos = lax.axis_index("col")
    row_ids = jnp.arange(blocks_r, dtype=jnp.int32) * n_row + row_pos
    col_ids = jnp.arange(blocks_c, dtype=jnp.int32) * n_col + col_pos
    identity = jnp.eye(width, dtype=jnp.float32)
    matrix = kernel
    for step in range(PANELS):
        corner = broadcast(matrix[0, :, 0, :], "row", step)
        corner = jnp.where(col_pos == step, corner, identity)
        factor = jnp.linalg.cholesky(corner)
        solved = solve_rows(factor, matrix[:, :, 0, :])
        rows_here = broadcast(keep_after(solved, row_ids, step), "col", step)
        pieces = []
        for member in range(ratio):
            pieces.append(broadcast(rows_here, "row", col_pos + member * n_col))
        cols_here = jnp.stack(pieces, axis=1).reshape(blocks_c, width, width)
        matrix = apply_update(matrix, rows_here, cols_here)
        ids = row_ids[:, None, None]
        new_panel = jnp.where(
            ids < step, jnp.float32(0.0), jnp.where(ids == step, factor[None, :, :], solved)
        )
        column = jnp.where(col_pos == step, new_panel, matrix[:, :, 0, :])
        matrix = matrix.at[:, :, 0, :].set(column)
    upper = (row_ids < PANELS)[:, None, None, None] & (col_ids >= PANELS)[None, None, :, None]
    return jnp.where(upper, jnp.float32(0.0), matrix)


def solution(mesh):
    in_specs = (P(None, "row", None, "col"),)
    out_specs = P(None, "row", None, "col")
    return jax.shard_map(shards, mesh=mesh, in_specs=in_specs, out_specs=out_specs, check_vma=False)
```

profile of v0, /device:TPU:13, one launch (start us, length us, event | category | flops | bytes accessed | tf_op | source)
XLA Modules:
  0.0 664.1 jit_solution(663324007558444433)
XLA Ops:
  8.6 54.7 %all-reduce.14.cloned.1.call-done = f32[256,256]{0,1:T(8,128)} async-done(((f32[256,256]{0,1:T(8,128)}), f32[256,256]{0,1:T(8,128)}) %all-reduce.14.cloned.1.call-update) | async-done | bytes 262160 | tf_op jit(solution)/shard_map/psum | solution.py:11
  64.4 11.7 %cholesky.172 = f32[128,128]{1,0:T(8,128)S(1)} custom-call(f32[128,128]{1,0:T(8,128)S(1)} %cholesky.270), custom_call_target="Cholesky" | custom-call | tf_op jit(solution)/shard_map/jit(cholesky)/cholesky | solution.py:51
  76.2 9.8 %custom-call.15 = f32[1,128,128]{1,2,0:T(8,128)S(1)} custom-call(f32[1,128,128]{2,1,0:T(8,128)S(1)} %get-tuple-element.129), custom_call_target="InvertDiagBlocksLowerTriangular" | custom-call | tf_op jit(solution)/shard_map/jit(cholesky)/cholesky | solution.py:51
  86.6 11.7 %cholesky.189 = f32[128,128]{1,0:T(8,128)S(1)} custom-call(f32[128,128]{1,0:T(8,128)S(1)} %convolution_subtract_fusion.5), custom_call_target="Cholesky" | custom-call | tf_op jit(solution)/shard_map/jit(cholesky)/cholesky | solution.py:51
  100.7 4.6 while.9
  101.6 1.4 dynamic-slice.44
  105.3 19.7 %custom-call.16 = f32[2,128,128]{1,2,0:T(8,128)S(1)} custom-call(f32[2,128,128]{2,1,0:T(8,128)S(1)} %get-tuple-element.63), custom_call_target="InvertDiagBlocksLowerTriangular" | custom-call | tf_op jit(solution)/shard_map/triangular_solve/custom-call.0 | solution.py:17
  126.8 35.0 %all-reduce.16.cloned.1.call-done = f32[1,256,256]{1,2,0:T(8,128)} async-done(((f32[1,256,256]{1,2,0:T(8,128)}), f32[1,256,256]{1,2,0:T(8,128)}) %all-reduce.16.cloned.1.call-update) | async-done | bytes 262160 | tf_op jit(solution)/shard_map/psum | solution.py:11
  161.8 1.8 select_bitcast_fusion.7
  163.7 55.3 %all-reduce.30.cloned.1.call-done = (f32[1,1,256,256]{2,3,1,0:T(8,128)}, f32[1,1,256,256]{2,3,1,0:T(8,128)}) async-done(((f32[1,1,256,256]{2,3,1,0:T(8,128)}, f32[1,1,256,256]{2,3,1,0:T(8,128)}), (f32[1,1,256,256]{2,3,1,0:T(8,128)}, f32[1,1,256,256]{2,3,1,0:T(8,128)})) %all-reduce.30.cloned.1.call-update) | async-done | bytes 524304 | tf_op jit(solution)/shard_map/psum | solution.py:11
  219.0 2.0 fusion
  221.9 53.3 %all-reduce.18.cloned.1.call-done = f32[256,256]{0,1:T(8,128)} async-done(((f32[256,256]{0,1:T(8,128)}), f32[256,256]{0,1:T(8,128)}) %all-reduce.18.cloned.1.call-update) | async-done | bytes 262160 | tf_op jit(solution)/shard_map/psum | solution.py:11
  277.2 11.7 %cholesky.206 = f32[128,128]{1,0:T(8,128)S(1)} custom-call(f32[128,128]{1,0:T(8,128)S(1)} %cholesky.273), custom_call_target="Cholesky" | custom-call | tf_op jit(solution)/shard_map/jit(cholesky)/cholesky | solution.py:51
  289.1 9.8 %custom-call.17 = f32[1,128,128]{1,2,0:T(8,128)S(1)} custom-call(f32[1,128,128]{2,1,0:T(8,128)S(1)} %get-tuple-element.127), custom_call_target="InvertDiagBlocksLowerTriangular" | custom-call | tf_op jit(solution)/shard_map/jit(cholesky)/cholesky | solution.py:51
  299.5 11.7 %cholesky.223 = f32[128,128]{1,0:T(8,128)S(1)} custom-call(f32[128,128]{1,0:T(8,128)S(1)} %convolution_subtract_fusion.4), custom_call_target="Cholesky" | custom-call | tf_op jit(solution)/shard_map/jit(cholesky)/cholesky | solution.py:51
  314.1 14.8 %while.10 = (s32[]{:T(128)}, f32[256,256]{0,1:T(8,128)S(1)}, s32[2,2]{1,0:T(2,128)S(1)}, f32[2,128,128]{2,1,0:T(8,128)S(1)}, s32[]{:T(128)}) while((s32[]{:T(128)}, f32[256,256]{0,1:T(8,128)S(1)}, s32[2,2]{1,0:T(2,128)S(1)}, f32[2,128,128]{2,1,0:T(8,128)S(1)}, s32[]{:T(128)}) %tuple.104), condition=%wide.while_cond.3.clone, body=%wide.while_body.3.clone.sunk | while | flops 2 | bytes 393329 | solution.py:17
  327.4 1.4 dynamic-slice.46
  329.0 19.7 %custom-call.18 = f32[2,128,128]{1,2,0:T(8,128)S(1)} custom-call(f32[2,128,128]{2,1,0:T(8,128)S(1)} %get-tuple-element.64), custom_call_target="InvertDiagBlocksLowerTriangular" | custom-call | tf_op jit(solution)/shard_map/triangular_solve/custom-call.0 | solution.py:17
  350.4 34.1 %all-reduce.20.cloned.1.call-done = f32[1,256,256]{1,2,0:T(8,128)} async-done(((f32[1,256,256]{1,2,0:T(8,128)}), f32[1,256,256]{1,2,0:T(8,128)}) %all-reduce.20.cloned.1.call-update) | async-done | bytes 262160 | tf_op jit(solution)/shard_map/psum | solution.py:11
  384.6 1.8 select_bitcast_fusion.4
  386.5 55.4 %all-reduce.28.cloned.1.call-done = (f32[1,1,256,256]{2,3,1,0:T(8,128)}, f32[1,1,256,256]{2,3,1,0:T(8,128)}) async-done(((f32[1,1,256,256]{2,3,1,0:T(8,128)}, f32[1,1,256,256]{2,3,1,0:T(8,128)}), (f32[1,1,256,256]{2,3,1,0:T(8,128)}, f32[1,1,256,256]{2,3,1,0:T(8,128)})) %all-reduce.28.cloned.1.call-update) | async-done | bytes 524304 | tf_op jit(solution)/shard_map/psum | solution.py:11
  441.9 2.0 fusion.1
  444.8 53.1 %all-reduce.22.cloned.1.call-done = f32[256,256]{0,1:T(8,128)} async-done(((f32[256,256]{0,1:T(8,128)}), f32[256,256]{0,1:T(8,128)}) %all-reduce.22.cloned.1.call-update) | async-done | bytes 262160 | tf_op jit(solution)/shard_map/psum | solution.py:11
  499.0 11.7 %cholesky.240 = f32[128,128]{1,0:T(8,128)S(1)} custom-call(f32[128,128]{1,0:T(8,128)S(1)} %cholesky.276), custom_call_target="Cholesky" | custom-call | tf_op jit(solution)/shard_map/jit(cholesky)/cholesky | solution.py:51
  510.8 9.8 %custom-call.19 = f32[1,128,128]{1,2,0:T(8,128)S(1)} custom-call(f32[1,128,128]{2,1,0:T(8,128)S(1)} %get-tuple-element.125), custom_call_target="InvertDiagBlocksLowerTriangular" | custom-call | tf_op jit(solution)/shard_map/jit(cholesky)/cholesky | solution.py:51
  521.2 11.7 %cholesky.257 = f32[128,128]{1,0:T(8,128)S(1)} custom-call(f32[128,128]{1,0:T(8,128)S(1)} %convolution_subtract_fusion.3), custom_call_target="Cholesky" | custom-call | tf_op jit(solution)/shard_map/jit(cholesky)/cholesky | solution.py:51
  535.9 4.6 while.11
  540.4 19.7 %custom-call.20 = f32[2,128,128]{1,2,0:T(8,128)S(1)} custom-call(f32[2,128,128]{2,1,0:T(8,128)S(1)} %get-tuple-element.65), custom_call_target="InvertDiagBlocksLowerTriangular" | custom-call | tf_op jit(solution)/shard_map/triangular_solve/custom-call.0 | solution.py:17
  561.9 35.1 %all-reduce.24.cloned.1.call-done = f32[1,256,256]{1,2,0:T(8,128)} async-done(((f32[1,256,256]{1,2,0:T(8,128)}), f32[1,256,256]{1,2,0:T(8,128)}) %all-reduce.24.cloned.1.call-update) | async-done | bytes 262160 | tf_op jit(solution)/shard_map/psum | solution.py:11
  596.9 1.8 select_bitcast_fusion.1
  598.8 55.3 %all-reduce.26.cloned.1.call-done = (f32[1,1,256,256]{2,3,1,0:T(8,128)}, f32[1,1,256,256]{2,3,1,0:T(8,128)}) async-done(((f32[1,1,256,256]{2,3,1,0:T(8,128)}, f32[1,1,256,256]{2,3,1,0:T(8,128)}), (f32[1,1,256,256]{2,3,1,0:T(8,128)}, f32[1,1,256,256]{2,3,1,0:T(8,128)})) %all-reduce.26.cloned.1.call-update) | async-done | bytes 524304 | tf_op jit(solution)/shard_map/psum | solution.py:11
  654.1 2.0 fusion.2
  (136 shorter events, 30.4 us)
Async XLA Ops:
  6.5 56.8 %all-reduce.14.cloned.1.call-start = ((), (), s32[]{:S(2)}) async-start(), calls=%async_computation | async-start | bytes 524288 | tf_op jit(solution)/shard_map/psum | solution.py:11
  8.5 153.3 %all-reduce.16.cloned.1.call-start = ((), (), s32[]{:S(2)}) async-start(), calls=%async_computation.1 | async-start | bytes 524288 | tf_op jit(solution)/shard_map/psum | solution.py:11
  63.4 1.0 copy-start.3
  126.8 92.3 %all-reduce.30.cloned.1.call-start = ((), (), s32[]{:S(2)}) async-start(), calls=%async_computation.8 | async-start | bytes 1048576 | tf_op jit(solution)/shard_map/psum | solution.py:11
  163.6 55.4 %copy-start.1 = (f32[1,256,256]{1,2,0:T(8,128)S(1)}, f32[1,256,256]{1,2,0:T(8,128)}, u32[]{:S(2)}) copy-start(f32[1,256,256]{1,2,0:T(8,128)} %all-reduce.16.cloned.1.call-done) | copy-start | bytes 786436
  163.7 111.6 %all-reduce.18.cloned.1.call-start = ((), (), s32[]{:S(2)}) async-start(), calls=%async_computation.2 | async-start | bytes 524288 | tf_op jit(solution)/shard_map/psum | solution.py:11
  221.9 162.7 %all-reduce.20.cloned.1.call-start = ((), (), s32[]{:S(2)}) async-start(), calls=%async_computation.3 | async-start | bytes 524288 | tf_op jit(solution)/shard_map/psum | solution.py:11
  276.2 1.0 copy-start.4
  350.4 91.5 %all-reduce.28.cloned.1.call-start = ((), (), s32[]{:S(2)}) async-start(), calls=%async_computation.7 | async-start | bytes 1048576 | tf_op jit(solution)/shard_map/psum | solution.py:11
  386.4 111.5 %all-reduce.22.cloned.1.call-start = ((), (), s32[]{:S(2)}) async-start(), calls=%async_computation.4 | async-start | bytes 524288 | tf_op jit(solution)/shard_map/psum | solution.py:11
  386.4 55.5 %copy-start.2 = (f32[1,256,256]{1,2,0:T(8,128)S(1)}, f32[1,256,256]{1,2,0:T(8,128)}, u32[]{:S(2)}) copy-start(f32[1,256,256]{1,2,0:T(8,128)} %all-reduce.20.cloned.1.call-done) | copy-start | bytes 786436
  444.7 152.2 %all-reduce.24.cloned.1.call-start = ((), (), s32[]{:S(2)}) async-start(), calls=%async_computation.5 | async-start | bytes 524288 | tf_op jit(solution)/shard_map/psum | solution.py:11
  498.0 1.0 copy-start.5
  561.8 92.3 %all-reduce.26.cloned.1.call-start = ((), (), s32[]{:S(2)}) async-start(), calls=%async_computation.6 | async-start | bytes 1048576 | tf_op jit(solution)/shard_map/psum | solution.py:11
  598.8 55.4 %copy-start = (f32[1,256,256]{1,2,0:T(8,128)S(1)}, f32[1,256,256]{1,2,0:T(8,128)}, u32[]{:S(2)}) copy-start(f32[1,256,256]{1,2,0:T(8,128)} %all-reduce.24.cloned.1.call-done) | copy-start | bytes 786436
Sparse Core Ops, SparseCore 0:
  10.4 52.8 all-reduce.13
  126.9 34.9 all-reduce.15
  165.0 53.9 all-reduce.29
  222.2 52.9 all-reduce.17
  350.5 34.0 all-reduce.19
  387.9 53.9 all-reduce.27
  445.0 52.9 all-reduce.21
  562.0 34.9 all-reduce.23
  600.1 53.9 all-reduce.25
where the time goes:
time: 671 us; the launch traced here: 664 us
  waiting for transfers between devices  432 us (64%)
  other arithmetic  174 us (26%)
  local copies, waits for them, and re-layouts  18.9 us (3%)
  between operations  18.1 us (3%)
  loops' own time  11.2 us (2%)
  matrix products  10.3 us (2%)
    psum x9, waiting for transfers between devices, broadcast(): return lax.psum(kept, axis)  431 us
    another operation x20, other arithmetic, shards(): factor = jnp.linalg.cholesky(corner)  103 us
    another operation x7, other arithmetic, solve_rows(): lax.linalg.triangular_solve(factor, flat, left_side=False, lower=True, tr...  59.1 us
  transfers between devices with their start and end apart: 9, of which 9 were waited for; matrix products, arithmetic and copies ran while one was open for 0% of the time, Pallas kernels for 0%

commit v1 on v0

v1 whole, which is shorter than its diff:
```python
import jax
import jax.numpy as jnp
from jax import lax
from jax.experimental import pallas as pl
from jax.experimental.pallas import tpu as pltpu
from jax.sharding import PartitionSpec as P

PANELS = 3
HALF = 128
GROUPS = HALF // 8
NN = (((1,), (0,)), ((), ()))
NT = (((1,), (1,)), ((), ()))


def lane_b(x, j):
    return jnp.broadcast_to(x[:, j:j + 1], (8, 128))


def sub_b(x, t):
    return jnp.broadcast_to(x[t:t + 1, :], x.shape)


def wide(x):
    return jnp.concatenate([x, x], axis=1)


def split(x):
    high = x.astype(jnp.bfloat16)
    low = (x - high.astype(jnp.float32)).astype(jnp.bfloat16)
    return high, low


def mm(a, b, dims):
    dot = lambda u, v: lax.dot_general(u, v, dims, preferred_element_type=jnp.float32)
    return dot(a[0], b[0]) + (dot(a[0], b[1]) + dot(a[1], b[0]))


def eliminate(rows, count):
    iota = lax.broadcasted_iota(jnp.int32, (8, 128), 0)
    rows = list(rows)
    out = []
    ahead = None
    for b in range(count):
        k = 8 * b
        cols = {g: [lane_b(rows[g], k + j) for j in range(8)] for g in range(b, count) if g > b or ahead is None}
        if ahead is not None:
            cols[b] = ahead
        ahead = None
        if b + 1 < count:
            ahead = [lane_b(rows[b + 1], k + 8 + j) for j in range(8)]
        da = jnp.ones((8, 128), jnp.float32)
        db = jnp.zeros((8, 128), jnp.float32)
        dc = jnp.ones((8, 128), jnp.float32)
        pp = jnp.zeros((8, 256), jnp.float32)
        for t in range(0, 8, 2):
            first = {j: sub_b(cols[b][j], t) for j in range(t, 8)}
            second = {j: sub_b(cols[b][j], t + 1) for j in range(t + 1, 8)}
            a, q, c = first[t], first[t + 1], second[t + 1]
            rd = 1.0 / (a * c - q * q)
            da = jnp.where((iota == t) | (iota == t + 1), a, da)
            db = jnp.where(iota == t + 1, q, db)
            dc = jnp.where(iota == t + 1, c, dc)
            p0, p1 = sub_b(rows[b], t), sub_b(rows[b], t + 1)
            pp = jnp.where(wide(iota == t + 1), p0, pp)
            for g in range(b, count):
                if g == b and t == 6:
                    continue
                c0, c1 = cols[g][t], cols[g][t + 1]
                n0, n1 = c0 * c - c1 * q, c1 * a - c0 * q
                if g == b:
                    n0 = jnp.where(iota > t + 1, n0, 0.0)
                    n1 = jnp.where(iota > t + 1, n1, 0.0)
                m0, m1 = n0 * rd, n1 * rd
                rows[g] = rows[g] - (wide(m0) * p0 + wide(m1) * p1)
                for j in range(t + 2, 8):
                    cols[g][j] = cols[g][j] - (m0 * first[j] + m1 * second[j])
                if g == b + 1:
                    for j in range(8):
                        ahead[j] = ahead[j] - (m0 * sub_b(c0, j) + m1 * sub_b(c1, j))
        odd = (iota % 2) == 1
        f = jnp.where(odd, db / da, 0.0)
        piv = jnp.where(odd, dc - db * f, da)
        out.append((rows[b] - wide(f) * pp) * wide(lax.rsqrt(piv)))
    return out


def factor_half(aug):
    rows = eliminate([aug[8 * g:8 * g + 8, :] for g in range(GROUPS)], GROUPS)
    for g in range(GROUPS):
        aug[8 * g:8 * g + 8, :] = rows[g]


def factor_panel(block, aug, inverse):
    r = lax.broadcasted_iota(jnp.int32, (HALF, HALF), 0)
    c = lax.broadcasted_iota(jnp.int32, (HALF, HALF), 1)
    eye = jnp.where(r == c, 1.0, 0.0).astype(jnp.float32)
    aug[:, :HALF] = block[:HALF, :HALF]
    aug[:, HALF:] = eye
    factor_half(aug)
    w0 = aug[:, HALF:]
    sw0 = split(w0)
    side = split(block[HALF:, :HALF])
    low = split(mm(side, sw0, NT))
    up = split(mm(sw0, side, NT))
    aug[:, :HALF] = block[HALF:, HALF:] - mm(low, up, NN)
    aug[:, HALF:] = eye
    factor_half(aug)
    w1 = aug[:, HALF:]
    corner = mm(split(w1), split(mm(low, sw0, NN)), NN)
    inverse[:HALF, :HALF] = w0
    inverse[:HALF, HALF:] = jnp.zeros((HALF, HALF), jnp.float32)
    inverse[HALF:, :HALF] = -corner
    inverse[HALF:, HALF:] = w1


def panels_kernel(place, mine_ref, other_ref, own_ref, *refs):
    n_side = len(refs) - 9
    side_refs = refs[:n_side]
    right_ref, top_ref, out_ref, lead, row, aug, inverse, block, work = refs[n_side:]
    p, c, n_col = place[0], place[1], place[2]
    core = lax.rem(p, 2)
    for b in range(6):
        lead[b, pl.ds(pl.multiple_of(core * HALF, HALF), HALF), :] = mine_ref[b]
        lead[b, pl.ds(pl.multiple_of((1 - core) * HALF, HALF), HALF), :] = other_ref[b]
    row[c] = own_ref[...]
    for d in range(n_side):
        row[lax.bitwise_xor(c, d + 1)] = side_refs[d][...]

    block[...] = lead[0]
    factor_panel(block, aug, inverse)
    w0 = split(inverse[...])
    s10, s20 = split(lead[1]), split(lead[3])
    l10, l20 = split(mm(s10, w0, NT)), split(mm(s20, w0, NT))
    u01, u02 = split(mm(w0, s10, NT)), split(mm(w0, s20, NT))
    block[...] = lead[2] - mm(l10, u01, NN)
    factor_panel(block, aug, inverse)
    w1 = split(inverse[...])
    s21 = split(lead[4] - mm(l20, u01, NN))
    l21, u12 = split(mm(s21, w1, NT)), split(mm(w1, s21, NT))
    block[...] = lead[5] - mm(l20, u02, NN) - mm(l21, u12, NN)
    factor_panel(block, aug, inverse)
    w2 = split(inverse[...])

    x0 = mm(split(row[0]), w0, NT)
    sx0 = split(x0)
    x1 = mm(split(row[1] - mm(sx0, u01, NN)), w1, NT)
    sx1 = split(x1)
    x2 = mm(split(row[2] - mm(sx0, u02, NN) - mm(sx1, u12, NN)), w2, NT)
    sx2 = split(x2)

    def schur(target, member):
        y0 = split(mm(w0, split(top_ref[0, :, member, :]), NN))
        y1 = split(mm(w1, split(top_ref[1, :, member, :] - mm(l10, y0, NN)), NN))
        y2 = split(mm(w2, split(top_ref[2, :, member, :] - mm(l20, y0, NN) - mm(l21, y1, NN)), NN))
        return target - (mm(sx0, y0, NN) + mm(sx1, y1, NN) + mm(sx2, y2, NN))

    r = lax.broadcasted_iota(jnp.int32, (2 * HALF, 2 * HALF), 0)
    q = lax.broadcasted_iota(jnp.int32, (2 * HALF, 2 * HALF), 1)
    keep = jnp.where(p > c, 1, 0)
    diagonal = jnp.where(p == c, 1, 0)
    mask = (keep + diagonal * jnp.where(r >= q, 1, 0)) > 0

    @pl.when(c < PANELS)
    def _():
        panel = jnp.where(c == 0, x0, jnp.where(c == 1, x1, x2))
        out_ref[0, :, 0, :] = jnp.where(mask, panel, 0.0)

    @pl.when((c >= PANELS) & (p >= PANELS))
    def _():
        out_ref[0, :, 0, :] = schur(own_ref[...], 0)

    @pl.when((c >= PANELS) & (p < PANELS))
    def _():
        out_ref[0, :, 0, :] = jnp.zeros((2 * HALF, 2 * HALF), jnp.float32)

    @pl.when(p >= PANELS)
    def _():
        out_ref[0, :, 1, :] = schur(right_ref[...], 1)

    @pl.when(p < PANELS)
    def _():
        out_ref[0, :, 1, :] = jnp.zeros((2 * HALF, 2 * HALF), jnp.float32)


def swap(value, axis, bit):
    n = lax.axis_size(axis)
    return lax.ppermute(value, axis, [(i, i ^ bit) for i in range(n)])


def shards(kernel):
    n_row = lax.axis_size("row")
    n_col = lax.axis_size("col")
    p = lax.axis_index("row")
    c = lax.axis_index("col")
    nb = kernel.shape[1]
    own = kernel[0, :, 0, :]
    right = kernel[0, :, 1, :]
    top = lax.all_gather(kernel[0], "row")

    side = [swap(own, "col", d) for d in range(1, n_col)]
    panel = []
    for k in range(PANELS):
        value = own
        for d in range(1, n_col):
            value = jnp.where(jnp.bitwise_xor(c, d) == k, side[d - 1], value)
        panel.append(value)
    panel = jnp.stack(panel)

    core, across, along = p & 1, (p >> 1) & 1, (p >> 2) & 1
    halves = panel.reshape(PANELS, 2, HALF, nb)
    kept = jnp.where(core == 0, halves[:, 0], halves[:, 1])
    given = jnp.where(core == 0, halves[:, 1], halves[:, 0])
    got = swap(given, "row", 1)
    even = jnp.where(core == 0, kept, got)
    odd = jnp.where(core == 0, got, kept)
    group = jnp.where(across == 0, jnp.stack([even[0], odd[0], odd[1]]), even)
    group_x = swap(group, "row", 2)
    group_y = swap(group, "row", 4)
    part_y = swap(group_x[:, :HALF // 2], "row", 4)
    part_x = swap(group_y[:, HALF // 2:], "row", 2)
    mine = jnp.where(along == 0, group, group_y)
    other = jnp.where(along == 0, group_x, jnp.concatenate([part_y, part_x], axis=1))
    lead = jnp.concatenate([jnp.where(across == 0, mine, other), jnp.where(across == 0, other, mine)])
    bit = 8
    while bit < n_row:
        came = swap(lead, "row", bit)
        lead = jnp.where((p & bit) == 0, lead, came)
        bit *= 2
    partner = swap(lead, "row", 1)

    place = jnp.stack([p, c, jnp.int32(n_col)]).astype(jnp.int32)
    f32 = jnp.float32
    vmem = pl.BlockSpec(memory_space=pltpu.VMEM)
    return pl.pallas_call(
        panels_kernel,
        grid=(1,),
        out_shape=jax.ShapeDtypeStruct(kernel.shape, f32),
        in_specs=[pl.BlockSpec(memory_space=pltpu.SMEM)] + [vmem] * (4 + len(side))
        + [pl.BlockSpec((PANELS, nb, 2, nb), lambda i: (0, 0, 0, 0))],
        out_specs=vmem,
        scratch_shapes=[
            pltpu.VMEM((6, nb, nb), f32),
            pltpu.VMEM((n_col, nb, nb), f32),
            pltpu.VMEM((HALF, nb), f32),
            pltpu.VMEM((nb, nb), f32),
            pltpu.VMEM((nb, nb), f32),
            pltpu.VMEM((nb, nb), f32),
        ],
        compiler_params=pltpu.CompilerParams(vmem_limit_bytes=48 * 1024 * 1024),
        name="panels",
    )(place, lead, partner, own, *side, right, top)


def solution(mesh):
    in_specs = (P(None, "row", None, "col"),)
    out_specs = P(None, "row", None, "col")
    return jax.shard_map(shards, mesh=mesh, in_specs=in_specs, out_specs=out_specs, check_vma=False)
```

time: 671 us -> 108 us (0.16)
  the two profiles are of different devices: /device:TPU:13 before, /device:TPU:27 now
where the time goes in v1:
time: 108 us
  waiting for transfers between devices  36.9 us (34%)
  Pallas kernels  31.8 us (29%)
  starting transfers between devices  13.8 us (13%)
  between operations  13.5 us (12%)
  local copies, waits for them, and re-layouts  10.4 us (10%)
  other arithmetic  1.56 us (1%)
    ppermute x9, waiting for transfers between devices, swap(): return lax.ppermute(value, axis, [(i, i ^ bit) for i in range(n)])  36.9 us
    pallas_call x1, Pallas kernels, shards(): pl.pallas_call(panels_kernel, grid=(1,), out_shape=jax.ShapeDtypeStruct(k...  31.8 us
    ppermute x9, starting transfers between devices, swap(): return lax.ppermute(value, axis, [(i, i ^ bit) for i in range(n)])  13.8 us
    all_gather x1, local copies, waits for them, and re-layouts, shards(): top = lax.all_gather(kernel[0], 'row')  7.39 us
  transfers between devices with their start and end apart: 10, of which 6 were waited for; matrix products, arithmetic and copies ran while one was open for 9% of the time, Pallas kernels for 0%

profile of v1, /device:TPU:27, one launch (start us, length us, event | category | flops | bytes accessed | tf_op | source)
XLA Modules:
  0.0 107.8 jit_solution(4154991392418268593)
XLA Ops:
  6.5 0.0 all-gather.2.cloned.1.call-start
  6.5 1.9 %copy.7 = f32[1,256,2,256]{3,1,2,0:T(8,128)} copy(f32[1,256,2,256]{3,2,1,0:T(2,128)} %param.1) | data formatting | bytes 1048576 | tf_op args[0]
  8.4 0.0 all-gather.2.cloned.1.call-update
  8.4 1.1 slice_bitcast_fusion
  9.5 0.2 collective-permute-start.2
  9.7 0.1 collective-permute-start.1
  9.8 3.3 %collective-permute-start = (f32[256,256]{1,0:T(8,128)S(1)}, f32[256,256]{1,0:T(8,128)S(1)}, u32[]{:S(2)}, u32[]{:S(2)}) collective-permute-start(f32[256,256]{1,0:T(8,128)S(1)} %get-tuple-element.13.own_ref), channel_id=1, source_target_pairs={{0,3},{1,2},{2,1},{3,0},{4,7},{5,6},{6,5},{7,4},{8,11},{9,10},{10,... | collective-permute-start | bytes 786440 | tf_op jit(solution)/shard_map/ppermute | solution.py:187
  13.1 8.0 %collective-permute-done.2.refs_0_ = f32[256,256]{1,0:T(8,128)S(1)} collective-permute-done((f32[256,256]{1,0:T(8,128)S(1)}, f32[256,256]{1,0:T(8,128)S(1)}, u32[]{:S(2)}, u32[]{:S(2)}) %collective-permute-start.2) | collective-permute-done | bytes 262176 | tf_op jit(solution)/shard_map/ppermute | solution.py:187
  21.1 0.0 collective-permute-done.1.refs_1_
  21.2 6.6 %collective-permute-done.refs_2_ = f32[256,256]{1,0:T(8,128)S(1)} collective-permute-done((f32[256,256]{1,0:T(8,128)S(1)}, f32[256,256]{1,0:T(8,128)S(1)}, u32[]{:S(2)}, u32[]{:S(2)}) %collective-permute-start) | collective-permute-done | bytes 262176 | tf_op jit(solution)/shard_map/ppermute | solution.py:187
  27.8 1.0 select_select_fusion.2
  28.8 0.1 pad_maximum_fusion
  28.9 0.1 select_bitcast_fusion
  29.0 4.3 %collective-permute-start.3 = (f32[3,128,256]{2,1,0:T(8,128)S(1)}, f32[3,128,256]{2,1,0:T(8,128)S(1)}, u32[]{:S(2)}, u32[]{:S(2)}) collective-permute-start(f32[3,128,256]{2,1,0:T(8,128)S(1)} %select_bitcast_fusion), channel_id=1, source_target_pairs={{0,4},{4,0},{8,12},{12,8},{16,20},{20,16},{24,28},{28,24},{1,5},{5... | collective-permute-start | bytes 1179656 | tf_op jit(solution)/shard_map/ppermute | solution.py:187
  33.3 1.6 %collective-permute-done.3 = f32[3,128,256]{2,1,0:T(8,128)S(1)} collective-permute-done((f32[3,128,256]{2,1,0:T(8,128)S(1)}, f32[3,128,256]{2,1,0:T(8,128)S(1)}, u32[]{:S(2)}, u32[]{:S(2)}) %collective-permute-start.3) | collective-permute-done | bytes 393248 | tf_op jit(solution)/shard_map/ppermute | solution.py:187
  34.9 0.1 broadcast_select_fusion
  35.0 0.1 maximum_select_fusion
  35.1 0.3 collective-permute-start.5
  35.4 1.2 %collective-permute-start.4 = (f32[3,128,256]{2,1,0:T(8,128)S(1)}, f32[3,128,256]{2,1,0:T(8,128)S(1)}, u32[]{:S(2)}, u32[]{:S(2)}) collective-permute-start(f32[3,128,256]{2,1,0:T(8,128)S(1)} %maximum_select_fusion), channel_id=1, source_target_pairs={{0,16},{4,20},{8,24},{12,28},{16,0},{20,4},{24,8},{28,12},{1,17},{... | collective-permute-start | bytes 1179656 | tf_op jit(solution)/shard_map/ppermute | solution.py:187
  36.6 16.3 %collective-permute-done.5 = f32[3,128,256]{2,1,0:T(8,128)S(1)} collective-permute-done((f32[3,128,256]{2,1,0:T(8,128)S(1)}, f32[3,128,256]{2,1,0:T(8,128)S(1)}, u32[]{:S(2)}, u32[]{:S(2)}) %collective-permute-start.5) | collective-permute-done | bytes 393248 | tf_op jit(solution)/shard_map/ppermute | solution.py:187
  52.9 1.1 %collective-permute-start.6 = (f32[3,64,256]{2,1,0:T(8,128)S(1)}, f32[3,64,256]{2,1,0:T(8,128)S(1)}, u32[]{:S(2)}, u32[]{:S(2)}) collective-permute-start(f32[3,64,256]{2,1,0:T(8,128)S(1)} %slice.42), channel_id=1, source_target_pairs={{0,16},{4,20},{8,24},{12,28},{16,0},{20,4},{24,8},{28,12},{1,17},{... | collective-permute-start | bytes 589832 | tf_op jit(solution)/shard_map/ppermute | solution.py:187
  54.1 0.0 collective-permute-done.4
  54.1 1.3 %collective-permute-start.7 = (f32[3,64,256]{2,1,0:T(8,128)S(1)}, f32[3,64,256]{2,1,0:T(8,128)S(1)}, u32[]{:S(2)}, u32[]{:S(2)}) collective-permute-start(f32[3,64,256]{2,1,0:T(8,128)S(1)} %slice.43), channel_id=1, source_target_pairs={{0,8},{4,12},{8,0},{12,4},{16,24},{20,28},{24,16},{28,20},{1,9},{5... | collective-permute-start | bytes 589832 | tf_op jit(solution)/shard_map/ppermute | solution.py:187
  55.4 3.6 %collective-permute-done.6 = f32[3,64,256]{2,1,0:T(8,128)S(1)} collective-permute-done((f32[3,64,256]{2,1,0:T(8,128)S(1)}, f32[3,64,256]{2,1,0:T(8,128)S(1)}, u32[]{:S(2)}, u32[]{:S(2)}) %collective-permute-start.6) | collective-permute-done | bytes 196640 | tf_op jit(solution)/shard_map/ppermute | solution.py:187
  58.9 0.7 collective-permute-done.7
  59.7 0.1 broadcast_select_fusion.3
  59.8 0.1 pad_maximum_fusion.1.mine_ref
  59.8 1.9 %collective-permute-start.8 = (f32[6,128,256]{2,1,0:T(8,128)S(1)}, f32[6,128,256]{2,1,0:T(8,128)S(1)}, u32[]{:S(2)}, u32[]{:S(2)}) collective-permute-start(f32[6,128,256]{2,1,0:T(8,128)S(1)} %pad_maximum_fusion.1.mine_ref), channel_id=1, source_target_pairs={{0,4},{4,0},{8,12},{12,8},{16,20},{20,16},{24,28},{28,24},{1,5},{5... | collective-permute-start | bytes 2359304 | tf_op jit(solution)/shard_map/ppermute | solution.py:187
  61.7 0.1 pad_add_fusion.place
  61.8 7.4 %copy.13.refs_4_ = f32[8,256,2,256]{3,2,1,0:T(2,128)} copy(f32[8,256,2,256]{3,1,2,0:T(8,128)} %all-gather.2.cloned.1.call-done) | data formatting | bytes 8388608 | tf_op jit(solution)/shard_map/all_gather | solution.py:198
  69.2 0.0 collective-permute-done.8.other_ref
  69.2 31.8 %panels.1 = f32[1,256,2,256]{3,2,1,0:T(2,128)} custom-call(s32[3]{0:T(128)S(1)} %pad_add_fusion.place, f32[6,128,256]{2,1,0:T(8,128)S(1)} %pad_maximum_fusion.1.mine_ref, f32[6,128,256]{2,1,0:T(8,128)S(1)} %collective-permute-done.8.other_ref, f32[256,256]{1,0:T(8,128)S(1)} %get-tuple-element.13.own_ref, f32[256,256]{1,0:T(8,128)S(1)} %collective-permute-done.2.refs_0_, ...), custom_call_target="tpu_custom_call" | custom-call | tf_op jit(solution)/shard_map/panels/pallas_call | solution.py:234
  (5 shorter events, 0.1 us)
Async XLA Ops:
  6.5 55.3 %all-gather.2.cloned.1.call-start = ((), (), s32[]{:S(2)}) async-start(), calls=%async_computation | async-start | bytes 4718592 | tf_op jit(solution)/shard_map/all_gather | solution.py:198
  9.5 11.6 %collective-permute-start.2 = (f32[256,256]{1,0:T(8,128)S(1)}, f32[256,256]{1,0:T(8,128)S(1)}, u32[]{:S(2)}, u32[]{:S(2)}) collective-permute-start(f32[256,256]{1,0:T(8,128)S(1)} %get-tuple-element.13.own_ref), channel_id=1, source_target_pairs={{0,1},{1,0},{2,3},{3,2},{4,5},{5,4},{6,7},{7,6},{8,9},{9,8},{10,11... | collective-permute-start | bytes 786440 | tf_op jit(solution)/shard_map/ppermute | solution.py:187
  9.7 11.4 %collective-permute-start.1 = (f32[256,256]{1,0:T(8,128)S(1)}, f32[256,256]{1,0:T(8,128)S(1)}, u32[]{:S(2)}, u32[]{:S(2)}) collective-permute-start(f32[256,256]{1,0:T(8,128)S(1)} %get-tuple-element.13.own_ref), channel_id=1, source_target_pairs={{0,2},{1,3},{2,0},{3,1},{4,6},{5,7},{6,4},{7,5},{8,10},{9,11},{10,... | collective-permute-start | bytes 786440 | tf_op jit(solution)/shard_map/ppermute | solution.py:187
  9.8 18.0 %collective-permute-start = (f32[256,256]{1,0:T(8,128)S(1)}, f32[256,256]{1,0:T(8,128)S(1)}, u32[]{:S(2)}, u32[]{:S(2)}) collective-permute-start(f32[256,256]{1,0:T(8,128)S(1)} %get-tuple-element.13.own_ref), channel_id=1, source_target_pairs={{0,3},{1,2},{2,1},{3,0},{4,7},{5,6},{6,5},{7,4},{8,11},{9,10},{10,... | collective-permute-start | bytes 786440 | tf_op jit(solution)/shard_map/ppermute | solution.py:187
  29.0 5.9 %collective-permute-start.3 = (f32[3,128,256]{2,1,0:T(8,128)S(1)}, f32[3,128,256]{2,1,0:T(8,128)S(1)}, u32[]{:S(2)}, u32[]{:S(2)}) collective-permute-start(f32[3,128,256]{2,1,0:T(8,128)S(1)} %select_bitcast_fusion), channel_id=1, source_target_pairs={{0,4},{4,0},{8,12},{12,8},{16,20},{20,16},{24,28},{28,24},{1,5},{5... | collective-permute-start | bytes 1179656 | tf_op jit(solution)/shard_map/ppermute | solution.py:187
  35.1 17.9 %collective-permute-start.5 = (f32[3,128,256]{2,1,0:T(8,128)S(1)}, f32[3,128,256]{2,1,0:T(8,128)S(1)}, u32[]{:S(2)}, u32[]{:S(2)}) collective-permute-start(f32[3,128,256]{2,1,0:T(8,128)S(1)} %maximum_select_fusion), channel_id=1, source_target_pairs={{0,8},{4,12},{8,0},{12,4},{16,24},{20,28},{24,16},{28,20},{1,9},{5... | collective-permute-start | bytes 1179656 | tf_op jit(solution)/shard_map/ppermute | solution.py:187
  35.4 18.7 %collective-permute-start.4 = (f32[3,128,256]{2,1,0:T(8,128)S(1)}, f32[3,128,256]{2,1,0:T(8,128)S(1)}, u32[]{:S(2)}, u32[]{:S(2)}) collective-permute-start(f32[3,128,256]{2,1,0:T(8,128)S(1)} %maximum_select_fusion), channel_id=1, source_target_pairs={{0,16},{4,20},{8,24},{12,28},{16,0},{20,4},{24,8},{28,12},{1,17},{... | collective-permute-start | bytes 1179656 | tf_op jit(solution)/shard_map/ppermute | solution.py:187
  52.9 6.0 %collective-permute-start.6 = (f32[3,64,256]{2,1,0:T(8,128)S(1)}, f32[3,64,256]{2,1,0:T(8,128)S(1)}, u32[]{:S(2)}, u32[]{:S(2)}) collective-permute-start(f32[3,64,256]{2,1,0:T(8,128)S(1)} %slice.42), channel_id=1, source_target_pairs={{0,16},{4,20},{8,24},{12,28},{16,0},{20,4},{24,8},{28,12},{1,17},{... | collective-permute-start | bytes 589832 | tf_op jit(solution)/shard_map/ppermute | solution.py:187
  54.1 5.6 %collective-permute-start.7 = (f32[3,64,256]{2,1,0:T(8,128)S(1)}, f32[3,64,256]{2,1,0:T(8,128)S(1)}, u32[]{:S(2)}, u32[]{:S(2)}) collective-permute-start(f32[3,64,256]{2,1,0:T(8,128)S(1)} %slice.43), channel_id=1, source_target_pairs={{0,8},{4,12},{8,0},{12,4},{16,24},{20,28},{24,16},{28,20},{1,9},{5... | collective-permute-start | bytes 589832 | tf_op jit(solution)/shard_map/ppermute | solution.py:187
  59.8 9.4 %collective-permute-start.8 = (f32[6,128,256]{2,1,0:T(8,128)S(1)}, f32[6,128,256]{2,1,0:T(8,128)S(1)}, u32[]{:S(2)}, u32[]{:S(2)}) collective-permute-start(f32[6,128,256]{2,1,0:T(8,128)S(1)} %pad_maximum_fusion.1.mine_ref), channel_id=1, source_target_pairs={{0,4},{4,0},{8,12},{12,8},{16,20},{20,16},{24,28},{28,24},{1,5},{5... | collective-permute-start | bytes 2359304 | tf_op jit(solution)/shard_map/ppermute | solution.py:187
Sparse Core Ops, SparseCore 0:
  9.2 45.4 all-gather.1

commit v2 on v1

--- a/solution.py
+++ b/solution.py
@@ -90,56 +90,81 @@
         aug[8 * g:8 * g + 8, :] = rows[g]
 
 
+def identity(n):
+    r = lax.broadcasted_iota(jnp.int32, (n, n), 0)
+    c = lax.broadcasted_iota(jnp.int32, (n, n), 1)
+    return jnp.where(r == c, 1.0, 0.0).astype(jnp.float32)
+
+
 def factor_panel(block, aug, inverse):
-    r = lax.broadcasted_iota(jnp.int32, (HALF, HALF), 0)
-    c = lax.broadcasted_iota(jnp.int32, (HALF, HALF), 1)
-    eye = jnp.where(r == c, 1.0, 0.0).astype(jnp.float32)
     aug[:, :HALF] = block[:HALF, :HALF]
-    aug[:, HALF:] = eye
-    factor_half(aug)
-    w0 = aug[:, HALF:]
-    sw0 = split(w0)
-    side = split(block[HALF:, :HALF])
-    low = split(mm(side, sw0, NT))
-    up = split(mm(sw0, side, NT))
-    aug[:, :HALF] = block[HALF:, HALF:] - mm(low, up, NN)
-    aug[:, HALF:] = eye
-    factor_half(aug)
-    w1 = aug[:, HALF:]
-    corner = mm(split(w1), split(mm(low, sw0, NN)), NN)
-    inverse[:HALF, :HALF] = w0
+    aug[:, HALF:] = identity(HALF)
     inverse[:HALF, HALF:] = jnp.zeros((HALF, HALF), jnp.float32)
-    inverse[HALF:, :HALF] = -corner
-    inverse[HALF:, HALF:] = w1
+
+    @pl.loop(0, 2)
+    def _(half):
+        factor_half(aug)
+        sw = split(aug[:, HALF:])
+
+        @pl.when(half == 0)
+        def _():
+            side = split(block[HALF:, :HALF])
+            low = split(mm(side, sw, NT))
+            up = split(mm(sw, side, NT))
+            inverse[:HALF, :HALF] = aug[:, HALF:]
+            inverse[HALF:, :HALF] = mm(low, sw, NN)
+            aug[:, :HALF] = block[HALF:, HALF:] - mm(low, up, NN)
+            aug[:, HALF:] = identity(HALF)
+
+        @pl.when(half == 1)
+        def _():
+            inverse[HALF:, :HALF] = -mm(sw, split(inverse[HALF:, :HALF]), NN)
+            inverse[HALF:, HALF:] = aug[:, HALF:]
 
 
 def panels_kernel(place, mine_ref, other_ref, own_ref, *refs):
-    n_side = len(refs) - 9
+    n_side = len(refs) - 12
     side_refs = refs[:n_side]
-    right_ref, top_ref, out_ref, lead, row, aug, inverse, block, work = refs[n_side:]
+    right_ref, top_ref, top_other_ref, out_ref, lead, top, row, aug, inverses, lower, upper, block = refs[n_side:]
     p, c, n_col = place[0], place[1], place[2]
     core = lax.rem(p, 2)
+    here = pl.ds(pl.multiple_of(core * HALF, HALF), HALF)
+    there = pl.ds(pl.multiple_of((1 - core) * HALF, HALF), HALF)
     for b in range(6):
-        lead[b, pl.ds(pl.multiple_of(core * HALF, HALF), HALF), :] = mine_ref[b]
-        lead[b, pl.ds(pl.multiple_of((1 - core) * HALF, HALF), HALF), :] = other_ref[b]
+        lead[b, here, :] = mine_ref[b]
+        lead[b, there, :] = other_ref[b]
+        top[b, here, :] = top_ref[b]
+        top[b, there, :] = top_other_ref[b]
     row[c] = own_ref[...]
     for d in range(n_side):
         row[lax.bitwise_xor(c, d + 1)] = side_refs[d][...]
 
     block[...] = lead[0]
-    factor_panel(block, aug, inverse)
-    w0 = split(inverse[...])
-    s10, s20 = split(lead[1]), split(lead[3])
-    l10, l20 = split(mm(s10, w0, NT)), split(mm(s20, w0, NT))
-    u01, u02 = split(mm(w0, s10, NT)), split(mm(w0, s20, NT))
-    block[...] = lead[2] - mm(l10, u01, NN)
-    factor_panel(block, aug, inverse)
-    w1 = split(inverse[...])
-    s21 = split(lead[4] - mm(l20, u01, NN))
-    l21, u12 = split(mm(s21, w1, NT)), split(mm(w1, s21, NT))
-    block[...] = lead[5] - mm(l20, u02, NN) - mm(l21, u12, NN)
-    factor_panel(block, aug, inverse)
-    w2 = split(inverse[...])
+
+    @pl.loop(0, PANELS)
+    def _(k):
+        factor_panel(block, aug, inverses.at[k])
+        w = split(inverses[k])
+
+        @pl.when(k == 0)
+        def _():
+            for i, b in enumerate((1, 3)):
+                s = split(lead[b])
+                lower[i] = mm(s, w, NT)
+                upper[i] = mm(w, s, NT)
+            block[...] = lead[2] - mm(split(lower[0]), split(upper[0]), NN)
+
+        @pl.when(k == 1)
+        def _():
+            s = split(lead[4] - mm(split(lower[1]), split(upper[0]), NN))
+            l21, u12 = mm(s, w, NT), mm(w, s, NT)
+            lower[2] = l21
+            upper[2] = u12
+            block[...] = lead[5] - mm(split(lower[1]), split(upper[1]), NN) - mm(split(l21), split(u12), NN)
+
+    w0, w1, w2 = [split(inverses[k]) for k in range(PANELS)]
+    l10, l20, l21 = [split(lower[k]) for k in range(PANELS)]
+    u01, u02, u12 = [split(upper[k]) for k in range(PANELS)]
 
     x0 = mm(split(row[0]), w0, NT)
     sx0 = split(x0)
@@ -149,9 +174,9 @@
     sx2 = split(x2)
 
     def schur(target, member):
-        y0 = split(mm(w0, split(top_ref[0, :, member, :]), NN))
-        y1 = split(mm(w1, split(top_ref[1, :, member, :] - mm(l10, y0, NN)), NN))
-        y2 = split(mm(w2, split(top_ref[2, :, member, :] - mm(l20, y0, NN) - mm(l21, y1, NN)), NN))
+        y0 = split(mm(w0, split(top[3 * member]), NN))
+        y1 = split(mm(w1, split(top[3 * member + 1] - mm(l10, y0, NN)), NN))
+        y2 = split(mm(w2, split(top[3 * member + 2] - mm(l20, y0, NN) - mm(l21, y1, NN)), NN))
         return target - (mm(sx0, y0, NN) + mm(sx1, y1, NN) + mm(sx2, y2, NN))
 
     r = lax.broadcasted_iota(jnp.int32, (2 * HALF, 2 * HALF), 0)
@@ -185,6 +210,25 @@
 def swap(value, axis, bit):
     n = lax.axis_size(axis)
     return lax.ppermute(value, axis, [(i, i ^ bit) for i in range(n)])
+
+
+def spread(kept, given, pick, p, n_row):
+    core, across, along = p & 1, (p >> 1) & 1, (p >> 2) & 1
+    got = swap(given, "row", 1)
+    group = pick(jnp.where(core == 0, kept, got), jnp.where(core == 0, got, kept), across)
+    group_x = swap(group, "row", 2)
+    group_y = swap(group, "row", 4)
+    part_y = swap(group_x[:, :HALF // 2], "row", 4)
+    part_x = swap(group_y[:, HALF // 2:], "row", 2)
+    mine = jnp.where(along == 0, group, group_y)
+    other = jnp.where(along == 0, group_x, jnp.concatenate([part_y, part_x], axis=1))
+    first, second = jnp.where(across == 0, mine, other), jnp.where(across == 0, other, mine)
+    bit = 8
+    while bit < n_row:
+        first = jnp.where((p & bit) == 0, first, swap(first, "row", bit))
+        second = jnp.where((p & bit) == 0, second, swap(second, "row", bit))
+        bit *= 2
+    return first, second
 
 
 def shards(kernel):
@@ -195,7 +239,16 @@
     nb = kernel.shape[1]
     own = kernel[0, :, 0, :]
     right = kernel[0, :, 1, :]
-    top = lax.all_gather(kernel[0], "row")
+    core = p & 1
+
+    def cut(blocks):
+        halves = blocks.reshape(blocks.shape[0], 2, HALF, nb)
+        return jnp.where(core == 0, halves[:, 0], halves[:, 1]), jnp.where(core == 0, halves[:, 1], halves[:, 0])
+
+    kept, given = cut(jnp.stack([own, right]))
+    first, second = spread(kept, given, lambda even, odd, across: jnp.stack([even[0], odd[0], even[1], odd[1]]), p, n_row)
+    top = jnp.stack([first[0], first[1], second[0], first[2], first[3], second[2]])
+    top_other = swap(top, "row", 1)
 
     side = [swap(own, "col", d) for d in range(1, n_col)]
     panel = []
@@ -204,51 +257,34 @@
         for d in range(1, n_col):
             value = jnp.where(jnp.bitwise_xor(c, d) == k, side[d - 1], value)
         panel.append(value)
-    panel = jnp.stack(panel)
-
-    core, across, along = p & 1, (p >> 1) & 1, (p >> 2) & 1
-    halves = panel.reshape(PANELS, 2, HALF, nb)
-    kept = jnp.where(core == 0, halves[:, 0], halves[:, 1])
-    given = jnp.where(core == 0, halves[:, 1], halves[:, 0])
-    got = swap(given, "row", 1)
-    even = jnp.where(core == 0, kept, got)
-    odd = jnp.where(core == 0, got, kept)
-    group = jnp.where(across == 0, jnp.stack([even[0], odd[0], odd[1]]), even)
-    group_x = swap(group, "row", 2)
-    group_y = swap(group, "row", 4)
-    part_y = swap(group_x[:, :HALF // 2], "row", 4)
-    part_x = swap(group_y[:, HALF // 2:], "row", 2)
-    mine = jnp.where(along == 0, group, group_y)
-    other = jnp.where(along == 0, group_x, jnp.concatenate([part_y, part_x], axis=1))
-    lead = jnp.concatenate([jnp.where(across == 0, mine, other), jnp.where(across == 0, other, mine)])
-    bit = 8
-    while bit < n_row:
-        came = swap(lead, "row", bit)
-        lead = jnp.where((p & bit) == 0, lead, came)
-        bit *= 2
-    partner = swap(lead, "row", 1)
+
+    kept, given = cut(jnp.stack(panel))
+    first, second = spread(
+        kept, given, lambda even, odd, across: jnp.where(across == 0, jnp.stack([even[0], odd[0], odd[1]]), even), p, n_row)
+    lead = jnp.concatenate([first, second])
+    lead_other = swap(lead, "row", 1)
 
     place = jnp.stack([p, c, jnp.int32(n_col)]).astype(jnp.int32)
     f32 = jnp.float32
     vmem = pl.BlockSpec(memory_space=pltpu.VMEM)
     return pl.pallas_call(
         panels_kernel,
-        grid=(1,),
         out_shape=jax.ShapeDtypeStruct(kernel.shape, f32),
-        in_specs=[pl.BlockSpec(memory_space=pltpu.SMEM)] + [vmem] * (4 + len(side))
-        + [pl.BlockSpec((PANELS, nb, 2, nb), lambda i: (0, 0, 0, 0))],
+        in_specs=[pl.BlockSpec(memory_space=pltpu.SMEM)] + [vmem] * (6 + len(side)),
         out_specs=vmem,
         scratch_shapes=[
             pltpu.VMEM((6, nb, nb), f32),
+            pltpu.VMEM((6, nb, nb), f32),
             pltpu.VMEM((n_col, nb, nb), f32),
             pltpu.VMEM((HALF, nb), f32),
-            pltpu.VMEM((nb, nb), f32),
-            pltpu.VMEM((nb, nb), f32),
+            pltpu.VMEM((PANELS, nb, nb), f32),
+            pltpu.VMEM((PANELS, nb, nb), f32),
+            pltpu.VMEM((PANELS, nb, nb), f32),
             pltpu.VMEM((nb, nb), f32),
         ],
         compiler_params=pltpu.CompilerParams(vmem_limit_bytes=48 * 1024 * 1024),
         name="panels",
-    )(place, lead, partner, own, *side, right, top)
+    )(place, lead, lead_other, own, *side, right, top, top_other)
 
 
 def solution(mesh):

time: 108 us -> 102 us (0.944)
  between operations: 13.5 us -> 0.17 us
  starting transfers between devices: 13.8 us -> 22 us
  local copies, waits for them, and re-layouts: 10.4 us -> 4.32 us
  waiting for transfers between devices: 36.9 us -> 40.7 us
  other arithmetic: 1.56 us -> 2.9 us
    ppermute x9 -> x15, starting transfers between devices: 13.8 us -> 22 us  [swap(): return lax.ppermute(value, axis, [(i, i ^ bit) for i in range(n)])]
    all_gather x1 -> x0, local copies, waits for them, and re-layouts: 7.39 us -> none  [shards(): top = lax.all_gather(kernel[0], 'row')]
    slice x3 -> x9, local copies, waits for them, and re-layouts: 0.04 us -> 4.29 us  [the longest x1 1.77 us: shards(): right = kernel[0, :, 1, :]]
    ppermute x9 -> x15, waiting for transfers between devices: 36.9 us -> 40.7 us  [swap(): return lax.ppermute(value, axis, [(i, i ^ bit) for i in range(n)])]
    select_n x5 -> x8, other arithmetic: 0.32 us -> 2.5 us  [the longest x2 2.19 us: spread(): jnp.where(across == 0, mine, other)]
    unnamed x1 -> x2, local copies, waits for them, and re-layouts: 1.87 us -> 0.04 us
  transfers between devices with their start and end apart: 10 -> 15, of which waited for: 6 -> 8; matrix products, arithmetic and copies ran while one was open for 9% -> 5% of each run, Pallas kernels for 0% -> 0%
where the time goes in v2:
time: 102 us
  waiting for transfers between devices  40.7 us (40%)
  Pallas kernels  32 us (31%)
  starting transfers between devices  22 us (22%)
  local copies, waits for them, and re-layouts  4.32 us (4%)
  other arithmetic  2.9 us (3%)
    ppermute x15, waiting for transfers between devices, swap(): return lax.ppermute(value, axis, [(i, i ^ bit) for i in range(n)])  40.7 us
    pallas_call x1, Pallas kernels, shards(): pl.pallas_call(panels_kernel, out_shape=jax.ShapeDtypeStruct(kernel.shape...  32 us
    ppermute x15, starting transfers between devices, swap(): return lax.ppermute(value, axis, [(i, i ^ bit) for i in range(n)])  22 us
    select_n x2, other arithmetic, spread(): jnp.where(across == 0, mine, other)  2.19 us
  transfers between devices with their start and end apart: 15, of which 8 were waited for; matrix products, arithmetic and copies ran while one was open for 5% of the time, Pallas kernels for 0%

profile of v2, /device:TPU:27, one launch (start us, length us, event | category | flops | bytes accessed | tf_op | source)
XLA Modules:
  0.0 102.1 jit_solution(8269535222942985407)
XLA Ops:
  0.0 1.8 %fusion.3 = (f32[1,256,1,256]{3,2,1,0:T(1,128)S(1)}, f32[1,256,1,256]{3,2,1,0:T(1,128)S(1)}) fusion(f32[1,256,2,256]{3,2,1,0:T(2,128)} %param.1), kind=kLoop, calls=%fused_computation.33 | loop fusion | bytes 1048576 | tf_op jit(solution)/shard_map/slice | solution.py:241
  1.9 1.3 %collective-permute-start.1 = (f32[256,256]{1,0:T(8,128)S(1)}, f32[256,256]{1,0:T(8,128)S(1)}, u32[]{:S(2)}, u32[]{:S(2)}) collective-permute-start(f32[256,256]{1,0:T(8,128)S(1)} %bitcast.31), channel_id=1, source_target_pairs={{0,2},{1,3},{2,0},{3,1},{4,6},{5,7},{6,4},{7,5},{8,10},{9,11},{10,... | collective-permute-start | bytes 786440 | tf_op jit(solution)/shard_map/ppermute | solution.py:212
  3.2 2.2 %collective-permute-start.2 = (f32[256,256]{1,0:T(8,128)S(1)}, f32[256,256]{1,0:T(8,128)S(1)}, u32[]{:S(2)}, u32[]{:S(2)}) collective-permute-start(f32[256,256]{1,0:T(8,128)S(1)} %bitcast.32), channel_id=1, source_target_pairs={{0,1},{1,0},{2,3},{3,2},{4,5},{5,4},{6,7},{7,6},{8,9},{9,8},{10,11... | collective-permute-start | bytes 786440 | tf_op jit(solution)/shard_map/ppermute | solution.py:212
  5.5 1.6 %collective-permute-start.9 = (f32[2,128,256]{2,1,0:T(8,128)S(1)}, f32[2,128,256]{2,1,0:T(8,128)S(1)}, u32[]{:S(2)}, u32[]{:S(2)}) collective-permute-start(f32[2,128,256]{2,1,0:T(8,128)S(1)} %select_bitcast_fusion.2), channel_id=1, source_target_pairs={{0,4},{4,0},{8,12},{12,8},{16,20},{20,16},{24,28},{28,24},{1,5},{5... | collective-permute-start | bytes 786440 | tf_op jit(solution)/shard_map/ppermute | solution.py:212
  7.1 3.9 %collective-permute-done.refs_2_ = f32[256,256]{1,0:T(8,128)S(1)} collective-permute-done((f32[256,256]{1,0:T(8,128)S(1)}, f32[256,256]{1,0:T(8,128)S(1)}, u32[]{:S(2)}, u32[]{:S(2)}) %collective-permute-start) | collective-permute-done | bytes 262176 | tf_op jit(solution)/shard_map/ppermute | solution.py:212
  11.0 14.8 %collective-permute-done.1.refs_1_ = f32[256,256]{1,0:T(8,128)S(1)} collective-permute-done((f32[256,256]{1,0:T(8,128)S(1)}, f32[256,256]{1,0:T(8,128)S(1)}, u32[]{:S(2)}, u32[]{:S(2)}) %collective-permute-start.1) | collective-permute-done | bytes 262176 | tf_op jit(solution)/shard_map/ppermute | solution.py:212
  25.8 0.1 select_select_fusion.2
  26.0 1.6 %collective-permute-start.3 = (f32[3,128,256]{2,1,0:T(8,128)S(1)}, f32[3,128,256]{2,1,0:T(8,128)S(1)}, u32[]{:S(2)}, u32[]{:S(2)}) collective-permute-start(f32[3,128,256]{2,1,0:T(8,128)S(1)} %select_bitcast_fusion), channel_id=1, source_target_pairs={{0,4},{4,0},{8,12},{12,8},{16,20},{20,16},{24,28},{28,24},{1,5},{5... | collective-permute-start | bytes 1179656 | tf_op jit(solution)/shard_map/ppermute | solution.py:212
  27.8 0.3 collective-permute-start.11
  28.1 1.2 %collective-permute-start.10 = (f32[4,128,256]{2,1,0:T(8,128)S(1)}, f32[4,128,256]{2,1,0:T(8,128)S(1)}, u32[]{:S(2)}, u32[]{:S(2)}) collective-permute-start(f32[4,128,256]{2,1,0:T(8,128)S(1)} %pad_maximum_fusion.3), channel_id=1, source_target_pairs={{0,16},{4,20},{8,24},{12,28},{16,0},{20,4},{24,8},{28,12},{1,17},{... | collective-permute-start | bytes 1572872 | tf_op jit(solution)/shard_map/ppermute | solution.py:212
  29.3 0.1 broadcast_select_fusion.3
  29.6 1.3 %collective-permute-start.5 = (f32[3,128,256]{2,1,0:T(8,128)S(1)}, f32[3,128,256]{2,1,0:T(8,128)}, u32[]{:S(2)}, u32[]{:S(2)}) collective-permute-start(f32[3,128,256]{2,1,0:T(8,128)S(1)} %maximum_select_fusion.1), channel_id=1, source_target_pairs={{0,8},{4,12},{8,0},{12,4},{16,24},{20,28},{24,16},{28,20},{1,9},{5... | collective-permute-start | bytes 1179656 | tf_op jit(solution)/shard_map/ppermute | solution.py:212
  30.8 10.5 %collective-permute-done.11 = f32[4,128,256]{2,1,0:T(8,128)S(1)} collective-permute-done((f32[4,128,256]{2,1,0:T(8,128)S(1)}, f32[4,128,256]{2,1,0:T(8,128)S(1)}, u32[]{:S(2)}, u32[]{:S(2)}) %collective-permute-start.11) | collective-permute-done | bytes 524320 | tf_op jit(solution)/shard_map/ppermute | solution.py:212
  41.4 0.7 slice.103
  42.1 1.2 %collective-permute-start.12 = (f32[4,64,256]{2,1,0:T(8,128)}, f32[4,64,256]{2,1,0:T(8,128)S(1)}, u32[]{:S(2)}, u32[]{:S(2)}) collective-permute-start(f32[4,64,256]{2,1,0:T(8,128)} %slice.103), channel_id=1, source_target_pairs={{0,16},{4,20},{8,24},{12,28},{16,0},{20,4},{24,8},{28,12},{1,17},{... | collective-permute-start | bytes 786440 | tf_op jit(solution)/shard_map/ppermute | solution.py:212
  43.4 0.7 slice.104
  44.1 0.3 collective-permute-start.13
  44.3 0.3 collective-permute-start.4
  44.6 5.3 %collective-permute-done.5 = f32[3,128,256]{2,1,0:T(8,128)} collective-permute-done((f32[3,128,256]{2,1,0:T(8,128)S(1)}, f32[3,128,256]{2,1,0:T(8,128)}, u32[]{:S(2)}, u32[]{:S(2)}) %collective-permute-start.5) | collective-permute-done | bytes 393248 | tf_op jit(solution)/shard_map/ppermute | solution.py:212
  49.9 0.9 slice.95
  50.9 1.3 %collective-permute-start.6 = (f32[3,64,256]{2,1,0:T(8,128)S(1)}, f32[3,64,256]{2,1,0:T(8,128)S(1)}, u32[]{:S(2)}, u32[]{:S(2)}) collective-permute-start(f32[3,64,256]{2,1,0:T(8,128)S(1)} %slice.95), channel_id=1, source_target_pairs={{0,16},{4,20},{8,24},{12,28},{16,0},{20,4},{24,8},{28,12},{1,17},{... | collective-permute-start | bytes 589832 | tf_op jit(solution)/shard_map/ppermute | solution.py:212
  52.2 3.4 %collective-permute-done.13 = f32[4,64,256]{2,1,0:T(8,128)} collective-permute-done((f32[4,64,256]{2,1,0:T(8,128)}, f32[4,64,256]{2,1,0:T(8,128)}, u32[]{:S(2)}, u32[]{:S(2)}) %collective-permute-start.13) | collective-permute-done | bytes 262176 | tf_op jit(solution)/shard_map/ppermute | solution.py:212
  55.5 1.1 %broadcast_select_fusion.2 = (f32[4,128,256]{2,1,0:T(8,128)S(1)}, f32[4,128,256]{2,1,0:T(8,128)S(1)}) fusion(pred[]{:T(512)S(6)} %eq.24, f32[4,128,256]{2,1,0:T(8,128)S(1)} %collective-permute-done.10, pred[]{:T(512)S(6)} %eq.25, f32[4,128,256]{2,1,0:T(8,128)S(1)} %collective-permute-done.11, f32[4,64,256]{2,1,0:T(8,128)} %collective-permute-done.13, ...), kind=kLoop, calls=%fused_computation.22 | loop fusion | flops 1048576 | bytes 3145730 | tf_op jit(solution)/shard_map/jit(_where)/select_n | solution.py:225
  56.7 0.7 collective-permute-done.4
  57.4 0.3 collective-permute-start.7
  57.7 0.1 pad_maximum_fusion.2.refs_4_
  57.8 4.2 %collective-permute-start.14 = (f32[6,128,256]{2,1,0:T(8,128)S(1)}, f32[6,128,256]{2,1,0:T(8,128)S(1)}, u32[]{:S(2)}, u32[]{:S(2)}) collective-permute-start(f32[6,128,256]{2,1,0:T(8,128)S(1)} %pad_maximum_fusion.2.refs_4_), channel_id=1, source_target_pairs={{0,4},{4,0},{8,12},{12,8},{16,20},{20,16},{24,28},{28,24},{1,5},{5... | collective-permute-start | bytes 2359304 | tf_op jit(solution)/shard_map/ppermute | solution.py:212
  62.0 0.2 collective-permute-done.7
  62.2 1.1 %broadcast_select_fusion.6 = (f32[3,128,256]{2,1,0:T(8,128)S(1)}, f32[3,128,256]{2,1,0:T(8,128)S(1)}) fusion(pred[]{:T(512)S(6)} %eq.24, f32[3,128,256]{2,1,0:T(8,128)S(1)} %maximum_select_fusion.1, f32[3,128,256]{2,1,0:T(8,128)S(1)} %collective-permute-done.4, pred[]{:T(512)S(6)} %eq.25, f32[3,128,256]{2,1,0:T(8,128)} %collective-permute-done.5, ...), kind=kLoop, calls=%fused_computation.26 | loop fusion | flops 491520 | bytes 2359298 | tf_op jit(solution)/shard_map/jit(_where)/select_n | solution.py:225
  63.4 4.8 %collective-permute-start.8 = (f32[6,128,256]{2,1,0:T(8,128)S(1)}, f32[6,128,256]{2,1,0:T(8,128)S(1)}, u32[]{:S(2)}, u32[]{:S(2)}) collective-permute-start(f32[6,128,256]{2,1,0:T(8,128)S(1)} %pad_maximum_fusion.1.mine_ref), channel_id=1, source_target_pairs={{0,4},{4,0},{8,12},{12,8},{16,20},{20,16},{24,28},{28,24},{1,5},{5... | collective-permute-start | bytes 2359304 | tf_op jit(solution)/shard_map/ppermute | solution.py:212
  68.3 1.8 %collective-permute-done.8.other_ref = f32[6,128,256]{2,1,0:T(8,128)S(1)} collective-permute-done((f32[6,128,256]{2,1,0:T(8,128)S(1)}, f32[6,128,256]{2,1,0:T(8,128)S(1)}, u32[]{:S(2)}, u32[]{:S(2)}) %collective-permute-start.8) | collective-permute-done | bytes 786464 | tf_op jit(solution)/shard_map/ppermute | solution.py:212
  70.1 32.0 %panels.1 = f32[1,256,2,256]{3,2,1,0:T(2,128)} custom-call(s32[3]{0:T(128)S(1)} %pad_add_fusion.place, f32[6,128,256]{2,1,0:T(8,128)S(1)} %pad_maximum_fusion.1.mine_ref, f32[6,128,256]{2,1,0:T(8,128)S(1)} %collective-permute-done.8.other_ref, f32[256,256]{1,0:T(8,128)S(1)} %bitcast.35, f32[256,256]{1,0:T(8,128)S(1)} %collective-permute-done.2.refs_0_, ...), custom_call_target="tpu_custom_call" | custom-call | tf_op jit(solution)/shard_map/panels/pallas_call | solution.py:270
  (24 shorter events, 0.7 us)
Async XLA Ops:
  1.8 9.2 %collective-permute-start = (f32[256,256]{1,0:T(8,128)S(1)}, f32[256,256]{1,0:T(8,128)S(1)}, u32[]{:S(2)}, u32[]{:S(2)}) collective-permute-start(f32[256,256]{1,0:T(8,128)S(1)} %bitcast.30), channel_id=1, source_target_pairs={{0,3},{1,2},{2,1},{3,0},{4,7},{5,6},{6,5},{7,4},{8,11},{9,10},{10,... | collective-permute-start | bytes 786440 | tf_op jit(solution)/shard_map/ppermute | solution.py:212
  1.9 23.9 %collective-permute-start.1 = (f32[256,256]{1,0:T(8,128)S(1)}, f32[256,256]{1,0:T(8,128)S(1)}, u32[]{:S(2)}, u32[]{:S(2)}) collective-permute-start(f32[256,256]{1,0:T(8,128)S(1)} %bitcast.31), channel_id=1, source_target_pairs={{0,2},{1,3},{2,0},{3,1},{4,6},{5,7},{6,4},{7,5},{8,10},{9,11},{10,... | collective-permute-start | bytes 786440 | tf_op jit(solution)/shard_map/ppermute | solution.py:212
  3.2 22.6 %collective-permute-start.2 = (f32[256,256]{1,0:T(8,128)S(1)}, f32[256,256]{1,0:T(8,128)S(1)}, u32[]{:S(2)}, u32[]{:S(2)}) collective-permute-start(f32[256,256]{1,0:T(8,128)S(1)} %bitcast.32), channel_id=1, source_target_pairs={{0,1},{1,0},{2,3},{3,2},{4,5},{5,4},{6,7},{7,6},{8,9},{9,8},{10,11... | collective-permute-start | bytes 786440 | tf_op jit(solution)/shard_map/ppermute | solution.py:212
  5.5 22.1 %collective-permute-start.9 = (f32[2,128,256]{2,1,0:T(8,128)S(1)}, f32[2,128,256]{2,1,0:T(8,128)S(1)}, u32[]{:S(2)}, u32[]{:S(2)}) collective-permute-start(f32[2,128,256]{2,1,0:T(8,128)S(1)} %select_bitcast_fusion.2), channel_id=1, source_target_pairs={{0,4},{4,0},{8,12},{12,8},{16,20},{20,16},{24,28},{28,24},{1,5},{5... | collective-permute-start | bytes 786440 | tf_op jit(solution)/shard_map/ppermute | solution.py:212
  26.0 3.3 %collective-permute-start.3 = (f32[3,128,256]{2,1,0:T(8,128)S(1)}, f32[3,128,256]{2,1,0:T(8,128)S(1)}, u32[]{:S(2)}, u32[]{:S(2)}) collective-permute-start(f32[3,128,256]{2,1,0:T(8,128)S(1)} %select_bitcast_fusion), channel_id=1, source_target_pairs={{0,4},{4,0},{8,12},{12,8},{16,20},{20,16},{24,28},{28,24},{1,5},{5... | collective-permute-start | bytes 1179656 | tf_op jit(solution)/shard_map/ppermute | solution.py:212
  27.8 13.6 %collective-permute-start.11 = (f32[4,128,256]{2,1,0:T(8,128)S(1)}, f32[4,128,256]{2,1,0:T(8,128)S(1)}, u32[]{:S(2)}, u32[]{:S(2)}) collective-permute-start(f32[4,128,256]{2,1,0:T(8,128)S(1)} %pad_maximum_fusion.3), channel_id=1, source_target_pairs={{0,8},{4,12},{8,0},{12,4},{16,24},{20,28},{24,16},{28,20},{1,9},{5... | collective-permute-start | bytes 1572872 | tf_op jit(solution)/shard_map/ppermute | solution.py:212
  28.1 15.3 %collective-permute-start.10 = (f32[4,128,256]{2,1,0:T(8,128)S(1)}, f32[4,128,256]{2,1,0:T(8,128)S(1)}, u32[]{:S(2)}, u32[]{:S(2)}) collective-permute-start(f32[4,128,256]{2,1,0:T(8,128)S(1)} %pad_maximum_fusion.3), channel_id=1, source_target_pairs={{0,16},{4,20},{8,24},{12,28},{16,0},{20,4},{24,8},{28,12},{1,17},{... | collective-permute-start | bytes 1572872 | tf_op jit(solution)/shard_map/ppermute | solution.py:212
  29.6 20.4 %collective-permute-start.5 = (f32[3,128,256]{2,1,0:T(8,128)S(1)}, f32[3,128,256]{2,1,0:T(8,128)}, u32[]{:S(2)}, u32[]{:S(2)}) collective-permute-start(f32[3,128,256]{2,1,0:T(8,128)S(1)} %maximum_select_fusion.1), channel_id=1, source_target_pairs={{0,8},{4,12},{8,0},{12,4},{16,24},{20,28},{24,16},{28,20},{1,9},{5... | collective-permute-start | bytes 1179656 | tf_op jit(solution)/shard_map/ppermute | solution.py:212
  42.1 10.0 %collective-permute-start.12 = (f32[4,64,256]{2,1,0:T(8,128)}, f32[4,64,256]{2,1,0:T(8,128)S(1)}, u32[]{:S(2)}, u32[]{:S(2)}) collective-permute-start(f32[4,64,256]{2,1,0:T(8,128)} %slice.103), channel_id=1, source_target_pairs={{0,16},{4,20},{8,24},{12,28},{16,0},{20,4},{24,8},{28,12},{1,17},{... | collective-permute-start | bytes 786440 | tf_op jit(solution)/shard_map/ppermute | solution.py:212
  44.1 11.4 %collective-permute-start.13 = (f32[4,64,256]{2,1,0:T(8,128)}, f32[4,64,256]{2,1,0:T(8,128)}, u32[]{:S(2)}, u32[]{:S(2)}) collective-permute-start(f32[4,64,256]{2,1,0:T(8,128)} %slice.104), channel_id=1, source_target_pairs={{0,8},{4,12},{8,0},{12,4},{16,24},{20,28},{24,16},{28,20},{1,9},{5... | collective-permute-start | bytes 786440 | tf_op jit(solution)/shard_map/ppermute | solution.py:212
  44.3 13.0 %collective-permute-start.4 = (f32[3,128,256]{2,1,0:T(8,128)S(1)}, f32[3,128,256]{2,1,0:T(8,128)S(1)}, u32[]{:S(2)}, u32[]{:S(2)}) collective-permute-start(f32[3,128,256]{2,1,0:T(8,128)S(1)} %maximum_select_fusion.1), channel_id=1, source_target_pairs={{0,16},{4,20},{8,24},{12,28},{16,0},{20,4},{24,8},{28,12},{1,17},{... | collective-permute-start | bytes 1179656 | tf_op jit(solution)/shard_map/ppermute | solution.py:212
  50.9 11.1 %collective-permute-start.6 = (f32[3,64,256]{2,1,0:T(8,128)S(1)}, f32[3,64,256]{2,1,0:T(8,128)S(1)}, u32[]{:S(2)}, u32[]{:S(2)}) collective-permute-start(f32[3,64,256]{2,1,0:T(8,128)S(1)} %slice.95), channel_id=1, source_target_pairs={{0,16},{4,20},{8,24},{12,28},{16,0},{20,4},{24,8},{28,12},{1,17},{... | collective-permute-start | bytes 589832 | tf_op jit(solution)/shard_map/ppermute | solution.py:212
  57.4 4.9 %collective-permute-start.7 = (f32[3,64,256]{2,1,0:T(8,128)S(1)}, f32[3,64,256]{2,1,0:T(8,128)S(1)}, u32[]{:S(2)}, u32[]{:S(2)}) collective-permute-start(f32[3,64,256]{2,1,0:T(8,128)S(1)} %slice.96), channel_id=1, source_target_pairs={{0,8},{4,12},{8,0},{12,4},{16,24},{20,28},{24,16},{28,20},{1,9},{5... | collective-permute-start | bytes 589832 | tf_op jit(solution)/shard_map/ppermute | solution.py:212
  57.8 10.5 %collective-permute-start.14 = (f32[6,128,256]{2,1,0:T(8,128)S(1)}, f32[6,128,256]{2,1,0:T(8,128)S(1)}, u32[]{:S(2)}, u32[]{:S(2)}) collective-permute-start(f32[6,128,256]{2,1,0:T(8,128)S(1)} %pad_maximum_fusion.2.refs_4_), channel_id=1, source_target_pairs={{0,4},{4,0},{8,12},{12,8},{16,20},{20,16},{24,28},{28,24},{1,5},{5... | collective-permute-start | bytes 2359304 | tf_op jit(solution)/shard_map/ppermute | solution.py:212
  63.4 6.7 %collective-permute-start.8 = (f32[6,128,256]{2,1,0:T(8,128)S(1)}, f32[6,128,256]{2,1,0:T(8,128)S(1)}, u32[]{:S(2)}, u32[]{:S(2)}) collective-permute-start(f32[6,128,256]{2,1,0:T(8,128)S(1)} %pad_maximum_fusion.1.mine_ref), channel_id=1, source_target_pairs={{0,4},{4,0},{8,12},{12,8},{16,20},{20,16},{24,28},{28,24},{1,5},{5... | collective-permute-start | bytes 2359304 | tf_op jit(solution)/shard_map/ppermute | solution.py:212

commit v3 on v2

v3 whole, which is shorter than its diff:
```python
import jax
import jax.numpy as jnp
from jax import lax
from jax.experimental import pallas as pl
from jax.experimental.pallas import tpu as pltpu
from jax.sharding import PartitionSpec as P

PANELS = 3
HALF = 128
GROUPS = HALF // 8
NN = (((1,), (0,)), ((), ()))
NT = (((1,), (1,)), ((), ()))
TN = (((0,), (0,)), ((), ()))


def lane_b(x, j):
    return jnp.broadcast_to(x[:, j:j + 1], (8, 128))


def sub_b(x, t):
    return jnp.broadcast_to(x[t:t + 1, :], x.shape)


def wide(x):
    return jnp.concatenate([x, x], axis=1)


def split(x):
    high = x.astype(jnp.bfloat16)
    low = (x - high.astype(jnp.float32)).astype(jnp.bfloat16)
    return high, low


def mm(a, b, dims):
    dot = lambda u, v: lax.dot_general(u, v, dims, preferred_element_type=jnp.float32)
    return dot(a[0], b[0]) + (dot(a[0], b[1]) + dot(a[1], b[0]))


def eliminate(rows, shift):
    count = len(rows)
    iota = lax.broadcasted_iota(jnp.int32, (8, 128), 0)
    rows = list(rows)
    out = []
    ahead = None
    for b in range(count):
        k = shift + 8 * b
        cols = {g: [lane_b(rows[g], k + j) for j in range(8)] for g in range(b, count) if g > b or ahead is None}
        if ahead is not None:
            cols[b] = ahead
        ahead = None
        if b + 1 < count:
            ahead = [lane_b(rows[b + 1], k + 8 + j) for j in range(8)]
        da = jnp.ones((8, 128), jnp.float32)
        db = jnp.zeros((8, 128), jnp.float32)
        dc = jnp.ones((8, 128), jnp.float32)
        pp = jnp.zeros((8, 256), jnp.float32)
        for t in range(0, 8, 2):
            first = {j: sub_b(cols[b][j], t) for j in range(t, 8)}
            second = {j: sub_b(cols[b][j], t + 1) for j in range(t + 1, 8)}
            a, q, c = first[t], first[t + 1], second[t + 1]
            rd = 1.0 / (a * c - q * q)
            da = jnp.where((iota == t) | (iota == t + 1), a, da)
            db = jnp.where(iota == t + 1, q, db)
            dc = jnp.where(iota == t + 1, c, dc)
            p0, p1 = sub_b(rows[b], t), sub_b(rows[b], t + 1)
            pp = jnp.where(wide(iota == t + 1), p0, pp)
            for g in range(b, count):
                if g == b and t == 6:
                    continue
                c0, c1 = cols[g][t], cols[g][t + 1]
                n0, n1 = c0 * c - c1 * q, c1 * a - c0 * q
                if g == b:
                    n0 = jnp.where(iota > t + 1, n0, 0.0)
                    n1 = jnp.where(iota > t + 1, n1, 0.0)
                m0, m1 = n0 * rd, n1 * rd
                rows[g] = rows[g] - (wide(m0) * p0 + wide(m1) * p1)
                for j in range(t + 2, 8):
                    cols[g][j] = cols[g][j] - (m0 * first[j] + m1 * second[j])
                if g == b + 1:
                    for j in range(8):
                        ahead[j] = ahead[j] - (m0 * sub_b(c0, j) + m1 * sub_b(c1, j))
        odd = (iota % 2) == 1
        f = jnp.where(odd, db / da, 0.0)
        piv = jnp.where(odd, dc - db * f, da)
        out.append((rows[b] - wide(f) * pp) * wide(lax.rsqrt(piv)))
    return out


def factor_half(aug):
    half = GROUPS // 2
    upper = eliminate([aug[8 * g:8 * g + 8, :] for g in range(half)], 0)
    high, low = split(jnp.concatenate(upper, axis=0))
    left = jnp.concatenate([high[:, :HALF], high[:, :HALF], low[:, :HALF]], axis=0)
    right = jnp.concatenate([high, low, high], axis=0)
    update = lax.dot_general(left, right, TN, preferred_element_type=jnp.float32)
    under = eliminate(
        [aug[8 * g:8 * g + 8, :] - update[8 * g:8 * g + 8, :] for g in range(half, GROUPS)], HALF // 2)
    for g, value in enumerate(upper + under):
        aug[8 * g:8 * g + 8, :] = value


def identity(n):
    r = lax.broadcasted_iota(jnp.int32, (n, n), 0)
    c = lax.broadcasted_iota(jnp.int32, (n, n), 1)
    return jnp.where(r == c, 1.0, 0.0).astype(jnp.float32)


def factor_panel(block, aug, inverse):
    aug[:, :HALF] = block[:HALF, :HALF]
    aug[:, HALF:] = identity(HALF)
    inverse[:HALF, HALF:] = jnp.zeros((HALF, HALF), jnp.float32)

    @pl.loop(0, 2)
    def _(half):
        factor_half(aug)
        sw = split(aug[:, HALF:])

        @pl.when(half == 0)
        def _():
            side = split(block[HALF:, :HALF])
            low = split(mm(side, sw, NT))
            up = split(mm(sw, side, NT))
            inverse[:HALF, :HALF] = aug[:, HALF:]
            inverse[HALF:, :HALF] = mm(low, sw, NN)
            aug[:, :HALF] = block[HALF:, HALF:] - mm(low, up, NN)
            aug[:, HALF:] = identity(HALF)

        @pl.when(half == 1)
        def _():
            inverse[HALF:, :HALF] = -mm(sw, split(inverse[HALF:, :HALF]), NN)
            inverse[HALF:, HALF:] = aug[:, HALF:]


def halves(mine, other, core):
    a, b = mine[...], other[...]
    return jnp.concatenate([jnp.where(core == 0, a, b), jnp.where(core == 0, b, a)], axis=0)


def three(refs, core):
    near, far, near_other, far_other = refs
    return [
        jnp.where(core == 0, near[...], near_other[...]),
        jnp.where(core == 0, near_other[...], near[...]),
        jnp.where(core == 0, far[...], far_other[...]),
    ]


def panels_kernel(place, own_ref, right_ref, b0_ref, b1_ref, b2_ref, *refs):
    lead_refs, top_refs, out_ref = refs[:4], refs[4:8], refs[8]
    lead, aug, inverses, upper, block = refs[9:]
    p, c = place[0], place[1]
    core = lax.rem(p, 2)
    nb = 2 * HALF
    for b in range(6):
        k = b % 3
        mine, other = lead_refs[b // 3], lead_refs[2 + b // 3]
        lead[b] = halves(mine.at[k], other.at[k], core)
    block[...] = lead[0]

    @pl.loop(0, PANELS)
    def _(k):
        factor_panel(block, aug, inverses.at[k])
        w = split(inverses[k])

        @pl.when(k == 0)
        def _():
            u01 = mm(w, split(lead[1]), NT)
            upper[0] = u01
            block[...] = lead[2] - mm(split(u01), split(u01), TN)

        @pl.when(k == 1)
        def _():
            w0 = split(inverses[0])
            u02 = split(mm(w0, split(lead[3]), NT))
            s12 = lead[4].T - mm(split(upper[0]), u02, TN)
            u12 = mm(w, split(s12), NN)
            upper[1] = mm(w0, split(lead[3]), NT)
            upper[2] = u12
            block[...] = lead[5] - mm(u02, u02, TN) - mm(split(u12), split(u12), TN)

    w0, w1, w2 = [split(inverses[k]) for k in range(PANELS)]
    u01, u02, u12 = [split(upper[k]) for k in range(PANELS)]

    x0 = mm(split(b0_ref[...]), w0, NT)
    sx0 = split(x0)
    x1 = mm(split(b1_ref[...] - mm(sx0, u01, NN)), w1, NT)
    sx1 = split(x1)
    x2 = mm(split(b2_ref[...] - mm(sx0, u02, NN) - mm(sx1, u12, NN)), w2, NT)
    sx2 = split(x2)

    @pl.when(c < PANELS)
    def _():
        r = lax.broadcasted_iota(jnp.int32, (nb, nb), 0)
        q = lax.broadcasted_iota(jnp.int32, (nb, nb), 1)
        keep = jnp.where(p > c, 1, 0)
        diagonal = jnp.where(p == c, 1, 0)
        mask = (keep + diagonal * jnp.where(r >= q, 1, 0)) > 0
        panel = jnp.where(c == 0, x0, jnp.where(c == 1, x1, x2))
        out_ref[0, :, 0, :] = jnp.where(mask, panel, 0.0)

    actives = [(c >= PANELS) & (p >= PANELS), p >= PANELS]
    for member, (active, target) in enumerate(zip(actives, (own_ref, right_ref))):
        @pl.when(active)
        def _():
            first = (1 - member) * nb
            t0, t1, t2 = three([ref.at[first:first + nb] for ref in top_refs], core)
            y0 = split(mm(w0, split(t0), NN))
            y1 = split(mm(w1, split(t1 - mm(u01, y0, TN)), NN))
            y2 = split(mm(w2, split(t2 - mm(u02, y0, TN) - mm(u12, y1, TN)), NN))
            out_ref[0, :, member, :] = target[...] - (mm(sx0, y0, NN) + mm(sx1, y1, NN) + mm(sx2, y2, NN))

        @pl.when((p < PANELS) & (c >= PANELS * (1 - member)))
        def _():
            out_ref[0, :, member, :] = jnp.zeros((nb, nb), jnp.float32)


def swap(value, axis, bit):
    n = lax.axis_size(axis)
    return lax.ppermute(value, axis, [(i, i ^ bit) for i in range(n)])


def after(value, *others):
    return lax.optimization_barrier((value, *others))[0]


def launch(value):
    far = swap(value, "row", 6)
    return [value, swap(value, "row", 2), swap(value, "row", 4), far]


def land(came, p, *others):
    n_row = lax.axis_size("row")
    came = lax.optimization_barrier((*came, *others))
    q = (p >> 1) & 3

    def pick(d):
        return jnp.where(d == 0, came[0], jnp.where(d == 1, came[1], jnp.where(d == 2, came[2], came[3])))

    near, far = pick(q), pick(q ^ 1)
    bit = 8
    while bit < n_row:
        near = jnp.where((p & bit) == 0, near, swap(near, "row", bit))
        far = jnp.where((p & bit) == 0, far, swap(far, "row", bit))
        bit *= 2
    return near, far


def shards(kernel):
    n_col = lax.axis_size("col")
    p = lax.axis_index("row")
    c = lax.axis_index("col")
    nb = kernel.shape[1]
    core = p & 1
    f32 = jnp.float32
    own = kernel[0, :, 0, :]
    right = kernel[0, :, 1, :]

    side = [own] + [swap(own, "col", d) for d in range(1, n_col)]
    top = land(launch(jnp.concatenate([right, own])), p)

    blocks = []
    for k in range(PANELS):
        value = side[0]
        for d in range(1, n_col):
            value = jnp.where(jnp.bitwise_xor(c, d) == k, side[d], value)
        blocks.append(value)

    panel = after(jnp.stack(blocks), *top).reshape(PANELS, 2, HALF, nb)
    kept = jnp.where(core == 0, panel[:, 0], panel[:, 1])
    got = swap(jnp.where(core == 0, panel[:, 1], panel[:, 0]), "row", 1)
    even, odd = jnp.where(core == 0, kept, got), jnp.where(core == 0, got, kept)
    group = jnp.where((p >> 1) & 3 == 0, jnp.stack([even[0], odd[0], odd[1]]), even)
    lead = land(launch(group), p)

    place = jnp.stack([p, c]).astype(jnp.int32)
    operands = [
        own, right, *blocks,
        *lead, swap(lead[0], "row", 1), swap(lead[1], "row", 1),
        *top, swap(top[0], "row", 1), swap(top[1], "row", 1),
    ]
    vmem = pl.BlockSpec(memory_space=pltpu.VMEM)
    return pl.pallas_call(
        panels_kernel,
        out_shape=jax.ShapeDtypeStruct(kernel.shape, f32),
        in_specs=[pl.BlockSpec(memory_space=pltpu.SMEM)] + [vmem] * len(operands),
        out_specs=vmem,
        scratch_shapes=[
            pltpu.VMEM((6, nb, nb), f32),
            pltpu.VMEM((HALF, nb), f32),
            pltpu.VMEM((PANELS, nb, nb), f32),
            pltpu.VMEM((PANELS, nb, nb), f32),
            pltpu.VMEM((nb, nb), f32),
        ],
        compiler_params=pltpu.CompilerParams(vmem_limit_bytes=48 * 1024 * 1024),
        name="panels",
    )(place, *operands)


def solution(mesh):
    in_specs = (P(None, "row", None, "col"),)
    out_specs = P(None, "row", None, "col")
    return jax.shard_map(shards, mesh=mesh, in_specs=in_specs, out_specs=out_specs, check_vma=False)
```

time: 102 us -> 86.2 us (0.85)
  the two profiles are of different devices: /device:TPU:27 before, /device:TPU:13 now
where the time goes in v3:
time: 86.2 us; the launch traced here: 86.1 us
  waiting for transfers between devices  42.3 us (49%)
  Pallas kernels  25.2 us (29%)
  starting transfers between devices  15 us (17%)
  local copies, waits for them, and re-layouts  1.76 us (2%)
  other arithmetic  1.68 us (2%)
    ppermute x14, waiting for transfers between devices, swap(): return lax.ppermute(value, axis, [(i, i ^ bit) for i in range(n)])  42.3 us
    pallas_call x1, Pallas kernels, shards(): pl.pallas_call(panels_kernel, out_shape=jax.ShapeDtypeStruct(kernel.shape...  25.2 us
    ppermute x14, starting transfers between devices, swap(): return lax.ppermute(value, axis, [(i, i ^ bit) for i in range(n)])  15 us
  transfers between devices with their start and end apart: 14, of which 8 were waited for; matrix products, arithmetic and copies ran while one was open for 2% of the time, Pallas kernels for 0%

profile of v3, /device:TPU:13, one launch (start us, length us, event | category | flops | bytes accessed | tf_op | source)
XLA Modules:
  0.0 86.1 jit_solution(2152883225008141153)
XLA Ops:
  0.0 1.7 %fusion = (f32[1,256,1,256]{3,2,1,0:T(1,128)S(1)}, f32[1,256,1,256]{3,2,1,0:T(1,128)S(1)}) fusion(f32[1,256,2,256]{3,2,1,0:T(2,128)} %param.1), kind=kLoop, calls=%fused_computation.19 | loop fusion | bytes 1048576 | tf_op jit(solution)/shard_map/slice | solution.py:256
  1.7 1.4 %collective-permute-start = (f32[256,256]{1,0:T(8,128)S(1)}, f32[256,256]{1,0:T(8,128)S(1)}, u32[]{:S(2)}, u32[]{:S(2)}) collective-permute-start(f32[256,256]{1,0:T(8,128)S(1)} %bitcast.37), channel_id=1, source_target_pairs={{0,3},{1,2},{2,1},{3,0},{4,7},{5,6},{6,5},{7,4},{8,11},{9,10},{10,... | collective-permute-start | bytes 786440 | tf_op jit(solution)/shard_map/ppermute | solution.py:219
  3.1 1.1 %collective-permute-start.1 = (f32[256,256]{1,0:T(8,128)S(1)}, f32[256,256]{1,0:T(8,128)S(1)}, u32[]{:S(2)}, u32[]{:S(2)}) collective-permute-start(f32[256,256]{1,0:T(8,128)S(1)} %bitcast.38), channel_id=1, source_target_pairs={{0,2},{1,3},{2,0},{3,1},{4,6},{5,7},{6,4},{7,5},{8,10},{9,11},{10,... | collective-permute-start | bytes 786440 | tf_op jit(solution)/shard_map/ppermute | solution.py:219
  4.2 1.1 %collective-permute-start.2 = (f32[256,256]{1,0:T(8,128)S(1)}, f32[256,256]{1,0:T(8,128)}, u32[]{:S(2)}, u32[]{:S(2)}) collective-permute-start(f32[256,256]{1,0:T(8,128)S(1)} %bitcast.39), channel_id=1, source_target_pairs={{0,1},{1,0},{2,3},{3,2},{4,5},{5,4},{6,7},{7,6},{8,9},{9,8},{10,11... | collective-permute-start | bytes 786440 | tf_op jit(solution)/shard_map/ppermute | solution.py:219
  5.4 1.3 %collective-permute-start.3 = (f32[512,256]{1,0:T(8,128)S(1)}, f32[512,256]{1,0:T(8,128)S(1)}, u32[]{:S(2)}, u32[]{:S(2)}) collective-permute-start(f32[512,256]{1,0:T(8,128)S(1)} %pad_maximum_fusion.1), channel_id=1, source_target_pairs={{0,8},{4,12},{8,0},{12,4},{16,24},{20,28},{24,16},{28,20},{1,9},{5... | collective-permute-start | bytes 1572872 | tf_op jit(solution)/shard_map/ppermute | solution.py:219
  6.6 0.2 collective-permute-start.4
  6.9 13.6 %collective-permute-done = f32[256,256]{1,0:T(8,128)S(1)} collective-permute-done((f32[256,256]{1,0:T(8,128)S(1)}, f32[256,256]{1,0:T(8,128)S(1)}, u32[]{:S(2)}, u32[]{:S(2)}) %collective-permute-start) | collective-permute-done | bytes 262176 | tf_op jit(solution)/shard_map/ppermute | solution.py:219
  20.5 1.2 %collective-permute-start.5 = (f32[512,256]{1,0:T(8,128)S(1)}, f32[512,256]{1,0:T(8,128)S(1)}, u32[]{:S(2)}, u32[]{:S(2)}) collective-permute-start(f32[512,256]{1,0:T(8,128)S(1)} %pad_maximum_fusion.1), channel_id=1, source_target_pairs={{0,24},{4,28},{8,16},{12,20},{16,8},{20,12},{24,0},{28,4},{1,25},{... | collective-permute-start | bytes 1572872 | tf_op jit(solution)/shard_map/ppermute | solution.py:219
  21.7 3.3 %collective-permute-done.1 = f32[256,256]{1,0:T(8,128)S(1)} collective-permute-done((f32[256,256]{1,0:T(8,128)S(1)}, f32[256,256]{1,0:T(8,128)S(1)}, u32[]{:S(2)}, u32[]{:S(2)}) %collective-permute-start.1) | collective-permute-done | bytes 262176 | tf_op jit(solution)/shard_map/ppermute | solution.py:219
  24.9 1.0 %select_select_fusion.4 = (f32[256,256]{1,0:T(8,128)S(1)}, f32[256,256]{1,0:T(8,128)S(1)}, f32[256,256]{1,0:T(8,128)S(1)}) fusion(f32[256,256]{1,0:T(8,128)S(1)} %collective-permute-done, f32[256,256]{1,0:T(8,128)S(1)} %collective-permute-done.1, f32[256,256]{1,0:T(8,128)} %collective-permute-done.2, pred[]{:T(512)S(6)} %eq.66, pred[]{:T(512)S(6)} %eq.65, ...), kind=kLoop, calls=%fused_computation.14 | loop fusion | flops 589824 | bytes 1835017 | tf_op jit(solution)/shard_map/jit(_where)/select_n | solution.py:265
  26.0 0.1 pad_maximum_fusion
  26.0 0.0 collective-permute-done.3
  26.1 6.5 %collective-permute-done.5 = f32[512,256]{1,0:T(8,128)S(1)} collective-permute-done((f32[512,256]{1,0:T(8,128)S(1)}, f32[512,256]{1,0:T(8,128)S(1)}, u32[]{:S(2)}, u32[]{:S(2)}) %collective-permute-start.5) | collective-permute-done | bytes 524320 | tf_op jit(solution)/shard_map/ppermute | solution.py:219
  32.6 0.1 select_select_fusion
  32.8 0.1 select_bitcast_fusion
  32.8 3.2 %collective-permute-start.6 = (f32[3,128,256]{2,1,0:T(8,128)S(1)}, f32[3,128,256]{2,1,0:T(8,128)S(1)}, u32[]{:S(2)}, u32[]{:S(2)}) collective-permute-start(f32[3,128,256]{2,1,0:T(8,128)S(1)} %select_bitcast_fusion), channel_id=1, source_target_pairs={{0,4},{4,0},{8,12},{12,8},{16,20},{20,16},{24,28},{28,24},{1,5},{5... | collective-permute-start | bytes 1179656 | tf_op jit(solution)/shard_map/ppermute | solution.py:219
  36.0 1.3 %collective-permute-done.6 = f32[3,128,256]{2,1,0:T(8,128)S(1)} collective-permute-done((f32[3,128,256]{2,1,0:T(8,128)S(1)}, f32[3,128,256]{2,1,0:T(8,128)S(1)}, u32[]{:S(2)}, u32[]{:S(2)}) %collective-permute-start.6) | collective-permute-done | bytes 393248 | tf_op jit(solution)/shard_map/ppermute | solution.py:219
  37.4 0.1 broadcast_select_fusion
  37.5 0.1 maximum_select_fusion
  37.6 1.3 %collective-permute-start.7 = (f32[3,128,256]{2,1,0:T(8,128)S(1)}, f32[3,128,256]{2,1,0:T(8,128)S(1)}, u32[]{:S(2)}, u32[]{:S(2)}) collective-permute-start(f32[3,128,256]{2,1,0:T(8,128)S(1)} %maximum_select_fusion), channel_id=1, source_target_pairs={{0,8},{4,12},{8,0},{12,4},{16,24},{20,28},{24,16},{28,20},{1,9},{5... | collective-permute-start | bytes 1179656 | tf_op jit(solution)/shard_map/ppermute | solution.py:219
  38.9 0.2 collective-permute-start.8
  39.1 1.2 %collective-permute-start.9 = (f32[3,128,256]{2,1,0:T(8,128)S(1)}, f32[3,128,256]{2,1,0:T(8,128)S(1)}, u32[]{:S(2)}, u32[]{:S(2)}) collective-permute-start(f32[3,128,256]{2,1,0:T(8,128)S(1)} %maximum_select_fusion), channel_id=1, source_target_pairs={{0,24},{4,28},{8,16},{12,20},{16,8},{20,12},{24,0},{28,4},{1,25},{... | collective-permute-start | bytes 1179656 | tf_op jit(solution)/shard_map/ppermute | solution.py:219
  40.3 1.2 %collective-permute-start.12 = (f32[512,256]{1,0:T(8,128)S(1)}, f32[512,256]{1,0:T(8,128)S(1)}, u32[]{:S(2)}, u32[]{:S(2)}) collective-permute-start(f32[512,256]{1,0:T(8,128)S(1)} %get-tuple-element.26.refs_4_), channel_id=1, source_target_pairs={{0,4},{4,0},{8,12},{12,8},{16,20},{20,16},{24,28},{28,24},{1,5},{5... | collective-permute-start | bytes 1572872 | tf_op jit(solution)/shard_map/ppermute | solution.py:219
  41.5 6.5 %collective-permute-done.7 = f32[3,128,256]{2,1,0:T(8,128)S(1)} collective-permute-done((f32[3,128,256]{2,1,0:T(8,128)S(1)}, f32[3,128,256]{2,1,0:T(8,128)S(1)}, u32[]{:S(2)}, u32[]{:S(2)}) %collective-permute-start.7) | collective-permute-done | bytes 393248 | tf_op jit(solution)/shard_map/ppermute | solution.py:219
  48.0 9.3 %collective-permute-done.8 = f32[3,128,256]{2,1,0:T(8,128)S(1)} collective-permute-done((f32[3,128,256]{2,1,0:T(8,128)S(1)}, f32[3,128,256]{2,1,0:T(8,128)S(1)}, u32[]{:S(2)}, u32[]{:S(2)}) %collective-permute-start.8) | collective-permute-done | bytes 393248 | tf_op jit(solution)/shard_map/ppermute | solution.py:219
  57.3 0.1 select_select_fusion.2
  57.4 1.6 %collective-permute-start.10 = (f32[3,128,256]{2,1,0:T(8,128)S(1)}, f32[3,128,256]{2,1,0:T(8,128)S(1)}, u32[]{:S(2)}, u32[]{:S(2)}) collective-permute-start(f32[3,128,256]{2,1,0:T(8,128)S(1)} %get-tuple-element.28.refs_0_), channel_id=1, source_target_pairs={{0,4},{4,0},{8,12},{12,8},{16,20},{20,16},{24,28},{28,24},{1,5},{5... | collective-permute-start | bytes 1179656 | tf_op jit(solution)/shard_map/ppermute | solution.py:219
  59.0 0.1 collective-permute-start.11
  59.1 0.1 pad_add_fusion.place
  59.2 1.2 %collective-permute-done.10.refs_2_ = f32[3,128,256]{2,1,0:T(8,128)S(1)} collective-permute-done((f32[3,128,256]{2,1,0:T(8,128)S(1)}, f32[3,128,256]{2,1,0:T(8,128)S(1)}, u32[]{:S(2)}, u32[]{:S(2)}) %collective-permute-start.10) | collective-permute-done | bytes 393248 | tf_op jit(solution)/shard_map/ppermute | solution.py:219
  60.4 0.6 collective-permute-done.11.refs_3_
  60.9 25.2 %panels.1 = f32[1,256,2,256]{3,2,1,0:T(2,128)} custom-call(s32[2]{0:T(128)S(1)} %pad_add_fusion.place, f32[256,256]{1,0:T(8,128)S(1)} %bitcast.41, f32[256,256]{1,0:T(8,128)S(1)} %bitcast.43, f32[256,256]{1,0:T(8,128)S(1)} %get-tuple-element.31.b0_ref, f32[256,256]{1,0:T(8,128)S(1)} %get-tuple-element.30.b1_ref, f32[256,256]{1,0:T(8,128)S(1)} %get-tuple-element.29.b2_ref, ...), custom_call_target="tpu_custom_call" | custom-call | tf_op jit(solution)/shard_map/panels/pallas_call | solution.py:282
  (11 shorter events, 0.1 us)
Async XLA Ops:
  1.7 18.8 %collective-permute-start = (f32[256,256]{1,0:T(8,128)S(1)}, f32[256,256]{1,0:T(8,128)S(1)}, u32[]{:S(2)}, u32[]{:S(2)}) collective-permute-start(f32[256,256]{1,0:T(8,128)S(1)} %bitcast.37), channel_id=1, source_target_pairs={{0,3},{1,2},{2,1},{3,0},{4,7},{5,6},{6,5},{7,4},{8,11},{9,10},{10,... | collective-permute-start | bytes 786440 | tf_op jit(solution)/shard_map/ppermute | solution.py:219
  3.1 21.8 %collective-permute-start.1 = (f32[256,256]{1,0:T(8,128)S(1)}, f32[256,256]{1,0:T(8,128)S(1)}, u32[]{:S(2)}, u32[]{:S(2)}) collective-permute-start(f32[256,256]{1,0:T(8,128)S(1)} %bitcast.38), channel_id=1, source_target_pairs={{0,2},{1,3},{2,0},{3,1},{4,6},{5,7},{6,4},{7,5},{8,10},{9,11},{10,... | collective-permute-start | bytes 786440 | tf_op jit(solution)/shard_map/ppermute | solution.py:219
  4.2 20.7 %collective-permute-start.2 = (f32[256,256]{1,0:T(8,128)S(1)}, f32[256,256]{1,0:T(8,128)}, u32[]{:S(2)}, u32[]{:S(2)}) collective-permute-start(f32[256,256]{1,0:T(8,128)S(1)} %bitcast.39), channel_id=1, source_target_pairs={{0,1},{1,0},{2,3},{3,2},{4,5},{5,4},{6,7},{7,6},{8,9},{9,8},{10,11... | collective-permute-start | bytes 786440 | tf_op jit(solution)/shard_map/ppermute | solution.py:219
  5.4 20.7 %collective-permute-start.3 = (f32[512,256]{1,0:T(8,128)S(1)}, f32[512,256]{1,0:T(8,128)S(1)}, u32[]{:S(2)}, u32[]{:S(2)}) collective-permute-start(f32[512,256]{1,0:T(8,128)S(1)} %pad_maximum_fusion.1), channel_id=1, source_target_pairs={{0,8},{4,12},{8,0},{12,4},{16,24},{20,28},{24,16},{28,20},{1,9},{5... | collective-permute-start | bytes 1572872 | tf_op jit(solution)/shard_map/ppermute | solution.py:219
  6.6 19.4 %collective-permute-start.4 = (f32[512,256]{1,0:T(8,128)S(1)}, f32[512,256]{1,0:T(8,128)S(1)}, u32[]{:S(2)}, u32[]{:S(2)}) collective-permute-start(f32[512,256]{1,0:T(8,128)S(1)} %pad_maximum_fusion.1), channel_id=1, source_target_pairs={{0,16},{4,20},{8,24},{12,28},{16,0},{20,4},{24,8},{28,12},{1,17},{... | collective-permute-start | bytes 1572872 | tf_op jit(solution)/shard_map/ppermute | solution.py:219
  20.5 12.1 %collective-permute-start.5 = (f32[512,256]{1,0:T(8,128)S(1)}, f32[512,256]{1,0:T(8,128)S(1)}, u32[]{:S(2)}, u32[]{:S(2)}) collective-permute-start(f32[512,256]{1,0:T(8,128)S(1)} %pad_maximum_fusion.1), channel_id=1, source_target_pairs={{0,24},{4,28},{8,16},{12,20},{16,8},{20,12},{24,0},{28,4},{1,25},{... | collective-permute-start | bytes 1572872 | tf_op jit(solution)/shard_map/ppermute | solution.py:219
  32.8 4.6 %collective-permute-start.6 = (f32[3,128,256]{2,1,0:T(8,128)S(1)}, f32[3,128,256]{2,1,0:T(8,128)S(1)}, u32[]{:S(2)}, u32[]{:S(2)}) collective-permute-start(f32[3,128,256]{2,1,0:T(8,128)S(1)} %select_bitcast_fusion), channel_id=1, source_target_pairs={{0,4},{4,0},{8,12},{12,8},{16,20},{20,16},{24,28},{28,24},{1,5},{5... | collective-permute-start | bytes 1179656 | tf_op jit(solution)/shard_map/ppermute | solution.py:219
  37.6 10.4 %collective-permute-start.7 = (f32[3,128,256]{2,1,0:T(8,128)S(1)}, f32[3,128,256]{2,1,0:T(8,128)S(1)}, u32[]{:S(2)}, u32[]{:S(2)}) collective-permute-start(f32[3,128,256]{2,1,0:T(8,128)S(1)} %maximum_select_fusion), channel_id=1, source_target_pairs={{0,8},{4,12},{8,0},{12,4},{16,24},{20,28},{24,16},{28,20},{1,9},{5... | collective-permute-start | bytes 1179656 | tf_op jit(solution)/shard_map/ppermute | solution.py:219
  38.9 18.4 %collective-permute-start.8 = (f32[3,128,256]{2,1,0:T(8,128)S(1)}, f32[3,128,256]{2,1,0:T(8,128)S(1)}, u32[]{:S(2)}, u32[]{:S(2)}) collective-permute-start(f32[3,128,256]{2,1,0:T(8,128)S(1)} %maximum_select_fusion), channel_id=1, source_target_pairs={{0,16},{4,20},{8,24},{12,28},{16,0},{20,4},{24,8},{28,12},{1,17},{... | collective-permute-start | bytes 1179656 | tf_op jit(solution)/shard_map/ppermute | solution.py:219
  39.1 18.2 %collective-permute-start.9 = (f32[3,128,256]{2,1,0:T(8,128)S(1)}, f32[3,128,256]{2,1,0:T(8,128)S(1)}, u32[]{:S(2)}, u32[]{:S(2)}) collective-permute-start(f32[3,128,256]{2,1,0:T(8,128)S(1)} %maximum_select_fusion), channel_id=1, source_target_pairs={{0,24},{4,28},{8,16},{12,20},{16,8},{20,12},{24,0},{28,4},{1,25},{... | collective-permute-start | bytes 1179656 | tf_op jit(solution)/shard_map/ppermute | solution.py:219
  40.3 18.9 %collective-permute-start.12 = (f32[512,256]{1,0:T(8,128)S(1)}, f32[512,256]{1,0:T(8,128)S(1)}, u32[]{:S(2)}, u32[]{:S(2)}) collective-permute-start(f32[512,256]{1,0:T(8,128)S(1)} %get-tuple-element.26.refs_4_), channel_id=1, source_target_pairs={{0,4},{4,0},{8,12},{12,8},{16,20},{20,16},{24,28},{28,24},{1,5},{5... | collective-permute-start | bytes 1572872 | tf_op jit(solution)/shard_map/ppermute | solution.py:219
  41.5 17.7 %collective-permute-start.13 = (f32[512,256]{1,0:T(8,128)S(1)}, f32[512,256]{1,0:T(8,128)S(1)}, u32[]{:S(2)}, u32[]{:S(2)}) collective-permute-start(f32[512,256]{1,0:T(8,128)S(1)} %get-tuple-element.25.refs_5_), channel_id=1, source_target_pairs={{0,4},{4,0},{8,12},{12,8},{16,20},{20,16},{24,28},{28,24},{1,5},{5... | collective-permute-start | bytes 1572872 | tf_op jit(solution)/shard_map/ppermute | solution.py:219
  57.4 2.9 %collective-permute-start.10 = (f32[3,128,256]{2,1,0:T(8,128)S(1)}, f32[3,128,256]{2,1,0:T(8,128)S(1)}, u32[]{:S(2)}, u32[]{:S(2)}) collective-permute-start(f32[3,128,256]{2,1,0:T(8,128)S(1)} %get-tuple-element.28.refs_0_), channel_id=1, source_target_pairs={{0,4},{4,0},{8,12},{12,8},{16,20},{20,16},{24,28},{28,24},{1,5},{5... | collective-permute-start | bytes 1179656 | tf_op jit(solution)/shard_map/ppermute | solution.py:219
  59.0 1.9 %collective-permute-start.11 = (f32[3,128,256]{2,1,0:T(8,128)S(1)}, f32[3,128,256]{2,1,0:T(8,128)S(1)}, u32[]{:S(2)}, u32[]{:S(2)}) collective-permute-start(f32[3,128,256]{2,1,0:T(8,128)S(1)} %get-tuple-element.27.refs_1_), channel_id=1, source_target_pairs={{0,4},{4,0},{8,12},{12,8},{16,20},{20,16},{24,28},{28,24},{1,5},{5... | collective-permute-start | bytes 1179656 | tf_op jit(solution)/shard_map/ppermute | solution.py:219

commit v4 on v3

--- a/solution.py
+++ b/solution.py
@@ -145,40 +145,47 @@
     ]
 
 
-def panels_kernel(place, own_ref, right_ref, b0_ref, b1_ref, b2_ref, *refs):
-    lead_refs, top_refs, out_ref = refs[:4], refs[4:8], refs[8]
-    lead, aug, inverses, upper, block = refs[9:]
+def first_kernel(place, mine_ref, other_ref, inverse_ref, block, aug):
+    block[...] = halves(mine_ref.at[:HALF], other_ref.at[:HALF], lax.rem(place[0], 2))
+    factor_panel(block, aug, inverse_ref)
+
+
+def rest_kernel(place, w0_ref, *refs):
+    pieces, inverses, upper, block, aug = (refs[:2], refs[2:4]), refs[4], refs[5], refs[6], refs[7]
+    core = lax.rem(place[0], 2)
+
+    def piece(group, k):
+        mine, other = pieces[group]
+        return halves(mine.at[k * HALF:(k + 1) * HALF], other.at[k * HALF:(k + 1) * HALF], core)
+
+    w0 = split(w0_ref[...])
+    u01 = mm(w0, split(piece(1, 0)), NN)
+    upper[0] = u01
+    su01 = split(u01)
+    block[...] = piece(1, 1) - mm(su01, su01, TN)
+
+    @pl.loop(0, 2)
+    def _(k):
+        factor_panel(block, aug, inverses.at[k])
+
+        @pl.when(k == 0)
+        def _():
+            u02 = mm(w0, split(piece(0, 1)), NT)
+            upper[1] = u02
+            su02 = split(u02)
+            s12 = split(piece(1, 2).T - mm(split(upper[0]), su02, TN))
+            u12 = mm(split(inverses[0]), s12, NN)
+            upper[2] = u12
+            su12 = split(u12)
+            block[...] = piece(1, 3) - mm(su02, su02, TN) - mm(su12, su12, TN)
+
+
+def apply_kernel(place, own_ref, right_ref, b0_ref, b1_ref, b2_ref, w0_ref, inverses, upper, *refs):
+    top_refs, out_ref = (refs[2:4], refs[:2]), refs[4]
     p, c = place[0], place[1]
     core = lax.rem(p, 2)
     nb = 2 * HALF
-    for b in range(6):
-        k = b % 3
-        mine, other = lead_refs[b // 3], lead_refs[2 + b // 3]
-        lead[b] = halves(mine.at[k], other.at[k], core)
-    block[...] = lead[0]
-
-    @pl.loop(0, PANELS)
-    def _(k):
-        factor_panel(block, aug, inverses.at[k])
-        w = split(inverses[k])
-
-        @pl.when(k == 0)
-        def _():
-            u01 = mm(w, split(lead[1]), NT)
-            upper[0] = u01
-            block[...] = lead[2] - mm(split(u01), split(u01), TN)
-
-        @pl.when(k == 1)
-        def _():
-            w0 = split(inverses[0])
-            u02 = split(mm(w0, split(lead[3]), NT))
-            s12 = lead[4].T - mm(split(upper[0]), u02, TN)
-            u12 = mm(w, split(s12), NN)
-            upper[1] = mm(w0, split(lead[3]), NT)
-            upper[2] = u12
-            block[...] = lead[5] - mm(u02, u02, TN) - mm(split(u12), split(u12), TN)
-
-    w0, w1, w2 = [split(inverses[k]) for k in range(PANELS)]
+    w0, w1, w2 = [split(w) for w in (w0_ref[...], inverses[0], inverses[1])]
     u01, u02, u12 = [split(upper[k]) for k in range(PANELS)]
 
     x0 = mm(split(b0_ref[...]), w0, NT)
@@ -187,6 +194,7 @@
     sx1 = split(x1)
     x2 = mm(split(b2_ref[...] - mm(sx0, u02, NN) - mm(sx1, u12, NN)), w2, NT)
     sx2 = split(x2)
+    row = tuple(jnp.concatenate(parts, axis=1) for parts in zip(sx0, sx1, sx2))
 
     @pl.when(c < PANELS)
     def _():
@@ -198,20 +206,34 @@
         panel = jnp.where(c == 0, x0, jnp.where(c == 1, x1, x2))
         out_ref[0, :, 0, :] = jnp.where(mask, panel, 0.0)
 
-    actives = [(c >= PANELS) & (p >= PANELS), p >= PANELS]
-    for member, (active, target) in enumerate(zip(actives, (own_ref, right_ref))):
-        @pl.when(active)
-        def _():
-            first = (1 - member) * nb
-            t0, t1, t2 = three([ref.at[first:first + nb] for ref in top_refs], core)
-            y0 = split(mm(w0, split(t0), NN))
-            y1 = split(mm(w1, split(t1 - mm(u01, y0, TN)), NN))
-            y2 = split(mm(w2, split(t2 - mm(u02, y0, TN) - mm(u12, y1, TN)), NN))
-            out_ref[0, :, member, :] = target[...] - (mm(sx0, y0, NN) + mm(sx1, y1, NN) + mm(sx2, y2, NN))
-
-        @pl.when((p < PANELS) & (c >= PANELS * (1 - member)))
-        def _():
-            out_ref[0, :, member, :] = jnp.zeros((nb, nb), jnp.float32)
+    def remaining(members):
+        tops = []
+        for member in members:
+            tops.append(three([ref.at[k:k + nb] for ref in top_refs[member] for k in (0, nb)], core))
+        t0, t1, t2 = [jnp.concatenate(t, axis=1) for t in zip(*tops)]
+        y0 = split(mm(w0, split(t0), NN))
+        y1 = split(mm(w1, split(t1 - mm(u01, y0, TN)), NN))
+        y2 = split(mm(w2, split(t2 - mm(u02, y0, TN) - mm(u12, y1, TN)), NN))
+        column = tuple(jnp.concatenate(parts, axis=0) for parts in zip(y0, y1, y2))
+        loss = mm(row, column, NN)
+        for i, member in enumerate(members):
+            out_ref[0, :, member, :] = (own_ref, right_ref)[member][...] - loss[:, i * nb:(i + 1) * nb]
+
+    @pl.when((p >= PANELS) & (c >= PANELS))
+    def _():
+        remaining((0, 1))
+
+    @pl.when((p >= PANELS) & (c < PANELS))
+    def _():
+        remaining((1,))
+
+    @pl.when(p < PANELS)
+    def _():
+        out_ref[0, :, 1, :] = jnp.zeros((nb, nb), jnp.float32)
+
+    @pl.when((p < PANELS) & (c >= PANELS))
+    def _():
+        out_ref[0, :, 0, :] = jnp.zeros((nb, nb), jnp.float32)
 
 
 def swap(value, axis, bit):
@@ -245,55 +267,112 @@
     return near, far
 
 
+def steps_right(s, n_col):
+    return [(k + s, k + s + 1) for k in range(PANELS) if k + s + 1 < n_col]
+
+
+def along_col(own, right_block, c):
+    n_row, n_col = lax.axis_size("row"), lax.axis_size("col")
+    direct = n_col == PANELS + 1
+    right, left, chips = [], [], [right_block]
+    value = back = own
+    for s in range(n_col - 2):
+        came = [lax.ppermute(value, "col", steps_right(s, n_col))]
+        if s < PANELS - 1:
+            pairs = [(r * n_col + k - s, r * n_col + k - s - 1) for r in range(n_row) for k in range(s + 1, PANELS)]
+            if direct and s == 0:
+                pairs += [(r * n_col, r * n_col + n_col - 1) for r in (0, 2)]
+            came.append(lax.ppermute(back, ("row", "col"), pairs))
+            if s == 0:
+                came += [swap(right_block, "row", 2), swap(right_block, "row", 4)]
+            if s == 1:
+                came.append(swap(chips[2], "row", 2))
+            value, back, *more = lax.optimization_barrier(tuple(came))
+            left.append(back)
+            chips += more
+        else:
+            value = came[0]
+        right.append(value)
+
+    def pick(k):
+        value = own
+        for s, came in enumerate(right):
+            value = jnp.where(c == k + 1 + s, came, value)
+        for s, came in enumerate(left):
+            value = jnp.where(c == k - 1 - s, came, value)
+        return value
+
+    def start_last(*others):
+        return lax.ppermute(after(value, *others), "col", steps_right(n_col - 2, n_col))
+
+    def finish(came, *others):
+        return jnp.where(c == n_col - 1, after(came, *others), pick(0))
+
+    if direct:
+        ahead = jnp.where(c == n_col - 1, left[0], pick(0))
+    else:
+        ahead = finish(start_last())
+    return ahead, [None, pick(1), pick(2)], chips, start_last, finish
+
+
 def shards(kernel):
     n_col = lax.axis_size("col")
     p = lax.axis_index("row")
     c = lax.axis_index("col")
     nb = kernel.shape[1]
     core = p & 1
+    chip = (p >> 1) & 3
     f32 = jnp.float32
     own = kernel[0, :, 0, :]
     right = kernel[0, :, 1, :]
-
-    side = [own] + [swap(own, "col", d) for d in range(1, n_col)]
-    top = land(launch(jnp.concatenate([right, own])), p)
-
-    blocks = []
-    for k in range(PANELS):
-        value = side[0]
-        for d in range(1, n_col):
-            value = jnp.where(jnp.bitwise_xor(c, d) == k, side[d], value)
-        blocks.append(value)
-
-    panel = after(jnp.stack(blocks), *top).reshape(PANELS, 2, HALF, nb)
-    kept = jnp.where(core == 0, panel[:, 0], panel[:, 1])
-    got = swap(jnp.where(core == 0, panel[:, 1], panel[:, 0]), "row", 1)
-    even, odd = jnp.where(core == 0, kept, got), jnp.where(core == 0, got, kept)
-    group = jnp.where((p >> 1) & 3 == 0, jnp.stack([even[0], odd[0], odd[1]]), even)
-    lead = land(launch(group), p)
-
     place = jnp.stack([p, c]).astype(jnp.int32)
-    operands = [
-        own, right, *blocks,
-        *lead, swap(lead[0], "row", 1), swap(lead[1], "row", 1),
-        *top, swap(top[0], "row", 1), swap(top[1], "row", 1),
-    ]
+    smem = pl.BlockSpec(memory_space=pltpu.SMEM)
     vmem = pl.BlockSpec(memory_space=pltpu.VMEM)
-    return pl.pallas_call(
-        panels_kernel,
-        out_shape=jax.ShapeDtypeStruct(kernel.shape, f32),
-        in_specs=[pl.BlockSpec(memory_space=pltpu.SMEM)] + [vmem] * len(operands),
-        out_specs=vmem,
-        scratch_shapes=[
-            pltpu.VMEM((6, nb, nb), f32),
-            pltpu.VMEM((HALF, nb), f32),
-            pltpu.VMEM((PANELS, nb, nb), f32),
-            pltpu.VMEM((PANELS, nb, nb), f32),
-            pltpu.VMEM((nb, nb), f32),
-        ],
-        compiler_params=pltpu.CompilerParams(vmem_limit_bytes=48 * 1024 * 1024),
-        name="panels",
-    )(place, *operands)
+    square = jax.ShapeDtypeStruct((nb, nb), f32)
+    chain = [pltpu.VMEM((nb, nb), f32), pltpu.VMEM((HALF, nb), f32)]
+
+    def call(body, name, outs, scratch, micros, *operands):
+        return pl.pallas_call(
+            body,
+            out_shape=outs,
+            in_specs=[smem] + [vmem] * len(operands),
+            out_specs=jax.tree.map(lambda _: vmem, outs),
+            scratch_shapes=scratch,
+            compiler_params=pltpu.CompilerParams(vmem_limit_bytes=24 * 1024 * 1024),
+            cost_estimate=pl.CostEstimate(flops=0, bytes_accessed=int(micros * 3.5e6), transcendentals=0),
+            name=name,
+        )(place, *operands)
+
+    def cut(blocks):
+        parts = blocks.reshape(-1, 2, HALF, nb)
+        kept = jnp.where(core == 0, parts[:, 0], parts[:, 1])
+        got = swap(jnp.where(core == 0, parts[:, 1], parts[:, 0]), "row", 1)
+        return jnp.where(core == 0, kept, got), jnp.where(core == 0, got, kept)
+
+    def cross(*values):
+        mine = jnp.concatenate(values)
+        return [mine, swap(mine, "row", 1)]
+
+    ahead, blocks, top, start_last, finish = along_col(own, right, c)
+    even, odd = cut(jnp.stack([ahead, blocks[1], blocks[2]]))
+    one = launch(even[0])
+    top = cross(*land(top, p))
+    one = land(one, p, *top)
+    two = launch(jnp.concatenate([even[1], jnp.where(chip == 0, odd[1], even[2])]))
+    last = start_last(*one)
+    one = cross(*one)
+    w0 = call(first_kernel, "first", square, chain, 6.5, *one)
+    blocks[0] = finish(last, w0)
+    two = cross(*land(two, p, w0, blocks[0]))
+    top_own = launch(after(own, w0))
+    inverses, upper = call(
+        rest_kernel, "rest",
+        (jax.ShapeDtypeStruct((2, nb, nb), f32), jax.ShapeDtypeStruct((PANELS, nb, nb), f32)), chain, 15.0,
+        w0, *one, *two)
+    top_own = cross(*land(top_own, p, inverses))
+    return call(
+        apply_kernel, "apply", jax.ShapeDtypeStruct(kernel.shape, f32), [], 6.0,
+        own, right, *blocks, w0, inverses, upper, *top, *top_own)
 
 
 def solution(mesh):

time: 86.2 us -> 81.6 us (0.947)
  waiting for transfers between devices: 42.3 us -> 22.3 us
  starting transfers between devices: 15 us -> 28.3 us
  Pallas kernels: 25.2 us -> 26.5 us
    ppermute x14 -> x17, waiting for transfers between devices: 42.3 us -> 14.2 us  [swap(): return lax.ppermute(value, axis, [(i, i ^ bit) for i in range(n)])]
    ppermute x0 -> x5, starting transfers between devices: none -> 10.5 us  [the longest x2 6.41 us: along_col(): came = [lax.ppermute(value, 'col', steps_right(s, n_col))]]
    ppermute x0 -> x5, waiting for transfers between devices: none -> 8.06 us  [the longest x2 4.21 us: along_col(): came.append(lax.ppermute(back, ('row', 'col'), pairs))]
    ppermute x14 -> x17, starting transfers between devices: 15 us -> 17.9 us  [swap(): return lax.ppermute(value, axis, [(i, i ^ bit) for i in range(n)])]
    pallas_call x1 -> x3, Pallas kernels: 25.2 us -> 26.5 us  [call(): pl.pallas_call(body, out_shape=outs, in_specs=[smem] + [vmem] * len(opera...]
    select_n x5 -> x4, other arithmetic: 1.26 us -> 0.29 us  [the longest x1 0.12 us: along_col(): ahead = jnp.where(c == n_col - 1, left[0], pick(0))]
    select_n x2 -> x4, other arithmetic: 0.25 us -> 1.2 us  [pick(): jnp.where(d == 0, came[0], jnp.where(d == 1, came[1], jnp.where(d == 2, c...]
  transfers between devices with their start and end apart: 14 -> 22, of which waited for: 8 -> 12; matrix products, arithmetic and copies ran while one was open for 2% -> 2% of each run, Pallas kernels for 0% -> 26%
where the time goes in v4:
time: 81.6 us; the launch traced here: 81.3 us
  starting transfers between devices  28.3 us (35%)
  Pallas kernels  26.5 us (32%)
  waiting for transfers between devices  22.3 us (27%)
  local copies, waits for them, and re-layouts  2.17 us (3%)
  other arithmetic  1.81 us (2%)
    pallas_call x3, Pallas kernels, call(): pl.pallas_call(body, out_shape=outs, in_specs=[smem] + [vmem] * len(opera...  26.5 us
    ppermute x17, starting transfers between devices, swap(): return lax.ppermute(value, axis, [(i, i ^ bit) for i in range(n)])  17.9 us
    ppermute x17, waiting for transfers between devices, swap(): return lax.ppermute(value, axis, [(i, i ^ bit) for i in range(n)])  14.2 us
    ppermute x2, starting transfers between devices, along_col(): came = [lax.ppermute(value, 'col', steps_right(s, n_col))]  6.41 us
    ppermute x2, waiting for transfers between devices, along_col(): came.append(lax.ppermute(back, ('row', 'col'), pairs))  4.21 us
    ppermute x2, waiting for transfers between devices, along_col(): came = [lax.ppermute(value, 'col', steps_right(s, n_col))]  3.85 us
    ppermute x2, starting transfers between devices, along_col(): came.append(lax.ppermute(back, ('row', 'col'), pairs))  3.4 us
    slice x1, local copies, waits for them, and re-layouts, shards(): right = kernel[0, :, 1, :]  1.77 us
  transfers between devices with their start and end apart: 22, of which 12 were waited for; matrix products, arithmetic and copies ran while one was open for 2% of the time, Pallas kernels for 26%

profile of v4, /device:TPU:13, one launch (start us, length us, event | category | flops | bytes accessed | tf_op | source)
XLA Modules:
  0.0 81.3 jit_solution(2877064721656843177)
XLA Ops:
  0.0 1.8 %fusion.1 = (f32[1,256,1,256]{3,2,1,0:T(1,128)S(1)}, f32[1,256,1,256]{3,2,1,0:T(1,128)S(1)}) fusion(f32[1,256,2,256]{3,2,1,0:T(2,128)} %param.1), kind=kLoop, calls=%fused_computation.30 | loop fusion | bytes 1048576 | tf_op jit(solution)/shard_map/slice | solution.py:327
  1.8 3.2 %collective-permute-start = (f32[256,256]{1,0:T(8,128)S(1)}, f32[256,256]{1,0:T(8,128)S(1)}, u32[]{:S(2)}, u32[]{:S(2)}) collective-permute-start(f32[256,256]{1,0:T(8,128)S(1)} %bitcast.35), channel_id=1, source_target_pairs={{0,1},{1,2},{2,3},{4,5},{5,6},{6,7},{8,9},{9,10},{10,11},{12,13},{... | collective-permute-start | bytes 786440 | tf_op jit(solution)/shard_map/ppermute | solution.py:280
  5.0 2.1 %collective-permute-start.1 = (f32[256,256]{1,0:T(8,128)S(1)}, f32[256,256]{1,0:T(8,128)S(1)}, u32[]{:S(2)}, u32[]{:S(2)}) collective-permute-start(f32[256,256]{1,0:T(8,128)S(1)} %bitcast.36), channel_id=1, source_target_pairs={{1,0},{2,1},{5,4},{6,5},{9,8},{10,9},{13,12},{14,13},{17,16},{18,1... | collective-permute-start | bytes 786440 | tf_op jit(solution)/shard_map/ppermute | solution.py:285
  7.1 1.3 %collective-permute-start.2 = (f32[256,256]{1,0:T(8,128)S(1)}, f32[256,256]{1,0:T(8,128)S(1)}, u32[]{:S(2)}, u32[]{:S(2)}) collective-permute-start(f32[256,256]{1,0:T(8,128)S(1)} %bitcast.42), channel_id=1, source_target_pairs={{0,8},{4,12},{8,0},{12,4},{16,24},{20,28},{24,16},{28,20},{1,9},{5... | collective-permute-start | bytes 786440 | tf_op jit(solution)/shard_map/ppermute | solution.py:241
  8.6 2.2 %collective-permute-done = f32[256,256]{1,0:T(8,128)S(1)} collective-permute-done((f32[256,256]{1,0:T(8,128)S(1)}, f32[256,256]{1,0:T(8,128)S(1)}, u32[]{:S(2)}, u32[]{:S(2)}) %collective-permute-start) | collective-permute-done | bytes 262176 | tf_op jit(solution)/shard_map/ppermute | solution.py:280
  10.9 2.9 %collective-permute-done.1 = f32[256,256]{1,0:T(8,128)S(1)} collective-permute-done((f32[256,256]{1,0:T(8,128)S(1)}, f32[256,256]{1,0:T(8,128)S(1)}, u32[]{:S(2)}, u32[]{:S(2)}) %collective-permute-start.1) | collective-permute-done | bytes 262176 | tf_op jit(solution)/shard_map/ppermute | solution.py:285
  13.8 0.9 %collective-permute-done.3 = f32[256,256]{1,0:T(8,128)S(1)} collective-permute-done((f32[256,256]{1,0:T(8,128)S(1)}, f32[256,256]{1,0:T(8,128)S(1)}, u32[]{:S(2)}, u32[]{:S(2)}) %collective-permute-start.3) | collective-permute-done | bytes 262176 | tf_op jit(solution)/shard_map/ppermute | solution.py:241
  14.7 3.2 %collective-permute-start.4 = (f32[256,256]{1,0:T(8,128)S(1)}, f32[256,256]{1,0:T(8,128)S(1)}, u32[]{:S(2)}, u32[]{:S(2)}) collective-permute-start(f32[256,256]{1,0:T(8,128)S(1)} %collective-permute-done), channel_id=1, source_target_pairs={{1,2},{2,3},{5,6},{6,7},{9,10},{10,11},{13,14},{14,15},{17,18},{18... | collective-permute-start | bytes 786440 | tf_op jit(solution)/shard_map/ppermute | solution.py:280
  17.9 1.3 %collective-permute-start.5 = (f32[256,256]{1,0:T(8,128)S(1)}, f32[256,256]{1,0:T(8,128)S(1)}, u32[]{:S(2)}, u32[]{:S(2)}) collective-permute-start(f32[256,256]{1,0:T(8,128)S(1)} %collective-permute-done.1), channel_id=1, source_target_pairs={{1,0},{5,4},{9,8},{13,12},{17,16},{21,20},{25,24},{29,28}} | collective-permute-start | bytes 786440 | tf_op jit(solution)/shard_map/ppermute | solution.py:285
  19.6 1.6 %collective-permute-done.4 = f32[256,256]{1,0:T(8,128)S(1)} collective-permute-done((f32[256,256]{1,0:T(8,128)S(1)}, f32[256,256]{1,0:T(8,128)S(1)}, u32[]{:S(2)}, u32[]{:S(2)}) %collective-permute-start.4) | collective-permute-done | bytes 262176 | tf_op jit(solution)/shard_map/ppermute | solution.py:280
  21.2 1.3 %collective-permute-done.5 = f32[256,256]{1,0:T(8,128)S(1)} collective-permute-done((f32[256,256]{1,0:T(8,128)S(1)}, f32[256,256]{1,0:T(8,128)S(1)}, u32[]{:S(2)}, u32[]{:S(2)}) %collective-permute-start.5) | collective-permute-done | bytes 262176 | tf_op jit(solution)/shard_map/ppermute | solution.py:285
  22.5 2.1 %collective-permute-done.6 = f32[256,256]{1,0:T(8,128)} collective-permute-done((f32[256,256]{1,0:T(8,128)S(1)}, f32[256,256]{1,0:T(8,128)}, u32[]{:S(2)}, u32[]{:S(2)}) %collective-permute-start.6) | collective-permute-done | bytes 262176 | tf_op jit(solution)/shard_map/ppermute | solution.py:241
  24.9 3.9 %collective-permute-start.7 = (f32[3,128,256]{2,1,0:T(8,128)S(1)}, f32[3,128,256]{2,1,0:T(8,128)S(1)}, u32[]{:S(2)}, u32[]{:S(2)}) collective-permute-start(f32[3,128,256]{2,1,0:T(8,128)S(1)} %select_bitcast_fusion), channel_id=1, source_target_pairs={{0,4},{4,0},{8,12},{12,8},{16,20},{20,16},{24,28},{28,24},{1,5},{5... | collective-permute-start | bytes 1179656 | tf_op jit(solution)/shard_map/ppermute | solution.py:241
  28.8 1.0 %select_select_fusion.5 = (f32[256,256]{1,0:T(8,128)S(1)}, f32[256,256]{1,0:T(8,128)S(1)}) fusion(f32[256,256]{1,0:T(8,128)S(1)} %bitcast.44, f32[256,256]{1,0:T(8,128)S(1)} %collective-permute-done.2, f32[256,256]{1,0:T(8,128)S(1)} %collective-permute-done.3, f32[256,256]{1,0:T(8,128)} %collective-permute-done.6, pred[]{:T(512)S(6)} %eq.38, pred[]{:T(512)S(6)} %eq.37, ...), kind=kLoop, calls=%fused_computation.15 | loop fusion | flops 393216 | bytes 1572870 | tf_op jit(solution)/shard_map/jit(_where)/select_n | solution.py:259
  30.6 1.2 %collective-permute-start.8 = (f32[128,256]{1,0:T(8,128)S(1)}, f32[128,256]{1,0:T(8,128)S(1)}, u32[]{:S(2)}, u32[]{:S(2)}) collective-permute-start(f32[128,256]{1,0:T(8,128)S(1)} %get-tuple-element.44), channel_id=1, source_target_pairs={{0,8},{4,12},{8,0},{12,4},{16,24},{20,28},{24,16},{28,20},{1,9},{5... | collective-permute-start | bytes 393224 | tf_op jit(solution)/shard_map/ppermute | solution.py:241
  31.8 1.2 %collective-permute-start.9 = (f32[128,256]{1,0:T(8,128)S(1)}, f32[128,256]{1,0:T(8,128)S(1)}, u32[]{:S(2)}, u32[]{:S(2)}) collective-permute-start(f32[128,256]{1,0:T(8,128)S(1)} %get-tuple-element.44), channel_id=1, source_target_pairs={{0,16},{4,20},{8,24},{12,28},{16,0},{20,4},{24,8},{28,12},{1,17},{... | collective-permute-start | bytes 393224 | tf_op jit(solution)/shard_map/ppermute | solution.py:241
  33.0 3.0 %collective-permute-done.10 = f32[128,256]{1,0:T(8,128)S(1)} collective-permute-done((f32[128,256]{1,0:T(8,128)S(1)}, f32[128,256]{1,0:T(8,128)S(1)}, u32[]{:S(2)}, u32[]{:S(2)}) %collective-permute-start.10) | collective-permute-done | bytes 131104 | tf_op jit(solution)/shard_map/ppermute | solution.py:241
  36.0 1.9 %collective-permute-done.8 = f32[128,256]{1,0:T(8,128)S(1)} collective-permute-done((f32[128,256]{1,0:T(8,128)S(1)}, f32[128,256]{1,0:T(8,128)S(1)}, u32[]{:S(2)}, u32[]{:S(2)}) %collective-permute-start.8) | collective-permute-done | bytes 131104 | tf_op jit(solution)/shard_map/ppermute | solution.py:241
  37.8 1.7 %collective-permute-done.9 = f32[128,256]{1,0:T(8,128)S(1)} collective-permute-done((f32[128,256]{1,0:T(8,128)S(1)}, f32[128,256]{1,0:T(8,128)S(1)}, u32[]{:S(2)}, u32[]{:S(2)}) %collective-permute-start.9) | collective-permute-done | bytes 131104 | tf_op jit(solution)/shard_map/ppermute | solution.py:241
  39.6 0.6 collective-permute-start.13
  40.1 0.4 copy-done.1
  40.5 0.7 collective-permute-start.12
  41.5 2.4 %collective-permute-start.16 = (f32[256,256]{1,0:T(8,128)S(1)}, f32[256,256]{1,0:T(8,128)S(1)}, u32[]{:S(2)}, u32[]{:S(2)}) collective-permute-start(f32[256,256]{1,0:T(8,128)S(1)} %pad_maximum_fusion.5), channel_id=1, source_target_pairs={{0,24},{4,28},{8,16},{12,20},{16,8},{20,12},{24,0},{28,4},{1,25},{... | collective-permute-start | bytes 786440 | tf_op jit(solution)/shard_map/ppermute | solution.py:241
  44.0 6.5 %first.1.w0_ref = f32[256,256]{1,0:T(8,128)S(1)} custom-call(s32[2]{0:T(128)S(1)} %pad_add_fusion.place, f32[256,256]{1,0:T(8,128)S(1)} %pad_maximum_fusion.4.mine_ref.refs_0_, f32[256,256]{1,0:T(8,128)S(1)} %collective-permute-done.13.other_ref.refs_1_), custom_call_target="tpu_custom_call" | custom-call | bytes 22750000 | tf_op jit(solution)/shard_map/first/pallas_call | solution.py:335
  50.6 2.9 %collective-permute-done.16 = f32[256,256]{1,0:T(8,128)S(1)} collective-permute-done((f32[256,256]{1,0:T(8,128)S(1)}, f32[256,256]{1,0:T(8,128)S(1)}, u32[]{:S(2)}, u32[]{:S(2)}) %collective-permute-start.16) | collective-permute-done | bytes 262176 | tf_op jit(solution)/shard_map/ppermute | solution.py:241
  53.7 2.4 %collective-permute-start.17 = (f32[512,256]{1,0:T(8,128)S(1)}, f32[512,256]{1,0:T(8,128)S(1)}, u32[]{:S(2)}, u32[]{:S(2)}) collective-permute-start(f32[512,256]{1,0:T(8,128)S(1)} %pad_maximum_fusion.2.refs_2_), channel_id=1, source_target_pairs={{0,4},{4,0},{8,12},{12,8},{16,20},{20,16},{24,28},{28,24},{1,5},{5... | collective-permute-start | bytes 1572872 | tf_op jit(solution)/shard_map/ppermute | solution.py:241
  56.0 1.2 %collective-permute-start.18 = (f32[256,256]{1,0:T(8,128)S(1)}, f32[256,256]{1,0:T(8,128)S(1)}, u32[]{:S(2)}, u32[]{:S(2)}) collective-permute-start(f32[256,256]{1,0:T(8,128)S(1)} %bitcast.37), channel_id=1, source_target_pairs={{0,8},{4,12},{8,0},{12,4},{16,24},{20,28},{24,16},{28,20},{1,9},{5... | collective-permute-start | bytes 786440 | tf_op jit(solution)/shard_map/ppermute | solution.py:241
  57.3 1.4 %collective-permute-start.20 = (f32[256,256]{1,0:T(8,128)S(1)}, f32[256,256]{1,0:T(8,128)S(1)}, u32[]{:S(2)}, u32[]{:S(2)}) collective-permute-start(f32[256,256]{1,0:T(8,128)S(1)} %bitcast.39), channel_id=1, source_target_pairs={{0,24},{4,28},{8,16},{12,20},{16,8},{20,12},{24,0},{28,4},{1,25},{... | collective-permute-start | bytes 786440 | tf_op jit(solution)/shard_map/ppermute | solution.py:241
  58.7 14.7 %rest.1 = (f32[2,256,256]{2,1,0:T(8,128)S(1)}, f32[3,256,256]{2,1,0:T(8,128)S(1)}) custom-call(s32[2]{0:T(128)S(1)} %pad_add_fusion.place, f32[256,256]{1,0:T(8,128)S(1)} %first.1.w0_ref, f32[256,256]{1,0:T(8,128)S(1)} %pad_maximum_fusion.4.mine_ref.refs_0_, f32[256,256]{1,0:T(8,128)S(1)} %collective-permute-done.13.other_ref.refs_1_, ...), custom_call_target="tpu_custom_call" | custom-call | bytes 52500000 | tf_op jit(solution)/shard_map/rest/pallas_call | solution.py:335
  73.5 1.0 %collective-permute-start.21 = (f32[512,256]{1,0:T(8,128)S(1)}, f32[512,256]{1,0:T(8,128)S(1)}, u32[]{:S(2)}, u32[]{:S(2)}) collective-permute-start(f32[512,256]{1,0:T(8,128)S(1)} %pad_maximum_fusion.3.refs_2_), channel_id=1, source_target_pairs={{0,4},{4,0},{8,12},{12,8},{16,20},{20,16},{24,28},{28,24},{1,5},{5... | collective-permute-start | bytes 1572872 | tf_op jit(solution)/shard_map/ppermute | solution.py:241
  74.5 1.5 %collective-permute-done.21.refs_3_ = f32[512,256]{1,0:T(8,128)S(1)} collective-permute-done((f32[512,256]{1,0:T(8,128)S(1)}, f32[512,256]{1,0:T(8,128)S(1)}, u32[]{:S(2)}, u32[]{:S(2)}) %collective-permute-start.21) | collective-permute-done | bytes 524320 | tf_op jit(solution)/shard_map/ppermute | solution.py:241
  76.0 5.3 %apply.1 = f32[1,256,2,256]{3,2,1,0:T(2,128)} custom-call(s32[2]{0:T(128)S(1)} %pad_add_fusion.place, f32[256,256]{1,0:T(8,128)S(1)} %bitcast.41, f32[256,256]{1,0:T(8,128)S(1)} %bitcast.45, f32[256,256]{1,0:T(8,128)S(1)} %broadcast_select_fusion.1.b0_ref, f32[256,256]{1,0:T(8,128)S(1)} %get-tuple-element.65.b1_ref, ...), custom_call_target="tpu_custom_call" | custom-call | bytes 21000000 | tf_op jit(solution)/shard_map/apply/pallas_call | solution.py:335
  (38 shorter events, 2.3 us)
Async XLA Ops:
  1.8 9.1 %collective-permute-start = (f32[256,256]{1,0:T(8,128)S(1)}, f32[256,256]{1,0:T(8,128)S(1)}, u32[]{:S(2)}, u32[]{:S(2)}) collective-permute-start(f32[256,256]{1,0:T(8,128)S(1)} %bitcast.35), channel_id=1, source_target_pairs={{0,1},{1,2},{2,3},{4,5},{5,6},{6,7},{8,9},{9,10},{10,11},{12,13},{... | collective-permute-start | bytes 786440 | tf_op jit(solution)/shard_map/ppermute | solution.py:280
  5.0 8.8 %collective-permute-start.1 = (f32[256,256]{1,0:T(8,128)S(1)}, f32[256,256]{1,0:T(8,128)S(1)}, u32[]{:S(2)}, u32[]{:S(2)}) collective-permute-start(f32[256,256]{1,0:T(8,128)S(1)} %bitcast.36), channel_id=1, source_target_pairs={{1,0},{2,1},{5,4},{6,5},{9,8},{10,9},{13,12},{14,13},{17,16},{18,1... | collective-permute-start | bytes 786440 | tf_op jit(solution)/shard_map/ppermute | solution.py:285
  7.1 6.6 %collective-permute-start.2 = (f32[256,256]{1,0:T(8,128)S(1)}, f32[256,256]{1,0:T(8,128)S(1)}, u32[]{:S(2)}, u32[]{:S(2)}) collective-permute-start(f32[256,256]{1,0:T(8,128)S(1)} %bitcast.42), channel_id=1, source_target_pairs={{0,8},{4,12},{8,0},{12,4},{16,24},{20,28},{24,16},{28,20},{1,9},{5... | collective-permute-start | bytes 786440 | tf_op jit(solution)/shard_map/ppermute | solution.py:241
  8.4 6.3 %collective-permute-start.3 = (f32[256,256]{1,0:T(8,128)S(1)}, f32[256,256]{1,0:T(8,128)S(1)}, u32[]{:S(2)}, u32[]{:S(2)}) collective-permute-start(f32[256,256]{1,0:T(8,128)S(1)} %bitcast.43), channel_id=1, source_target_pairs={{0,16},{4,20},{8,24},{12,28},{16,0},{20,4},{24,8},{28,12},{1,17},{... | collective-permute-start | bytes 786440 | tf_op jit(solution)/shard_map/ppermute | solution.py:241
  14.7 6.5 %collective-permute-start.4 = (f32[256,256]{1,0:T(8,128)S(1)}, f32[256,256]{1,0:T(8,128)S(1)}, u32[]{:S(2)}, u32[]{:S(2)}) collective-permute-start(f32[256,256]{1,0:T(8,128)S(1)} %collective-permute-done), channel_id=1, source_target_pairs={{1,2},{2,3},{5,6},{6,7},{9,10},{10,11},{13,14},{14,15},{17,18},{18... | collective-permute-start | bytes 786440 | tf_op jit(solution)/shard_map/ppermute | solution.py:280
  17.9 4.6 %collective-permute-start.5 = (f32[256,256]{1,0:T(8,128)S(1)}, f32[256,256]{1,0:T(8,128)S(1)}, u32[]{:S(2)}, u32[]{:S(2)}) collective-permute-start(f32[256,256]{1,0:T(8,128)S(1)} %collective-permute-done.1), channel_id=1, source_target_pairs={{1,0},{5,4},{9,8},{13,12},{17,16},{21,20},{25,24},{29,28}} | collective-permute-start | bytes 786440 | tf_op jit(solution)/shard_map/ppermute | solution.py:285
  19.2 5.4 %collective-permute-start.6 = (f32[256,256]{1,0:T(8,128)S(1)}, f32[256,256]{1,0:T(8,128)}, u32[]{:S(2)}, u32[]{:S(2)}) collective-permute-start(f32[256,256]{1,0:T(8,128)S(1)} %collective-permute-done.3), channel_id=1, source_target_pairs={{0,8},{4,12},{8,0},{12,4},{16,24},{20,28},{24,16},{28,20},{1,9},{5... | collective-permute-start | bytes 786440 | tf_op jit(solution)/shard_map/ppermute | solution.py:241
  21.2 3.6 %copy-start = (f32[256,256]{1,0:T(8,128)}, f32[256,256]{1,0:T(8,128)S(1)}, u32[]{:S(2)}) copy-start(f32[256,256]{1,0:T(8,128)S(1)} %collective-permute-done.4) | copy-start | bytes 786436
  24.9 5.3 %collective-permute-start.7 = (f32[3,128,256]{2,1,0:T(8,128)S(1)}, f32[3,128,256]{2,1,0:T(8,128)S(1)}, u32[]{:S(2)}, u32[]{:S(2)}) collective-permute-start(f32[3,128,256]{2,1,0:T(8,128)S(1)} %select_bitcast_fusion), channel_id=1, source_target_pairs={{0,4},{4,0},{8,12},{12,8},{16,20},{20,16},{24,28},{28,24},{1,5},{5... | collective-permute-start | bytes 1179656 | tf_op jit(solution)/shard_map/ppermute | solution.py:241
  29.9 3.1 %collective-permute-start.11 = (f32[512,256]{1,0:T(8,128)S(1)}, f32[512,256]{1,0:T(8,128)S(1)}, u32[]{:S(2)}, u32[]{:S(2)}) collective-permute-start(f32[512,256]{1,0:T(8,128)S(1)} %pad_maximum_fusion.1.refs_0_), channel_id=1, source_target_pairs={{0,4},{4,0},{8,12},{12,8},{16,20},{20,16},{24,28},{28,24},{1,5},{5... | collective-permute-start | bytes 1572872 | tf_op jit(solution)/shard_map/ppermute | solution.py:241
  30.3 5.7 %collective-permute-start.10 = (f32[128,256]{1,0:T(8,128)S(1)}, f32[128,256]{1,0:T(8,128)S(1)}, u32[]{:S(2)}, u32[]{:S(2)}) collective-permute-start(f32[128,256]{1,0:T(8,128)S(1)} %get-tuple-element.44), channel_id=1, source_target_pairs={{0,24},{4,28},{8,16},{12,20},{16,8},{20,12},{24,0},{28,4},{1,25},{... | collective-permute-start | bytes 393224 | tf_op jit(solution)/shard_map/ppermute | solution.py:241
  30.6 7.3 %collective-permute-start.8 = (f32[128,256]{1,0:T(8,128)S(1)}, f32[128,256]{1,0:T(8,128)S(1)}, u32[]{:S(2)}, u32[]{:S(2)}) collective-permute-start(f32[128,256]{1,0:T(8,128)S(1)} %get-tuple-element.44), channel_id=1, source_target_pairs={{0,8},{4,12},{8,0},{12,4},{16,24},{20,28},{24,16},{28,20},{1,9},{5... | collective-permute-start | bytes 393224 | tf_op jit(solution)/shard_map/ppermute | solution.py:241
  31.8 7.7 %collective-permute-start.9 = (f32[128,256]{1,0:T(8,128)S(1)}, f32[128,256]{1,0:T(8,128)S(1)}, u32[]{:S(2)}, u32[]{:S(2)}) collective-permute-start(f32[128,256]{1,0:T(8,128)S(1)} %get-tuple-element.44), channel_id=1, source_target_pairs={{0,16},{4,20},{8,24},{12,28},{16,0},{20,4},{24,8},{28,12},{1,17},{... | collective-permute-start | bytes 393224 | tf_op jit(solution)/shard_map/ppermute | solution.py:241
  39.5 1.0 %copy-start.1 = (f32[256,256]{1,0:T(8,128)S(1)}, f32[256,256]{1,0:T(8,128)}, u32[]{:S(2)}) copy-start(f32[256,256]{1,0:T(8,128)} %copy-done) | copy-start | bytes 786436
  39.6 4.4 %collective-permute-start.13 = (f32[256,256]{1,0:T(8,128)S(1)}, f32[256,256]{1,0:T(8,128)S(1)}, u32[]{:S(2)}, u32[]{:S(2)}) collective-permute-start(f32[256,256]{1,0:T(8,128)S(1)} %pad_maximum_fusion.4.mine_ref.refs_0_), channel_id=1, source_target_pairs={{0,4},{4,0},{8,12},{12,8},{16,20},{20,16},{24,28},{28,24},{1,5},{5... | collective-permute-start | bytes 786440 | tf_op jit(solution)/shard_map/ppermute | solution.py:241
  40.5 10.0 %collective-permute-start.12 = (f32[256,256]{1,0:T(8,128)S(1)}, f32[256,256]{1,0:T(8,128)S(1)}, u32[]{:S(2)}, u32[]{:S(2)}) collective-permute-start(f32[256,256]{1,0:T(8,128)S(1)} %copy-done.1), channel_id=1, source_target_pairs={{2,3},{6,7},{10,11},{14,15},{18,19},{22,23},{26,27},{30,31}} | collective-permute-start | bytes 786440 | tf_op jit(solution)/shard_map/ppermute | solution.py:306
  41.2 9.4 %collective-permute-start.14 = (f32[256,256]{1,0:T(8,128)S(1)}, f32[256,256]{1,0:T(8,128)S(1)}, u32[]{:S(2)}, u32[]{:S(2)}) collective-permute-start(f32[256,256]{1,0:T(8,128)S(1)} %pad_maximum_fusion.5), channel_id=1, source_target_pairs={{0,8},{4,12},{8,0},{12,4},{16,24},{20,28},{24,16},{28,20},{1,9},{5... | collective-permute-start | bytes 786440 | tf_op jit(solution)/shard_map/ppermute | solution.py:241
  41.5 9.1 %collective-permute-start.15 = (f32[256,256]{1,0:T(8,128)S(1)}, f32[256,256]{1,0:T(8,128)S(1)}, u32[]{:S(2)}, u32[]{:S(2)}) collective-permute-start(f32[256,256]{1,0:T(8,128)S(1)} %pad_maximum_fusion.5), channel_id=1, source_target_pairs={{0,16},{4,20},{8,24},{12,28},{16,0},{20,4},{24,8},{28,12},{1,17},{... | collective-permute-start | bytes 786440 | tf_op jit(solution)/shard_map/ppermute | solution.py:241
  41.5 12.0 %collective-permute-start.16 = (f32[256,256]{1,0:T(8,128)S(1)}, f32[256,256]{1,0:T(8,128)S(1)}, u32[]{:S(2)}, u32[]{:S(2)}) collective-permute-start(f32[256,256]{1,0:T(8,128)S(1)} %pad_maximum_fusion.5), channel_id=1, source_target_pairs={{0,24},{4,28},{8,16},{12,20},{16,8},{20,12},{24,0},{28,4},{1,25},{... | collective-permute-start | bytes 786440 | tf_op jit(solution)/shard_map/ppermute | solution.py:241
  53.7 5.0 %collective-permute-start.17 = (f32[512,256]{1,0:T(8,128)S(1)}, f32[512,256]{1,0:T(8,128)S(1)}, u32[]{:S(2)}, u32[]{:S(2)}) collective-permute-start(f32[512,256]{1,0:T(8,128)S(1)} %pad_maximum_fusion.2.refs_2_), channel_id=1, source_target_pairs={{0,4},{4,0},{8,12},{12,8},{16,20},{20,16},{24,28},{28,24},{1,5},{5... | collective-permute-start | bytes 1572872 | tf_op jit(solution)/shard_map/ppermute | solution.py:241
  56.0 17.3 %collective-permute-start.18 = (f32[256,256]{1,0:T(8,128)S(1)}, f32[256,256]{1,0:T(8,128)S(1)}, u32[]{:S(2)}, u32[]{:S(2)}) collective-permute-start(f32[256,256]{1,0:T(8,128)S(1)} %bitcast.37), channel_id=1, source_target_pairs={{0,8},{4,12},{8,0},{12,4},{16,24},{20,28},{24,16},{28,20},{1,9},{5... | collective-permute-start | bytes 786440 | tf_op jit(solution)/shard_map/ppermute | solution.py:241
  57.2 16.1 %collective-permute-start.19 = (f32[256,256]{1,0:T(8,128)S(1)}, f32[256,256]{1,0:T(8,128)S(1)}, u32[]{:S(2)}, u32[]{:S(2)}) collective-permute-start(f32[256,256]{1,0:T(8,128)S(1)} %bitcast.38), channel_id=1, source_target_pairs={{0,16},{4,20},{8,24},{12,28},{16,0},{20,4},{24,8},{28,12},{1,17},{... | collective-permute-start | bytes 786440 | tf_op jit(solution)/shard_map/ppermute | solution.py:241
  57.3 16.1 %collective-permute-start.20 = (f32[256,256]{1,0:T(8,128)S(1)}, f32[256,256]{1,0:T(8,128)S(1)}, u32[]{:S(2)}, u32[]{:S(2)}) collective-permute-start(f32[256,256]{1,0:T(8,128)S(1)} %bitcast.39), channel_id=1, source_target_pairs={{0,24},{4,28},{8,16},{12,20},{16,8},{20,12},{24,0},{28,4},{1,25},{... | collective-permute-start | bytes 786440 | tf_op jit(solution)/shard_map/ppermute | solution.py:241
  73.5 2.5 %collective-permute-start.21 = (f32[512,256]{1,0:T(8,128)S(1)}, f32[512,256]{1,0:T(8,128)S(1)}, u32[]{:S(2)}, u32[]{:S(2)}) collective-permute-start(f32[512,256]{1,0:T(8,128)S(1)} %pad_maximum_fusion.3.refs_2_), channel_id=1, source_target_pairs={{0,4},{4,0},{8,12},{12,8},{16,20},{20,16},{24,28},{28,24},{1,5},{5... | collective-permute-start | bytes 1572872 | tf_op jit(solution)/shard_map/ppermute | solution.py:241

commit v5 on v4

--- a/solution.py
+++ b/solution.py
@@ -86,8 +86,9 @@
     return out
 
 
-def factor_half(aug):
+def factor_half(a):
     half = GROUPS // 2
+    aug = jnp.concatenate([a, identity(HALF)], axis=1)
     upper = eliminate([aug[8 * g:8 * g + 8, :] for g in range(half)], 0)
     high, low = split(jnp.concatenate(upper, axis=0))
     left = jnp.concatenate([high[:, :HALF], high[:, :HALF], low[:, :HALF]], axis=0)
@@ -95,8 +96,7 @@
     update = lax.dot_general(left, right, TN, preferred_element_type=jnp.float32)
     under = eliminate(
         [aug[8 * g:8 * g + 8, :] - update[8 * g:8 * g + 8, :] for g in range(half, GROUPS)], HALF // 2)
-    for g, value in enumerate(upper + under):
-        aug[8 * g:8 * g + 8, :] = value
+    return jnp.concatenate(upper + under, axis=0)[:, HALF:]
 
 
 def identity(n):
@@ -105,30 +105,16 @@
     return jnp.where(r == c, 1.0, 0.0).astype(jnp.float32)
 
 
-def factor_panel(block, aug, inverse):
-    aug[:, :HALF] = block[:HALF, :HALF]
-    aug[:, HALF:] = identity(HALF)
+def factor_panel(block, inverse):
+    w0 = factor_half(block[:HALF, :HALF])
+    sw0 = split(w0)
+    side = split(block[HALF:, :HALF])
+    low = split(mm(side, sw0, NT))
+    w1 = factor_half(block[HALF:, HALF:] - mm(low, split(mm(sw0, side, NT)), NN))
+    inverse[:HALF, :HALF] = w0
     inverse[:HALF, HALF:] = jnp.zeros((HALF, HALF), jnp.float32)
-
-    @pl.loop(0, 2)
-    def _(half):
-        factor_half(aug)
-        sw = split(aug[:, HALF:])
-
-        @pl.when(half == 0)
-        def _():
-            side = split(block[HALF:, :HALF])
-            low = split(mm(side, sw, NT))
-            up = split(mm(sw, side, NT))
-            inverse[:HALF, :HALF] = aug[:, HALF:]
-            inverse[HALF:, :HALF] = mm(low, sw, NN)
-            aug[:, :HALF] = block[HALF:, HALF:] - mm(low, up, NN)
-            aug[:, HALF:] = identity(HALF)
-
-        @pl.when(half == 1)
-        def _():
-            inverse[HALF:, :HALF] = -mm(sw, split(inverse[HALF:, :HALF]), NN)
-            inverse[HALF:, HALF:] = aug[:, HALF:]
+    inverse[HALF:, :HALF] = -mm(split(w1), split(mm(low, sw0, NN)), NN)
+    inverse[HALF:, HALF:] = w1
 
 
 def halves(mine, other, core):
@@ -145,13 +131,13 @@
     ]
 
 
-def first_kernel(place, mine_ref, other_ref, inverse_ref, block, aug):
+def first_kernel(place, mine_ref, other_ref, inverse_ref, block):
     block[...] = halves(mine_ref.at[:HALF], other_ref.at[:HALF], lax.rem(place[0], 2))
-    factor_panel(block, aug, inverse_ref)
+    factor_panel(block, inverse_ref)
 
 
 def rest_kernel(place, w0_ref, *refs):
-    pieces, inverses, upper, block, aug = (refs[:2], refs[2:4]), refs[4], refs[5], refs[6], refs[7]
+    pieces, inverses, upper, block, later = (refs[:2], refs[2:4]), refs[4], refs[5], refs[6], refs[7]
     core = lax.rem(place[0], 2)
 
     def piece(group, k):
@@ -160,24 +146,24 @@
 
     w0 = split(w0_ref[...])
     u01 = mm(w0, split(piece(1, 0)), NN)
+    u02 = mm(w0, split(piece(0, 1)), NT)
     upper[0] = u01
-    su01 = split(u01)
+    upper[1] = u02
+    su01, su02 = split(u01), split(u02)
     block[...] = piece(1, 1) - mm(su01, su01, TN)
+    later[0] = piece(1, 2).T - mm(su01, su02, TN)
+    later[1] = piece(1, 3) - mm(su02, su02, TN)
 
     @pl.loop(0, 2)
     def _(k):
-        factor_panel(block, aug, inverses.at[k])
+        factor_panel(block, inverses.at[k])
 
         @pl.when(k == 0)
         def _():
-            u02 = mm(w0, split(piece(0, 1)), NT)
-            upper[1] = u02
-            su02 = split(u02)
-            s12 = split(piece(1, 2).T - mm(split(upper[0]), su02, TN))
-            u12 = mm(split(inverses[0]), s12, NN)
+            u12 = mm(split(inverses[0]), split(later[0]), NN)
             upper[2] = u12
             su12 = split(u12)
-            block[...] = piece(1, 3) - mm(su02, su02, TN) - mm(su12, su12, TN)
+            block[...] = later[1] - mm(su12, su12, TN)
 
 
 def apply_kernel(place, own_ref, right_ref, b0_ref, b1_ref, b2_ref, w0_ref, inverses, upper, *refs):
@@ -185,55 +171,56 @@
     p, c = place[0], place[1]
     core = lax.rem(p, 2)
     nb = 2 * HALF
-    w0, w1, w2 = [split(w) for w in (w0_ref[...], inverses[0], inverses[1])]
-    u01, u02, u12 = [split(upper[k]) for k in range(PANELS)]
-
-    x0 = mm(split(b0_ref[...]), w0, NT)
-    sx0 = split(x0)
-    x1 = mm(split(b1_ref[...] - mm(sx0, u01, NN)), w1, NT)
-    sx1 = split(x1)
-    x2 = mm(split(b2_ref[...] - mm(sx0, u02, NN) - mm(sx1, u12, NN)), w2, NT)
-    sx2 = split(x2)
-    row = tuple(jnp.concatenate(parts, axis=1) for parts in zip(sx0, sx1, sx2))
-
-    @pl.when(c < PANELS)
-    def _():
+
+    def blocks(members):
+        w0, w1, w2 = [split(w) for w in (w0_ref[...], inverses[0], inverses[1])]
+        u01, u02, u12 = [split(upper[k]) for k in range(PANELS)]
+        x0 = mm(split(b0_ref[...]), w0, NT)
+        if members:
+            tops = [three([ref.at[k:k + nb] for ref in top_refs[member] for k in (0, nb)], core) for member in members]
+            t0, t1, t2 = [jnp.concatenate(t, axis=1) for t in zip(*tops)]
+            y0 = split(mm(w0, split(t0), NN))
+        sx0 = split(x0)
+        x1 = mm(split(b1_ref[...] - mm(sx0, u01, NN)), w1, NT)
+        if members:
+            y1 = split(mm(w1, split(t1 - mm(u01, y0, TN)), NN))
+        sx1 = split(x1)
+        x2 = mm(split(b2_ref[...] - mm(sx0, u02, NN) - mm(sx1, u12, NN)), w2, NT)
+        if members:
+            y2 = split(mm(w2, split(t2 - mm(u02, y0, TN) - mm(u12, y1, TN)), NN))
+            row = tuple(jnp.concatenate(parts, axis=1) for parts in zip(sx0, sx1, split(x2)))
+            column = tuple(jnp.concatenate(parts, axis=0) for parts in zip(y0, y1, y2))
+            loss = mm(row, column, NN)
+            for i, member in enumerate(members):
+                out_ref[0, :, member, :] = (own_ref, right_ref)[member][...] - loss[:, i * nb:(i + 1) * nb]
+        return x0, x1, x2
+
+    def panel(x0, x1, x2):
         r = lax.broadcasted_iota(jnp.int32, (nb, nb), 0)
         q = lax.broadcasted_iota(jnp.int32, (nb, nb), 1)
         keep = jnp.where(p > c, 1, 0)
         diagonal = jnp.where(p == c, 1, 0)
         mask = (keep + diagonal * jnp.where(r >= q, 1, 0)) > 0
-        panel = jnp.where(c == 0, x0, jnp.where(c == 1, x1, x2))
-        out_ref[0, :, 0, :] = jnp.where(mask, panel, 0.0)
-
-    def remaining(members):
-        tops = []
-        for member in members:
-            tops.append(three([ref.at[k:k + nb] for ref in top_refs[member] for k in (0, nb)], core))
-        t0, t1, t2 = [jnp.concatenate(t, axis=1) for t in zip(*tops)]
-        y0 = split(mm(w0, split(t0), NN))
-        y1 = split(mm(w1, split(t1 - mm(u01, y0, TN)), NN))
-        y2 = split(mm(w2, split(t2 - mm(u02, y0, TN) - mm(u12, y1, TN)), NN))
-        column = tuple(jnp.concatenate(parts, axis=0) for parts in zip(y0, y1, y2))
-        loss = mm(row, column, NN)
-        for i, member in enumerate(members):
-            out_ref[0, :, member, :] = (own_ref, right_ref)[member][...] - loss[:, i * nb:(i + 1) * nb]
+        value = jnp.where(c == 0, x0, jnp.where(c == 1, x1, x2))
+        out_ref[0, :, 0, :] = jnp.where(mask, value, 0.0)
 
     @pl.when((p >= PANELS) & (c >= PANELS))
     def _():
-        remaining((0, 1))
+        blocks((0, 1))
 
     @pl.when((p >= PANELS) & (c < PANELS))
     def _():
-        remaining((1,))
-
-    @pl.when(p < PANELS)
+        panel(*blocks((1,)))
+
+    @pl.when((p < PANELS) & (c < PANELS))
     def _():
+        panel(*blocks(()))
         out_ref[0, :, 1, :] = jnp.zeros((nb, nb), jnp.float32)
 
     @pl.when((p < PANELS) & (c >= PANELS))
     def _():
         out_ref[0, :, 0, :] = jnp.zeros((nb, nb), jnp.float32)
+        out_ref[0, :, 1, :] = jnp.zeros((nb, nb), jnp.float32)
 
 
 def swap(value, axis, bit):
@@ -329,7 +316,7 @@
     smem = pl.BlockSpec(memory_space=pltpu.SMEM)
     vmem = pl.BlockSpec(memory_space=pltpu.VMEM)
     square = jax.ShapeDtypeStruct((nb, nb), f32)
-    chain = [pltpu.VMEM((nb, nb), f32), pltpu.VMEM((HALF, nb), f32)]
+    chain = [pltpu.VMEM((nb, nb), f32)]
 
     def call(body, name, outs, scratch, micros, *operands):
         return pl.pallas_call(
@@ -356,9 +343,9 @@
     ahead, blocks, top, start_last, finish = along_col(own, right, c)
     even, odd = cut(jnp.stack([ahead, blocks[1], blocks[2]]))
     one = launch(even[0])
+    two = launch(jnp.concatenate([even[1], jnp.where(chip == 0, odd[1], even[2])]))
     top = cross(*land(top, p))
-    one = land(one, p, *top)
-    two = launch(jnp.concatenate([even[1], jnp.where(chip == 0, odd[1], even[2])]))
+    one = land(one, p, *top, *two[1:3])
     last = start_last(*one)
     one = cross(*one)
     w0 = call(first_kernel, "first", square, chain, 6.5, *one)
@@ -367,7 +354,8 @@
     top_own = launch(after(own, w0))
     inverses, upper = call(
         rest_kernel, "rest",
-        (jax.ShapeDtypeStruct((2, nb, nb), f32), jax.ShapeDtypeStruct((PANELS, nb, nb), f32)), chain, 15.0,
+        (jax.ShapeDtypeStruct((2, nb, nb), f32), jax.ShapeDtypeStruct((PANELS, nb, nb), f32)),
+        [*chain, pltpu.VMEM((2, nb, nb), f32)], 15.0,
         w0, *one, *two)
     top_own = cross(*land(top_own, p, inverses))
     return call(

time: 81.6 us -> 79.9 us (0.979)
  Pallas kernels: 26.5 us -> 25 us
    pallas_call x3, Pallas kernels: 26.5 us -> 25 us  [call(): pl.pallas_call(body, out_shape=outs, in_specs=[smem] + [vmem] * len(opera...]
  transfers between devices with their start and end apart: 22 -> 22, of which waited for: 12 -> 11; matrix products, arithmetic and copies ran while one was open for 2% -> 2% of each run, Pallas kernels for 26% -> 26%
where the time goes in v5:
time: 79.9 us; the launch traced here: 79.6 us
  starting transfers between devices  27.9 us (35%)
  Pallas kernels  25 us (31%)
  waiting for transfers between devices  23 us (29%)
  other arithmetic  1.81 us (2%)
  local copies, waits for them, and re-layouts  1.7 us (2%)
    pallas_call x3, Pallas kernels, call(): pl.pallas_call(body, out_shape=outs, in_specs=[smem] + [vmem] * len(opera...  25 us
    ppermute x17, starting transfers between devices, swap(): return lax.ppermute(value, axis, [(i, i ^ bit) for i in range(n)])  17.2 us
    ppermute x17, waiting for transfers between devices, swap(): return lax.ppermute(value, axis, [(i, i ^ bit) for i in range(n)])  14.9 us
    ppermute x2, starting transfers between devices, along_col(): came = [lax.ppermute(value, 'col', steps_right(s, n_col))]  6.41 us
    ppermute x2, waiting for transfers between devices, along_col(): came.append(lax.ppermute(back, ('row', 'col'), pairs))  4.21 us
    ppermute x2, waiting for transfers between devices, along_col(): came = [lax.ppermute(value, 'col', steps_right(s, n_col))]  3.85 us
    ppermute x2, starting transfers between devices, along_col(): came.append(lax.ppermute(back, ('row', 'col'), pairs))  3.4 us
    slice x1, local copies, waits for them, and re-layouts, shards(): right = kernel[0, :, 1, :]  1.65 us
  transfers between devices with their start and end apart: 22, of which 11 were waited for; matrix products, arithmetic and copies ran while one was open for 2% of the time, Pallas kernels for 26%

profile of v5, /device:TPU:13, one launch (start us, length us, event | category | flops | bytes accessed | tf_op | source)
XLA Modules:
  0.0 79.6 jit_solution(7229264410426902247)
XLA Ops:
  0.0 1.6 %fusion.1 = (f32[1,256,1,256]{3,2,1,0:T(1,128)S(1)}, f32[1,256,1,256]{3,2,1,0:T(1,128)S(1)}) fusion(f32[1,256,2,256]{3,2,1,0:T(2,128)} %param.1), kind=kLoop, calls=%fused_computation.30 | loop fusion | bytes 1048576 | tf_op jit(solution)/shard_map/slice | solution.py:314
  1.7 3.2 %collective-permute-start = (f32[256,256]{1,0:T(8,128)S(1)}, f32[256,256]{1,0:T(8,128)S(1)}, u32[]{:S(2)}, u32[]{:S(2)}) collective-permute-start(f32[256,256]{1,0:T(8,128)S(1)} %bitcast.35), channel_id=1, source_target_pairs={{0,1},{1,2},{2,3},{4,5},{5,6},{6,7},{8,9},{9,10},{10,11},{12,13},{... | collective-permute-start | bytes 786440 | tf_op jit(solution)/shard_map/ppermute | solution.py:267
  4.9 2.1 %collective-permute-start.1 = (f32[256,256]{1,0:T(8,128)S(1)}, f32[256,256]{1,0:T(8,128)S(1)}, u32[]{:S(2)}, u32[]{:S(2)}) collective-permute-start(f32[256,256]{1,0:T(8,128)S(1)} %bitcast.36), channel_id=1, source_target_pairs={{1,0},{2,1},{5,4},{6,5},{9,8},{10,9},{13,12},{14,13},{17,16},{18,1... | collective-permute-start | bytes 786440 | tf_op jit(solution)/shard_map/ppermute | solution.py:272
  7.0 1.3 %collective-permute-start.2 = (f32[256,256]{1,0:T(8,128)S(1)}, f32[256,256]{1,0:T(8,128)S(1)}, u32[]{:S(2)}, u32[]{:S(2)}) collective-permute-start(f32[256,256]{1,0:T(8,128)S(1)} %bitcast.42), channel_id=1, source_target_pairs={{0,8},{4,12},{8,0},{12,4},{16,24},{20,28},{24,16},{28,20},{1,9},{5... | collective-permute-start | bytes 786440 | tf_op jit(solution)/shard_map/ppermute | solution.py:228
  8.5 2.2 %collective-permute-done = f32[256,256]{1,0:T(8,128)S(1)} collective-permute-done((f32[256,256]{1,0:T(8,128)S(1)}, f32[256,256]{1,0:T(8,128)S(1)}, u32[]{:S(2)}, u32[]{:S(2)}) %collective-permute-start) | collective-permute-done | bytes 262176 | tf_op jit(solution)/shard_map/ppermute | solution.py:267
  10.7 2.9 %collective-permute-done.1 = f32[256,256]{1,0:T(8,128)S(1)} collective-permute-done((f32[256,256]{1,0:T(8,128)S(1)}, f32[256,256]{1,0:T(8,128)S(1)}, u32[]{:S(2)}, u32[]{:S(2)}) %collective-permute-start.1) | collective-permute-done | bytes 262176 | tf_op jit(solution)/shard_map/ppermute | solution.py:272
  13.6 0.9 %collective-permute-done.3 = f32[256,256]{1,0:T(8,128)S(1)} collective-permute-done((f32[256,256]{1,0:T(8,128)S(1)}, f32[256,256]{1,0:T(8,128)S(1)}, u32[]{:S(2)}, u32[]{:S(2)}) %collective-permute-start.3) | collective-permute-done | bytes 262176 | tf_op jit(solution)/shard_map/ppermute | solution.py:228
  14.6 3.2 %collective-permute-start.4 = (f32[256,256]{1,0:T(8,128)S(1)}, f32[256,256]{1,0:T(8,128)S(1)}, u32[]{:S(2)}, u32[]{:S(2)}) collective-permute-start(f32[256,256]{1,0:T(8,128)S(1)} %collective-permute-done), channel_id=1, source_target_pairs={{1,2},{2,3},{5,6},{6,7},{9,10},{10,11},{13,14},{14,15},{17,18},{18... | collective-permute-start | bytes 786440 | tf_op jit(solution)/shard_map/ppermute | solution.py:267
  17.8 1.3 %collective-permute-start.5 = (f32[256,256]{1,0:T(8,128)S(1)}, f32[256,256]{1,0:T(8,128)S(1)}, u32[]{:S(2)}, u32[]{:S(2)}) collective-permute-start(f32[256,256]{1,0:T(8,128)S(1)} %collective-permute-done.1), channel_id=1, source_target_pairs={{1,0},{5,4},{9,8},{13,12},{17,16},{21,20},{25,24},{29,28}} | collective-permute-start | bytes 786440 | tf_op jit(solution)/shard_map/ppermute | solution.py:272
  19.1 0.3 collective-permute-start.6
  19.5 1.6 %collective-permute-done.4 = f32[256,256]{1,0:T(8,128)S(1)} collective-permute-done((f32[256,256]{1,0:T(8,128)S(1)}, f32[256,256]{1,0:T(8,128)S(1)}, u32[]{:S(2)}, u32[]{:S(2)}) %collective-permute-start.4) | collective-permute-done | bytes 262176 | tf_op jit(solution)/shard_map/ppermute | solution.py:267
  21.1 1.3 %collective-permute-done.5 = f32[256,256]{1,0:T(8,128)S(1)} collective-permute-done((f32[256,256]{1,0:T(8,128)S(1)}, f32[256,256]{1,0:T(8,128)S(1)}, u32[]{:S(2)}, u32[]{:S(2)}) %collective-permute-start.5) | collective-permute-done | bytes 262176 | tf_op jit(solution)/shard_map/ppermute | solution.py:272
  22.4 2.1 %collective-permute-done.6 = f32[256,256]{1,0:T(8,128)} collective-permute-done((f32[256,256]{1,0:T(8,128)S(1)}, f32[256,256]{1,0:T(8,128)}, u32[]{:S(2)}, u32[]{:S(2)}) %collective-permute-start.6) | collective-permute-done | bytes 262176 | tf_op jit(solution)/shard_map/ppermute | solution.py:228
  24.8 3.9 %collective-permute-start.7 = (f32[3,128,256]{2,1,0:T(8,128)S(1)}, f32[3,128,256]{2,1,0:T(8,128)S(1)}, u32[]{:S(2)}, u32[]{:S(2)}) collective-permute-start(f32[3,128,256]{2,1,0:T(8,128)S(1)} %select_bitcast_fusion), channel_id=1, source_target_pairs={{0,4},{4,0},{8,12},{12,8},{16,20},{20,16},{24,28},{28,24},{1,5},{5... | collective-permute-start | bytes 1179656 | tf_op jit(solution)/shard_map/ppermute | solution.py:228
  28.7 1.0 %select_select_fusion.5 = (f32[256,256]{1,0:T(8,128)S(1)}, f32[256,256]{1,0:T(8,128)S(1)}) fusion(f32[256,256]{1,0:T(8,128)S(1)} %bitcast.44, f32[256,256]{1,0:T(8,128)S(1)} %collective-permute-done.2, f32[256,256]{1,0:T(8,128)S(1)} %collective-permute-done.3, f32[256,256]{1,0:T(8,128)} %collective-permute-done.6, pred[]{:T(512)S(6)} %eq.38, pred[]{:T(512)S(6)} %eq.37, ...), kind=kLoop, calls=%fused_computation.15 | loop fusion | flops 393216 | bytes 1572870 | tf_op jit(solution)/shard_map/jit(_where)/select_n | solution.py:246
  30.2 0.3 collective-permute-start.12
  30.7 2.2 %collective-permute-start.10 = (f32[128,256]{1,0:T(8,128)S(1)}, f32[128,256]{1,0:T(8,128)S(1)}, u32[]{:S(2)}, u32[]{:S(2)}) collective-permute-start(f32[128,256]{1,0:T(8,128)S(1)} %get-tuple-element.44), channel_id=1, source_target_pairs={{0,24},{4,28},{8,16},{12,20},{16,8},{20,12},{24,0},{28,4},{1,25},{... | collective-permute-start | bytes 393224 | tf_op jit(solution)/shard_map/ppermute | solution.py:228
  32.9 0.3 collective-permute-start.8
  33.2 0.2 collective-permute-start.9
  33.4 7.2 %collective-permute-done.10 = f32[128,256]{1,0:T(8,128)S(1)} collective-permute-done((f32[128,256]{1,0:T(8,128)S(1)}, f32[128,256]{1,0:T(8,128)S(1)}, u32[]{:S(2)}, u32[]{:S(2)}) %collective-permute-start.10) | collective-permute-done | bytes 131104 | tf_op jit(solution)/shard_map/ppermute | solution.py:228
  40.6 2.9 %collective-permute-done.8 = f32[128,256]{1,0:T(8,128)S(1)} collective-permute-done((f32[128,256]{1,0:T(8,128)S(1)}, f32[128,256]{1,0:T(8,128)S(1)}, u32[]{:S(2)}, u32[]{:S(2)}) %collective-permute-start.8) | collective-permute-done | bytes 131104 | tf_op jit(solution)/shard_map/ppermute | solution.py:228
  43.5 1.5 %collective-permute-start.15 = (f32[256,256]{1,0:T(8,128)S(1)}, f32[256,256]{1,0:T(8,128)S(1)}, u32[]{:S(2)}, u32[]{:S(2)}) collective-permute-start(f32[256,256]{1,0:T(8,128)S(1)} %pad_maximum_fusion.5.mine_ref.refs_0_), channel_id=1, source_target_pairs={{0,4},{4,0},{8,12},{12,8},{16,20},{20,16},{24,28},{28,24},{1,5},{5... | collective-permute-start | bytes 786440 | tf_op jit(solution)/shard_map/ppermute | solution.py:228
  45.0 0.8 %collective-permute-start.14 = (f32[256,256]{1,0:T(8,128)S(1)}, f32[256,256]{1,0:T(8,128)S(1)}, u32[]{:S(2)}, u32[]{:S(2)}) collective-permute-start(f32[256,256]{1,0:T(8,128)S(1)} %copy-done.1), channel_id=1, source_target_pairs={{2,3},{6,7},{10,11},{14,15},{18,19},{22,23},{26,27},{30,31}} | collective-permute-start | bytes 786440 | tf_op jit(solution)/shard_map/ppermute | solution.py:293
  45.9 1.2 %collective-permute-start.16 = (f32[256,256]{1,0:T(8,128)S(1)}, f32[256,256]{1,0:T(8,128)S(1)}, u32[]{:S(2)}, u32[]{:S(2)}) collective-permute-start(f32[256,256]{1,0:T(8,128)S(1)} %pad_maximum_fusion.4), channel_id=1, source_target_pairs={{0,24},{4,28},{8,16},{12,20},{16,8},{20,12},{24,0},{28,4},{1,25},{... | collective-permute-start | bytes 786440 | tf_op jit(solution)/shard_map/ppermute | solution.py:228
  47.2 6.5 %first.1.w0_ref = f32[256,256]{1,0:T(8,128)S(1)} custom-call(s32[2]{0:T(128)S(1)} %pad_add_fusion.place, f32[256,256]{1,0:T(8,128)S(1)} %pad_maximum_fusion.5.mine_ref.refs_0_, f32[256,256]{1,0:T(8,128)S(1)} %collective-permute-done.15.other_ref.refs_1_), custom_call_target="tpu_custom_call" | custom-call | bytes 22750000 | tf_op jit(solution)/shard_map/first/pallas_call | solution.py:322
  53.9 1.8 %collective-permute-start.17 = (f32[512,256]{1,0:T(8,128)S(1)}, f32[512,256]{1,0:T(8,128)S(1)}, u32[]{:S(2)}, u32[]{:S(2)}) collective-permute-start(f32[512,256]{1,0:T(8,128)S(1)} %pad_maximum_fusion.2.refs_2_), channel_id=1, source_target_pairs={{0,4},{4,0},{8,12},{12,8},{16,20},{20,16},{24,28},{28,24},{1,5},{5... | collective-permute-start | bytes 1572872 | tf_op jit(solution)/shard_map/ppermute | solution.py:228
  55.7 1.2 %collective-permute-start.18 = (f32[256,256]{1,0:T(8,128)S(1)}, f32[256,256]{1,0:T(8,128)S(1)}, u32[]{:S(2)}, u32[]{:S(2)}) collective-permute-start(f32[256,256]{1,0:T(8,128)S(1)} %bitcast.37), channel_id=1, source_target_pairs={{0,8},{4,12},{8,0},{12,4},{16,24},{20,28},{24,16},{28,20},{1,9},{5... | collective-permute-start | bytes 786440 | tf_op jit(solution)/shard_map/ppermute | solution.py:228
  57.2 1.2 %collective-permute-start.20 = (f32[256,256]{1,0:T(8,128)S(1)}, f32[256,256]{1,0:T(8,128)S(1)}, u32[]{:S(2)}, u32[]{:S(2)}) collective-permute-start(f32[256,256]{1,0:T(8,128)S(1)} %bitcast.39), channel_id=1, source_target_pairs={{0,24},{4,28},{8,16},{12,20},{16,8},{20,12},{24,0},{28,4},{1,25},{... | collective-permute-start | bytes 786440 | tf_op jit(solution)/shard_map/ppermute | solution.py:228
  58.4 14.0 %rest.1 = (f32[2,256,256]{2,1,0:T(8,128)S(1)}, f32[3,256,256]{2,1,0:T(8,128)S(1)}) custom-call(s32[2]{0:T(128)S(1)} %pad_add_fusion.place, f32[256,256]{1,0:T(8,128)S(1)} %first.1.w0_ref, f32[256,256]{1,0:T(8,128)S(1)} %pad_maximum_fusion.5.mine_ref.refs_0_, f32[256,256]{1,0:T(8,128)S(1)} %collective-permute-done.15.other_ref.refs_1_, ...), custom_call_target="tpu_custom_call" | custom-call | bytes 52500000 | tf_op jit(solution)/shard_map/rest/pallas_call | solution.py:322
  72.6 1.0 %collective-permute-start.21 = (f32[512,256]{1,0:T(8,128)S(1)}, f32[512,256]{1,0:T(8,128)S(1)}, u32[]{:S(2)}, u32[]{:S(2)}) collective-permute-start(f32[512,256]{1,0:T(8,128)S(1)} %pad_maximum_fusion.3.refs_2_), channel_id=1, source_target_pairs={{0,4},{4,0},{8,12},{12,8},{16,20},{20,16},{24,28},{28,24},{1,5},{5... | collective-permute-start | bytes 1572872 | tf_op jit(solution)/shard_map/ppermute | solution.py:228
  73.6 1.5 %collective-permute-done.21.refs_3_ = f32[512,256]{1,0:T(8,128)S(1)} collective-permute-done((f32[512,256]{1,0:T(8,128)S(1)}, f32[512,256]{1,0:T(8,128)S(1)}, u32[]{:S(2)}, u32[]{:S(2)}) %collective-permute-start.21) | collective-permute-done | bytes 524320 | tf_op jit(solution)/shard_map/ppermute | solution.py:228
  75.1 4.5 %apply.1 = f32[1,256,2,256]{3,2,1,0:T(2,128)} custom-call(s32[2]{0:T(128)S(1)} %pad_add_fusion.place, f32[256,256]{1,0:T(8,128)S(1)} %bitcast.41, f32[256,256]{1,0:T(8,128)S(1)} %bitcast.45, f32[256,256]{1,0:T(8,128)S(1)} %broadcast_select_fusion.1.b0_ref, f32[256,256]{1,0:T(8,128)S(1)} %get-tuple-element.65.b1_ref, ...), custom_call_target="tpu_custom_call" | custom-call | bytes 21000000 | tf_op jit(solution)/shard_map/apply/pallas_call | solution.py:322
  (38 shorter events, 1.9 us)
Async XLA Ops:
  1.7 9.1 %collective-permute-start = (f32[256,256]{1,0:T(8,128)S(1)}, f32[256,256]{1,0:T(8,128)S(1)}, u32[]{:S(2)}, u32[]{:S(2)}) collective-permute-start(f32[256,256]{1,0:T(8,128)S(1)} %bitcast.35), channel_id=1, source_target_pairs={{0,1},{1,2},{2,3},{4,5},{5,6},{6,7},{8,9},{9,10},{10,11},{12,13},{... | collective-permute-start | bytes 786440 | tf_op jit(solution)/shard_map/ppermute | solution.py:267
  4.9 8.8 %collective-permute-start.1 = (f32[256,256]{1,0:T(8,128)S(1)}, f32[256,256]{1,0:T(8,128)S(1)}, u32[]{:S(2)}, u32[]{:S(2)}) collective-permute-start(f32[256,256]{1,0:T(8,128)S(1)} %bitcast.36), channel_id=1, source_target_pairs={{1,0},{2,1},{5,4},{6,5},{9,8},{10,9},{13,12},{14,13},{17,16},{18,1... | collective-permute-start | bytes 786440 | tf_op jit(solution)/shard_map/ppermute | solution.py:272
  7.0 6.6 %collective-permute-start.2 = (f32[256,256]{1,0:T(8,128)S(1)}, f32[256,256]{1,0:T(8,128)S(1)}, u32[]{:S(2)}, u32[]{:S(2)}) collective-permute-start(f32[256,256]{1,0:T(8,128)S(1)} %bitcast.42), channel_id=1, source_target_pairs={{0,8},{4,12},{8,0},{12,4},{16,24},{20,28},{24,16},{28,20},{1,9},{5... | collective-permute-start | bytes 786440 | tf_op jit(solution)/shard_map/ppermute | solution.py:228
  8.3 6.3 %collective-permute-start.3 = (f32[256,256]{1,0:T(8,128)S(1)}, f32[256,256]{1,0:T(8,128)S(1)}, u32[]{:S(2)}, u32[]{:S(2)}) collective-permute-start(f32[256,256]{1,0:T(8,128)S(1)} %bitcast.43), channel_id=1, source_target_pairs={{0,16},{4,20},{8,24},{12,28},{16,0},{20,4},{24,8},{28,12},{1,17},{... | collective-permute-start | bytes 786440 | tf_op jit(solution)/shard_map/ppermute | solution.py:228
  14.6 6.5 %collective-permute-start.4 = (f32[256,256]{1,0:T(8,128)S(1)}, f32[256,256]{1,0:T(8,128)S(1)}, u32[]{:S(2)}, u32[]{:S(2)}) collective-permute-start(f32[256,256]{1,0:T(8,128)S(1)} %collective-permute-done), channel_id=1, source_target_pairs={{1,2},{2,3},{5,6},{6,7},{9,10},{10,11},{13,14},{14,15},{17,18},{18... | collective-permute-start | bytes 786440 | tf_op jit(solution)/shard_map/ppermute | solution.py:267
  17.8 4.6 %collective-permute-start.5 = (f32[256,256]{1,0:T(8,128)S(1)}, f32[256,256]{1,0:T(8,128)S(1)}, u32[]{:S(2)}, u32[]{:S(2)}) collective-permute-start(f32[256,256]{1,0:T(8,128)S(1)} %collective-permute-done.1), channel_id=1, source_target_pairs={{1,0},{5,4},{9,8},{13,12},{17,16},{21,20},{25,24},{29,28}} | collective-permute-start | bytes 786440 | tf_op jit(solution)/shard_map/ppermute | solution.py:272
  19.1 5.4 %collective-permute-start.6 = (f32[256,256]{1,0:T(8,128)S(1)}, f32[256,256]{1,0:T(8,128)}, u32[]{:S(2)}, u32[]{:S(2)}) collective-permute-start(f32[256,256]{1,0:T(8,128)S(1)} %collective-permute-done.3), channel_id=1, source_target_pairs={{0,8},{4,12},{8,0},{12,4},{16,24},{20,28},{24,16},{28,20},{1,9},{5... | collective-permute-start | bytes 786440 | tf_op jit(solution)/shard_map/ppermute | solution.py:228
  21.1 3.6 %copy-start = (f32[256,256]{1,0:T(8,128)}, f32[256,256]{1,0:T(8,128)S(1)}, u32[]{:S(2)}) copy-start(f32[256,256]{1,0:T(8,128)S(1)} %collective-permute-done.4) | copy-start | bytes 786436
  24.8 5.3 %collective-permute-start.7 = (f32[3,128,256]{2,1,0:T(8,128)S(1)}, f32[3,128,256]{2,1,0:T(8,128)S(1)}, u32[]{:S(2)}, u32[]{:S(2)}) collective-permute-start(f32[3,128,256]{2,1,0:T(8,128)S(1)} %select_bitcast_fusion), channel_id=1, source_target_pairs={{0,4},{4,0},{8,12},{12,8},{16,20},{20,16},{24,28},{28,24},{1,5},{5... | collective-permute-start | bytes 1179656 | tf_op jit(solution)/shard_map/ppermute | solution.py:228
  29.8 3.4 %collective-permute-start.11 = (f32[512,256]{1,0:T(8,128)S(1)}, f32[512,256]{1,0:T(8,128)S(1)}, u32[]{:S(2)}, u32[]{:S(2)}) collective-permute-start(f32[512,256]{1,0:T(8,128)S(1)} %pad_maximum_fusion.1.refs_0_), channel_id=1, source_target_pairs={{0,4},{4,0},{8,12},{12,8},{16,20},{20,16},{24,28},{28,24},{1,5},{5... | collective-permute-start | bytes 1572872 | tf_op jit(solution)/shard_map/ppermute | solution.py:228
  30.2 13.3 %collective-permute-start.12 = (f32[256,256]{1,0:T(8,128)S(1)}, f32[256,256]{1,0:T(8,128)S(1)}, u32[]{:S(2)}, u32[]{:S(2)}) collective-permute-start(f32[256,256]{1,0:T(8,128)S(1)} %pad_maximum_fusion.4), channel_id=1, source_target_pairs={{0,8},{4,12},{8,0},{12,4},{16,24},{20,28},{24,16},{28,20},{1,9},{5... | collective-permute-start | bytes 786440 | tf_op jit(solution)/shard_map/ppermute | solution.py:228
  30.5 12.9 %collective-permute-start.13 = (f32[256,256]{1,0:T(8,128)S(1)}, f32[256,256]{1,0:T(8,128)S(1)}, u32[]{:S(2)}, u32[]{:S(2)}) collective-permute-start(f32[256,256]{1,0:T(8,128)S(1)} %pad_maximum_fusion.4), channel_id=1, source_target_pairs={{0,16},{4,20},{8,24},{12,28},{16,0},{20,4},{24,8},{28,12},{1,17},{... | collective-permute-start | bytes 786440 | tf_op jit(solution)/shard_map/ppermute | solution.py:228
  30.7 9.8 %collective-permute-start.10 = (f32[128,256]{1,0:T(8,128)S(1)}, f32[128,256]{1,0:T(8,128)S(1)}, u32[]{:S(2)}, u32[]{:S(2)}) collective-permute-start(f32[128,256]{1,0:T(8,128)S(1)} %get-tuple-element.44), channel_id=1, source_target_pairs={{0,24},{4,28},{8,16},{12,20},{16,8},{20,12},{24,0},{28,4},{1,25},{... | collective-permute-start | bytes 393224 | tf_op jit(solution)/shard_map/ppermute | solution.py:228
  32.9 10.5 %collective-permute-start.8 = (f32[128,256]{1,0:T(8,128)S(1)}, f32[128,256]{1,0:T(8,128)S(1)}, u32[]{:S(2)}, u32[]{:S(2)}) collective-permute-start(f32[128,256]{1,0:T(8,128)S(1)} %get-tuple-element.44), channel_id=1, source_target_pairs={{0,8},{4,12},{8,0},{12,4},{16,24},{20,28},{24,16},{28,20},{1,9},{5... | collective-permute-start | bytes 393224 | tf_op jit(solution)/shard_map/ppermute | solution.py:228
  33.2 10.3 %collective-permute-start.9 = (f32[128,256]{1,0:T(8,128)S(1)}, f32[128,256]{1,0:T(8,128)S(1)}, u32[]{:S(2)}, u32[]{:S(2)}) collective-permute-start(f32[128,256]{1,0:T(8,128)S(1)} %get-tuple-element.44), channel_id=1, source_target_pairs={{0,16},{4,20},{8,24},{12,28},{16,0},{20,4},{24,8},{28,12},{1,17},{... | collective-permute-start | bytes 393224 | tf_op jit(solution)/shard_map/ppermute | solution.py:228
  43.5 1.5 %copy-start.1 = (f32[256,256]{1,0:T(8,128)S(1)}, f32[256,256]{1,0:T(8,128)}, u32[]{:S(2)}) copy-start(f32[256,256]{1,0:T(8,128)} %copy-done) | copy-start | bytes 786436
  43.5 3.6 %collective-permute-start.15 = (f32[256,256]{1,0:T(8,128)S(1)}, f32[256,256]{1,0:T(8,128)S(1)}, u32[]{:S(2)}, u32[]{:S(2)}) collective-permute-start(f32[256,256]{1,0:T(8,128)S(1)} %pad_maximum_fusion.5.mine_ref.refs_0_), channel_id=1, source_target_pairs={{0,4},{4,0},{8,12},{12,8},{16,20},{20,16},{24,28},{28,24},{1,5},{5... | collective-permute-start | bytes 786440 | tf_op jit(solution)/shard_map/ppermute | solution.py:228
  45.0 8.7 %collective-permute-start.14 = (f32[256,256]{1,0:T(8,128)S(1)}, f32[256,256]{1,0:T(8,128)S(1)}, u32[]{:S(2)}, u32[]{:S(2)}) collective-permute-start(f32[256,256]{1,0:T(8,128)S(1)} %copy-done.1), channel_id=1, source_target_pairs={{2,3},{6,7},{10,11},{14,15},{18,19},{22,23},{26,27},{30,31}} | collective-permute-start | bytes 786440 | tf_op jit(solution)/shard_map/ppermute | solution.py:293
  45.9 7.9 %collective-permute-start.16 = (f32[256,256]{1,0:T(8,128)S(1)}, f32[256,256]{1,0:T(8,128)S(1)}, u32[]{:S(2)}, u32[]{:S(2)}) collective-permute-start(f32[256,256]{1,0:T(8,128)S(1)} %pad_maximum_fusion.4), channel_id=1, source_target_pairs={{0,24},{4,28},{8,16},{12,20},{16,8},{20,12},{24,0},{28,4},{1,25},{... | collective-permute-start | bytes 786440 | tf_op jit(solution)/shard_map/ppermute | solution.py:228
  53.9 4.5 %collective-permute-start.17 = (f32[512,256]{1,0:T(8,128)S(1)}, f32[512,256]{1,0:T(8,128)S(1)}, u32[]{:S(2)}, u32[]{:S(2)}) collective-permute-start(f32[512,256]{1,0:T(8,128)S(1)} %pad_maximum_fusion.2.refs_2_), channel_id=1, source_target_pairs={{0,4},{4,0},{8,12},{12,8},{16,20},{20,16},{24,28},{28,24},{1,5},{5... | collective-permute-start | bytes 1572872 | tf_op jit(solution)/shard_map/ppermute | solution.py:228
  55.7 16.7 %collective-permute-start.18 = (f32[256,256]{1,0:T(8,128)S(1)}, f32[256,256]{1,0:T(8,128)S(1)}, u32[]{:S(2)}, u32[]{:S(2)}) collective-permute-start(f32[256,256]{1,0:T(8,128)S(1)} %bitcast.37), channel_id=1, source_target_pairs={{0,8},{4,12},{8,0},{12,4},{16,24},{20,28},{24,16},{28,20},{1,9},{5... | collective-permute-start | bytes 786440 | tf_op jit(solution)/shard_map/ppermute | solution.py:228
  57.0 15.5 %collective-permute-start.19 = (f32[256,256]{1,0:T(8,128)S(1)}, f32[256,256]{1,0:T(8,128)S(1)}, u32[]{:S(2)}, u32[]{:S(2)}) collective-permute-start(f32[256,256]{1,0:T(8,128)S(1)} %bitcast.38), channel_id=1, source_target_pairs={{0,16},{4,20},{8,24},{12,28},{16,0},{20,4},{24,8},{28,12},{1,17},{... | collective-permute-start | bytes 786440 | tf_op jit(solution)/shard_map/ppermute | solution.py:228
  57.2 15.3 %collective-permute-start.20 = (f32[256,256]{1,0:T(8,128)S(1)}, f32[256,256]{1,0:T(8,128)S(1)}, u32[]{:S(2)}, u32[]{:S(2)}) collective-permute-start(f32[256,256]{1,0:T(8,128)S(1)} %bitcast.39), channel_id=1, source_target_pairs={{0,24},{4,28},{8,16},{12,20},{16,8},{20,12},{24,0},{28,4},{1,25},{... | collective-permute-start | bytes 786440 | tf_op jit(solution)/shard_map/ppermute | solution.py:228
  72.6 2.5 %collective-permute-start.21 = (f32[512,256]{1,0:T(8,128)S(1)}, f32[512,256]{1,0:T(8,128)S(1)}, u32[]{:S(2)}, u32[]{:S(2)}) collective-permute-start(f32[512,256]{1,0:T(8,128)S(1)} %pad_maximum_fusion.3.refs_2_), channel_id=1, source_target_pairs={{0,4},{4,0},{8,12},{12,8},{16,20},{20,16},{24,28},{28,24},{1,5},{5... | collective-permute-start | bytes 1572872 | tf_op jit(solution)/shard_map/ppermute | solution.py:228

commit v6 on v5

--- a/solution.py
+++ b/solution.py
@@ -105,16 +105,25 @@
     return jnp.where(r == c, 1.0, 0.0).astype(jnp.float32)
 
 
-def factor_panel(block, inverse):
-    w0 = factor_half(block[:HALF, :HALF])
+def factor_panel(corner, side, rest, inverse):
+    w0 = factor_half(corner)
     sw0 = split(w0)
-    side = split(block[HALF:, :HALF])
+    side = split(side)
     low = split(mm(side, sw0, NT))
-    w1 = factor_half(block[HALF:, HALF:] - mm(low, split(mm(sw0, side, NT)), NN))
+    w1 = factor_half(rest - mm(low, split(mm(sw0, side, NT)), NN))
     inverse[:HALF, :HALF] = w0
     inverse[:HALF, HALF:] = jnp.zeros((HALF, HALF), jnp.float32)
     inverse[HALF:, :HALF] = -mm(split(w1), split(mm(low, sw0, NN)), NN)
     inverse[HALF:, HALF:] = w1
+
+
+def quarters(block):
+    return block[:HALF, :HALF], block[HALF:, :HALF], block[HALF:, HALF:]
+
+
+def less_square(block, a, b):
+    q00, q10, q11 = quarters(block)
+    return q00 - mm(a, a, TN), q10 - mm(b, a, TN), q11 - mm(b, b, TN)
 
 
 def halves(mine, other, core):
@@ -133,11 +142,11 @@
 
 def first_kernel(place, mine_ref, other_ref, inverse_ref, block):
     block[...] = halves(mine_ref.at[:HALF], other_ref.at[:HALF], lax.rem(place[0], 2))
-    factor_panel(block, inverse_ref)
+    factor_panel(*quarters(block[...]), inverse_ref)
 
 
 def rest_kernel(place, w0_ref, *refs):
-    pieces, inverses, upper, block, later = (refs[:2], refs[2:4]), refs[4], refs[5], refs[6], refs[7]
+    pieces, inverses, upper = (refs[:2], refs[2:4]), refs[4], refs[5]
     core = lax.rem(place[0], 2)
 
     def piece(group, k):
@@ -145,25 +154,22 @@
         return halves(mine.at[k * HALF:(k + 1) * HALF], other.at[k * HALF:(k + 1) * HALF], core)
 
     w0 = split(w0_ref[...])
-    u01 = mm(w0, split(piece(1, 0)), NN)
+    a01 = piece(1, 0)
+    u01a = mm(w0, split(a01[:, :HALF]), NN)
+    u01b = mm(w0, split(a01[:, HALF:]), NN)
+    factor_panel(*less_square(piece(1, 1), split(u01a), split(u01b)), inverses.at[0])
+    u01 = jnp.concatenate([u01a, u01b], axis=1)
     u02 = mm(w0, split(piece(0, 1)), NT)
     upper[0] = u01
     upper[1] = u02
     su01, su02 = split(u01), split(u02)
-    block[...] = piece(1, 1) - mm(su01, su01, TN)
-    later[0] = piece(1, 2).T - mm(su01, su02, TN)
-    later[1] = piece(1, 3) - mm(su02, su02, TN)
-
-    @pl.loop(0, 2)
-    def _(k):
-        factor_panel(block, inverses.at[k])
-
-        @pl.when(k == 0)
-        def _():
-            u12 = mm(split(inverses[0]), split(later[0]), NN)
-            upper[2] = u12
-            su12 = split(u12)
-            block[...] = later[1] - mm(su12, su12, TN)
+    s21 = piece(1, 2) - mm(su02, su01, TN)
+    rest = piece(1, 3) - mm(su02, su02, TN)
+    w1 = split(inverses[0])
+    u12a = mm(w1, split(s21[:HALF]), NT)
+    u12b = mm(w1, split(s21[HALF:]), NT)
+    factor_panel(*less_square(rest, split(u12a), split(u12b)), inverses.at[1])
+    upper[2] = jnp.concatenate([u12a, u12b], axis=1)
 
 
 def apply_kernel(place, own_ref, right_ref, b0_ref, b1_ref, b2_ref, w0_ref, inverses, upper, *refs):
@@ -355,7 +361,7 @@
     inverses, upper = call(
         rest_kernel, "rest",
         (jax.ShapeDtypeStruct((2, nb, nb), f32), jax.ShapeDtypeStruct((PANELS, nb, nb), f32)),
-        [*chain, pltpu.VMEM((2, nb, nb), f32)], 15.0,
+        [], 15.0,
         w0, *one, *two)
     top_own = cross(*land(top_own, p, inverses))
     return call(

time: 79.9 us -> 79.6 us (level)
  no operation moved by 1% of the time
where the time goes in v6:
time: 79.6 us; the launch traced here: 79.4 us
  starting transfers between devices  27.9 us (35%)
  Pallas kernels  24.8 us (31%)
  waiting for transfers between devices  23 us (29%)
  other arithmetic  1.81 us (2%)
  local copies, waits for them, and re-layouts  1.7 us (2%)
    pallas_call x3, Pallas kernels, call(): pl.pallas_call(body, out_shape=outs, in_specs=[smem] + [vmem] * len(opera...  24.8 us
    ppermute x17, starting transfers between devices, swap(): return lax.ppermute(value, axis, [(i, i ^ bit) for i in range(n)])  17.2 us
    ppermute x17, waiting for transfers between devices, swap(): return lax.ppermute(value, axis, [(i, i ^ bit) for i in range(n)])  14.9 us
    ppermute x2, starting transfers between devices, along_col(): came = [lax.ppermute(value, 'col', steps_right(s, n_col))]  6.41 us
    ppermute x2, waiting for transfers between devices, along_col(): came.append(lax.ppermute(back, ('row', 'col'), pairs))  4.21 us
    ppermute x2, waiting for transfers between devices, along_col(): came = [lax.ppermute(value, 'col', steps_right(s, n_col))]  3.85 us
    ppermute x2, starting transfers between devices, along_col(): came.append(lax.ppermute(back, ('row', 'col'), pairs))  3.4 us
    slice x1, local copies, waits for them, and re-layouts, shards(): right = kernel[0, :, 1, :]  1.65 us
  transfers between devices with their start and end apart: 22, of which 11 were waited for; matrix products, arithmetic and copies ran while one was open for 2% of the time, Pallas kernels for 26%

profile of v6, /device:TPU:13, one launch (start us, length us, event | category | flops | bytes accessed | tf_op | source)
XLA Modules:
  0.0 79.4 jit_solution(6456969006900780733)
XLA Ops:
  0.0 1.6 %fusion.1 = (f32[1,256,1,256]{3,2,1,0:T(1,128)S(1)}, f32[1,256,1,256]{3,2,1,0:T(1,128)S(1)}) fusion(f32[1,256,2,256]{3,2,1,0:T(2,128)} %param.1), kind=kLoop, calls=%fused_computation.30 | loop fusion | bytes 1048576 | tf_op jit(solution)/shard_map/slice | solution.py:320
  1.7 3.2 %collective-permute-start = (f32[256,256]{1,0:T(8,128)S(1)}, f32[256,256]{1,0:T(8,128)S(1)}, u32[]{:S(2)}, u32[]{:S(2)}) collective-permute-start(f32[256,256]{1,0:T(8,128)S(1)} %bitcast.35), channel_id=1, source_target_pairs={{0,1},{1,2},{2,3},{4,5},{5,6},{6,7},{8,9},{9,10},{10,11},{12,13},{... | collective-permute-start | bytes 786440 | tf_op jit(solution)/shard_map/ppermute | solution.py:273
  4.9 2.1 %collective-permute-start.1 = (f32[256,256]{1,0:T(8,128)S(1)}, f32[256,256]{1,0:T(8,128)S(1)}, u32[]{:S(2)}, u32[]{:S(2)}) collective-permute-start(f32[256,256]{1,0:T(8,128)S(1)} %bitcast.36), channel_id=1, source_target_pairs={{1,0},{2,1},{5,4},{6,5},{9,8},{10,9},{13,12},{14,13},{17,16},{18,1... | collective-permute-start | bytes 786440 | tf_op jit(solution)/shard_map/ppermute | solution.py:278
  7.0 1.3 %collective-permute-start.2 = (f32[256,256]{1,0:T(8,128)S(1)}, f32[256,256]{1,0:T(8,128)S(1)}, u32[]{:S(2)}, u32[]{:S(2)}) collective-permute-start(f32[256,256]{1,0:T(8,128)S(1)} %bitcast.42), channel_id=1, source_target_pairs={{0,8},{4,12},{8,0},{12,4},{16,24},{20,28},{24,16},{28,20},{1,9},{5... | collective-permute-start | bytes 786440 | tf_op jit(solution)/shard_map/ppermute | solution.py:234
  8.5 2.2 %collective-permute-done = f32[256,256]{1,0:T(8,128)S(1)} collective-permute-done((f32[256,256]{1,0:T(8,128)S(1)}, f32[256,256]{1,0:T(8,128)S(1)}, u32[]{:S(2)}, u32[]{:S(2)}) %collective-permute-start) | collective-permute-done | bytes 262176 | tf_op jit(solution)/shard_map/ppermute | solution.py:273
  10.7 2.9 %collective-permute-done.1 = f32[256,256]{1,0:T(8,128)S(1)} collective-permute-done((f32[256,256]{1,0:T(8,128)S(1)}, f32[256,256]{1,0:T(8,128)S(1)}, u32[]{:S(2)}, u32[]{:S(2)}) %collective-permute-start.1) | collective-permute-done | bytes 262176 | tf_op jit(solution)/shard_map/ppermute | solution.py:278
  13.6 0.9 %collective-permute-done.3 = f32[256,256]{1,0:T(8,128)S(1)} collective-permute-done((f32[256,256]{1,0:T(8,128)S(1)}, f32[256,256]{1,0:T(8,128)S(1)}, u32[]{:S(2)}, u32[]{:S(2)}) %collective-permute-start.3) | collective-permute-done | bytes 262176 | tf_op jit(solution)/shard_map/ppermute | solution.py:234
  14.6 3.2 %collective-permute-start.4 = (f32[256,256]{1,0:T(8,128)S(1)}, f32[256,256]{1,0:T(8,128)S(1)}, u32[]{:S(2)}, u32[]{:S(2)}) collective-permute-start(f32[256,256]{1,0:T(8,128)S(1)} %collective-permute-done), channel_id=1, source_target_pairs={{1,2},{2,3},{5,6},{6,7},{9,10},{10,11},{13,14},{14,15},{17,18},{18... | collective-permute-start | bytes 786440 | tf_op jit(solution)/shard_map/ppermute | solution.py:273
  17.8 1.3 %collective-permute-start.5 = (f32[256,256]{1,0:T(8,128)S(1)}, f32[256,256]{1,0:T(8,128)S(1)}, u32[]{:S(2)}, u32[]{:S(2)}) collective-permute-start(f32[256,256]{1,0:T(8,128)S(1)} %collective-permute-done.1), channel_id=1, source_target_pairs={{1,0},{5,4},{9,8},{13,12},{17,16},{21,20},{25,24},{29,28}} | collective-permute-start | bytes 786440 | tf_op jit(solution)/shard_map/ppermute | solution.py:278
  19.1 0.3 collective-permute-start.6
  19.5 1.6 %collective-permute-done.4 = f32[256,256]{1,0:T(8,128)S(1)} collective-permute-done((f32[256,256]{1,0:T(8,128)S(1)}, f32[256,256]{1,0:T(8,128)S(1)}, u32[]{:S(2)}, u32[]{:S(2)}) %collective-permute-start.4) | collective-permute-done | bytes 262176 | tf_op jit(solution)/shard_map/ppermute | solution.py:273
  21.1 1.3 %collective-permute-done.5 = f32[256,256]{1,0:T(8,128)S(1)} collective-permute-done((f32[256,256]{1,0:T(8,128)S(1)}, f32[256,256]{1,0:T(8,128)S(1)}, u32[]{:S(2)}, u32[]{:S(2)}) %collective-permute-start.5) | collective-permute-done | bytes 262176 | tf_op jit(solution)/shard_map/ppermute | solution.py:278
  22.4 2.1 %collective-permute-done.6 = f32[256,256]{1,0:T(8,128)} collective-permute-done((f32[256,256]{1,0:T(8,128)S(1)}, f32[256,256]{1,0:T(8,128)}, u32[]{:S(2)}, u32[]{:S(2)}) %collective-permute-start.6) | collective-permute-done | bytes 262176 | tf_op jit(solution)/shard_map/ppermute | solution.py:234
  24.8 3.9 %collective-permute-start.7 = (f32[3,128,256]{2,1,0:T(8,128)S(1)}, f32[3,128,256]{2,1,0:T(8,128)S(1)}, u32[]{:S(2)}, u32[]{:S(2)}) collective-permute-start(f32[3,128,256]{2,1,0:T(8,128)S(1)} %select_bitcast_fusion), channel_id=1, source_target_pairs={{0,4},{4,0},{8,12},{12,8},{16,20},{20,16},{24,28},{28,24},{1,5},{5... | collective-permute-start | bytes 1179656 | tf_op jit(solution)/shard_map/ppermute | solution.py:234
  28.7 1.0 %select_select_fusion.5 = (f32[256,256]{1,0:T(8,128)S(1)}, f32[256,256]{1,0:T(8,128)S(1)}) fusion(f32[256,256]{1,0:T(8,128)S(1)} %bitcast.44, f32[256,256]{1,0:T(8,128)S(1)} %collective-permute-done.2, f32[256,256]{1,0:T(8,128)S(1)} %collective-permute-done.3, f32[256,256]{1,0:T(8,128)} %collective-permute-done.6, pred[]{:T(512)S(6)} %eq.38, pred[]{:T(512)S(6)} %eq.37, ...), kind=kLoop, calls=%fused_computation.15 | loop fusion | flops 393216 | bytes 1572870 | tf_op jit(solution)/shard_map/jit(_where)/select_n | solution.py:252
  30.2 0.3 collective-permute-start.12
  30.7 2.2 %collective-permute-start.10 = (f32[128,256]{1,0:T(8,128)S(1)}, f32[128,256]{1,0:T(8,128)S(1)}, u32[]{:S(2)}, u32[]{:S(2)}) collective-permute-start(f32[128,256]{1,0:T(8,128)S(1)} %get-tuple-element.44), channel_id=1, source_target_pairs={{0,24},{4,28},{8,16},{12,20},{16,8},{20,12},{24,0},{28,4},{1,25},{... | collective-permute-start | bytes 393224 | tf_op jit(solution)/shard_map/ppermute | solution.py:234
  32.9 0.3 collective-permute-start.8
  33.2 0.2 collective-permute-start.9
  33.4 7.2 %collective-permute-done.10 = f32[128,256]{1,0:T(8,128)S(1)} collective-permute-done((f32[128,256]{1,0:T(8,128)S(1)}, f32[128,256]{1,0:T(8,128)S(1)}, u32[]{:S(2)}, u32[]{:S(2)}) %collective-permute-start.10) | collective-permute-done | bytes 131104 | tf_op jit(solution)/shard_map/ppermute | solution.py:234
  40.6 2.9 %collective-permute-done.8 = f32[128,256]{1,0:T(8,128)S(1)} collective-permute-done((f32[128,256]{1,0:T(8,128)S(1)}, f32[128,256]{1,0:T(8,128)S(1)}, u32[]{:S(2)}, u32[]{:S(2)}) %collective-permute-start.8) | collective-permute-done | bytes 131104 | tf_op jit(solution)/shard_map/ppermute | solution.py:234
  43.5 1.5 %collective-permute-start.15 = (f32[256,256]{1,0:T(8,128)S(1)}, f32[256,256]{1,0:T(8,128)S(1)}, u32[]{:S(2)}, u32[]{:S(2)}) collective-permute-start(f32[256,256]{1,0:T(8,128)S(1)} %pad_maximum_fusion.5.mine_ref.refs_0_), channel_id=1, source_target_pairs={{0,4},{4,0},{8,12},{12,8},{16,20},{20,16},{24,28},{28,24},{1,5},{5... | collective-permute-start | bytes 786440 | tf_op jit(solution)/shard_map/ppermute | solution.py:234
  45.0 0.8 %collective-permute-start.14 = (f32[256,256]{1,0:T(8,128)S(1)}, f32[256,256]{1,0:T(8,128)S(1)}, u32[]{:S(2)}, u32[]{:S(2)}) collective-permute-start(f32[256,256]{1,0:T(8,128)S(1)} %copy-done.1), channel_id=1, source_target_pairs={{2,3},{6,7},{10,11},{14,15},{18,19},{22,23},{26,27},{30,31}} | collective-permute-start | bytes 786440 | tf_op jit(solution)/shard_map/ppermute | solution.py:299
  45.9 1.2 %collective-permute-start.16 = (f32[256,256]{1,0:T(8,128)S(1)}, f32[256,256]{1,0:T(8,128)S(1)}, u32[]{:S(2)}, u32[]{:S(2)}) collective-permute-start(f32[256,256]{1,0:T(8,128)S(1)} %pad_maximum_fusion.4), channel_id=1, source_target_pairs={{0,24},{4,28},{8,16},{12,20},{16,8},{20,12},{24,0},{28,4},{1,25},{... | collective-permute-start | bytes 786440 | tf_op jit(solution)/shard_map/ppermute | solution.py:234
  47.2 6.5 %first.1.w0_ref = f32[256,256]{1,0:T(8,128)S(1)} custom-call(s32[2]{0:T(128)S(1)} %pad_add_fusion.place, f32[256,256]{1,0:T(8,128)S(1)} %pad_maximum_fusion.5.mine_ref.refs_0_, f32[256,256]{1,0:T(8,128)S(1)} %collective-permute-done.15.other_ref.refs_1_), custom_call_target="tpu_custom_call" | custom-call | bytes 22750000 | tf_op jit(solution)/shard_map/first/pallas_call | solution.py:328
  53.9 1.8 %collective-permute-start.17 = (f32[512,256]{1,0:T(8,128)S(1)}, f32[512,256]{1,0:T(8,128)S(1)}, u32[]{:S(2)}, u32[]{:S(2)}) collective-permute-start(f32[512,256]{1,0:T(8,128)S(1)} %pad_maximum_fusion.2.refs_2_), channel_id=1, source_target_pairs={{0,4},{4,0},{8,12},{12,8},{16,20},{20,16},{24,28},{28,24},{1,5},{5... | collective-permute-start | bytes 1572872 | tf_op jit(solution)/shard_map/ppermute | solution.py:234
  55.7 1.2 %collective-permute-start.18 = (f32[256,256]{1,0:T(8,128)S(1)}, f32[256,256]{1,0:T(8,128)S(1)}, u32[]{:S(2)}, u32[]{:S(2)}) collective-permute-start(f32[256,256]{1,0:T(8,128)S(1)} %bitcast.37), channel_id=1, source_target_pairs={{0,8},{4,12},{8,0},{12,4},{16,24},{20,28},{24,16},{28,20},{1,9},{5... | collective-permute-start | bytes 786440 | tf_op jit(solution)/shard_map/ppermute | solution.py:234
  57.2 1.2 %collective-permute-start.20 = (f32[256,256]{1,0:T(8,128)S(1)}, f32[256,256]{1,0:T(8,128)S(1)}, u32[]{:S(2)}, u32[]{:S(2)}) collective-permute-start(f32[256,256]{1,0:T(8,128)S(1)} %bitcast.39), channel_id=1, source_target_pairs={{0,24},{4,28},{8,16},{12,20},{16,8},{20,12},{24,0},{28,4},{1,25},{... | collective-permute-start | bytes 786440 | tf_op jit(solution)/shard_map/ppermute | solution.py:234
  58.4 14.0 %rest.1 = (f32[2,256,256]{2,1,0:T(8,128)S(1)}, f32[3,256,256]{2,1,0:T(8,128)S(1)}) custom-call(s32[2]{0:T(128)S(1)} %pad_add_fusion.place, f32[256,256]{1,0:T(8,128)S(1)} %first.1.w0_ref, f32[256,256]{1,0:T(8,128)S(1)} %pad_maximum_fusion.5.mine_ref.refs_0_, f32[256,256]{1,0:T(8,128)S(1)} %collective-permute-done.15.other_ref.refs_1_, ...), custom_call_target="tpu_custom_call" | custom-call | bytes 52500000 | tf_op jit(solution)/shard_map/rest/pallas_call | solution.py:328
  72.6 1.0 %collective-permute-start.21 = (f32[512,256]{1,0:T(8,128)S(1)}, f32[512,256]{1,0:T(8,128)S(1)}, u32[]{:S(2)}, u32[]{:S(2)}) collective-permute-start(f32[512,256]{1,0:T(8,128)S(1)} %pad_maximum_fusion.3.refs_2_), channel_id=1, source_target_pairs={{0,4},{4,0},{8,12},{12,8},{16,20},{20,16},{24,28},{28,24},{1,5},{5... | collective-permute-start | bytes 1572872 | tf_op jit(solution)/shard_map/ppermute | solution.py:234
  73.5 1.5 %collective-permute-done.21.refs_3_ = f32[512,256]{1,0:T(8,128)S(1)} collective-permute-done((f32[512,256]{1,0:T(8,128)S(1)}, f32[512,256]{1,0:T(8,128)S(1)}, u32[]{:S(2)}, u32[]{:S(2)}) %collective-permute-start.21) | collective-permute-done | bytes 524320 | tf_op jit(solution)/shard_map/ppermute | solution.py:234
  75.1 4.3 %apply.1 = f32[1,256,2,256]{3,2,1,0:T(2,128)} custom-call(s32[2]{0:T(128)S(1)} %pad_add_fusion.place, f32[256,256]{1,0:T(8,128)S(1)} %bitcast.41, f32[256,256]{1,0:T(8,128)S(1)} %bitcast.45, f32[256,256]{1,0:T(8,128)S(1)} %broadcast_select_fusion.1.b0_ref, f32[256,256]{1,0:T(8,128)S(1)} %get-tuple-element.65.b1_ref, ...), custom_call_target="tpu_custom_call" | custom-call | bytes 21000000 | tf_op jit(solution)/shard_map/apply/pallas_call | solution.py:328
  (38 shorter events, 1.9 us)
Async XLA Ops:
  1.7 9.1 %collective-permute-start = (f32[256,256]{1,0:T(8,128)S(1)}, f32[256,256]{1,0:T(8,128)S(1)}, u32[]{:S(2)}, u32[]{:S(2)}) collective-permute-start(f32[256,256]{1,0:T(8,128)S(1)} %bitcast.35), channel_id=1, source_target_pairs={{0,1},{1,2},{2,3},{4,5},{5,6},{6,7},{8,9},{9,10},{10,11},{12,13},{... | collective-permute-start | bytes 786440 | tf_op jit(solution)/shard_map/ppermute | solution.py:273
  4.9 8.8 %collective-permute-start.1 = (f32[256,256]{1,0:T(8,128)S(1)}, f32[256,256]{1,0:T(8,128)S(1)}, u32[]{:S(2)}, u32[]{:S(2)}) collective-permute-start(f32[256,256]{1,0:T(8,128)S(1)} %bitcast.36), channel_id=1, source_target_pairs={{1,0},{2,1},{5,4},{6,5},{9,8},{10,9},{13,12},{14,13},{17,16},{18,1... | collective-permute-start | bytes 786440 | tf_op jit(solution)/shard_map/ppermute | solution.py:278
  7.0 6.6 %collective-permute-start.2 = (f32[256,256]{1,0:T(8,128)S(1)}, f32[256,256]{1,0:T(8,128)S(1)}, u32[]{:S(2)}, u32[]{:S(2)}) collective-permute-start(f32[256,256]{1,0:T(8,128)S(1)} %bitcast.42), channel_id=1, source_target_pairs={{0,8},{4,12},{8,0},{12,4},{16,24},{20,28},{24,16},{28,20},{1,9},{5... | collective-permute-start | bytes 786440 | tf_op jit(solution)/shard_map/ppermute | solution.py:234
  8.3 6.3 %collective-permute-start.3 = (f32[256,256]{1,0:T(8,128)S(1)}, f32[256,256]{1,0:T(8,128)S(1)}, u32[]{:S(2)}, u32[]{:S(2)}) collective-permute-start(f32[256,256]{1,0:T(8,128)S(1)} %bitcast.43), channel_id=1, source_target_pairs={{0,16},{4,20},{8,24},{12,28},{16,0},{20,4},{24,8},{28,12},{1,17},{... | collective-permute-start | bytes 786440 | tf_op jit(solution)/shard_map/ppermute | solution.py:234
  14.6 6.5 %collective-permute-start.4 = (f32[256,256]{1,0:T(8,128)S(1)}, f32[256,256]{1,0:T(8,128)S(1)}, u32[]{:S(2)}, u32[]{:S(2)}) collective-permute-start(f32[256,256]{1,0:T(8,128)S(1)} %collective-permute-done), channel_id=1, source_target_pairs={{1,2},{2,3},{5,6},{6,7},{9,10},{10,11},{13,14},{14,15},{17,18},{18... | collective-permute-start | bytes 786440 | tf_op jit(solution)/shard_map/ppermute | solution.py:273
  17.8 4.6 %collective-permute-start.5 = (f32[256,256]{1,0:T(8,128)S(1)}, f32[256,256]{1,0:T(8,128)S(1)}, u32[]{:S(2)}, u32[]{:S(2)}) collective-permute-start(f32[256,256]{1,0:T(8,128)S(1)} %collective-permute-done.1), channel_id=1, source_target_pairs={{1,0},{5,4},{9,8},{13,12},{17,16},{21,20},{25,24},{29,28}} | collective-permute-start | bytes 786440 | tf_op jit(solution)/shard_map/ppermute | solution.py:278
  19.1 5.4 %collective-permute-start.6 = (f32[256,256]{1,0:T(8,128)S(1)}, f32[256,256]{1,0:T(8,128)}, u32[]{:S(2)}, u32[]{:S(2)}) collective-permute-start(f32[256,256]{1,0:T(8,128)S(1)} %collective-permute-done.3), channel_id=1, source_target_pairs={{0,8},{4,12},{8,0},{12,4},{16,24},{20,28},{24,16},{28,20},{1,9},{5... | collective-permute-start | bytes 786440 | tf_op jit(solution)/shard_map/ppermute | solution.py:234
  21.1 3.6 %copy-start = (f32[256,256]{1,0:T(8,128)}, f32[256,256]{1,0:T(8,128)S(1)}, u32[]{:S(2)}) copy-start(f32[256,256]{1,0:T(8,128)S(1)} %collective-permute-done.4) | copy-start | bytes 786436
  24.8 5.3 %collective-permute-start.7 = (f32[3,128,256]{2,1,0:T(8,128)S(1)}, f32[3,128,256]{2,1,0:T(8,128)S(1)}, u32[]{:S(2)}, u32[]{:S(2)}) collective-permute-start(f32[3,128,256]{2,1,0:T(8,128)S(1)} %select_bitcast_fusion), channel_id=1, source_target_pairs={{0,4},{4,0},{8,12},{12,8},{16,20},{20,16},{24,28},{28,24},{1,5},{5... | collective-permute-start | bytes 1179656 | tf_op jit(solution)/shard_map/ppermute | solution.py:234
  29.8 3.4 %collective-permute-start.11 = (f32[512,256]{1,0:T(8,128)S(1)}, f32[512,256]{1,0:T(8,128)S(1)}, u32[]{:S(2)}, u32[]{:S(2)}) collective-permute-start(f32[512,256]{1,0:T(8,128)S(1)} %pad_maximum_fusion.1.refs_0_), channel_id=1, source_target_pairs={{0,4},{4,0},{8,12},{12,8},{16,20},{20,16},{24,28},{28,24},{1,5},{5... | collective-permute-start | bytes 1572872 | tf_op jit(solution)/shard_map/ppermute | solution.py:234
  30.2 13.3 %collective-permute-start.12 = (f32[256,256]{1,0:T(8,128)S(1)}, f32[256,256]{1,0:T(8,128)S(1)}, u32[]{:S(2)}, u32[]{:S(2)}) collective-permute-start(f32[256,256]{1,0:T(8,128)S(1)} %pad_maximum_fusion.4), channel_id=1, source_target_pairs={{0,8},{4,12},{8,0},{12,4},{16,24},{20,28},{24,16},{28,20},{1,9},{5... | collective-permute-start | bytes 786440 | tf_op jit(solution)/shard_map/ppermute | solution.py:234
  30.5 12.9 %collective-permute-start.13 = (f32[256,256]{1,0:T(8,128)S(1)}, f32[256,256]{1,0:T(8,128)S(1)}, u32[]{:S(2)}, u32[]{:S(2)}) collective-permute-start(f32[256,256]{1,0:T(8,128)S(1)} %pad_maximum_fusion.4), channel_id=1, source_target_pairs={{0,16},{4,20},{8,24},{12,28},{16,0},{20,4},{24,8},{28,12},{1,17},{... | collective-permute-start | bytes 786440 | tf_op jit(solution)/shard_map/ppermute | solution.py:234
  30.7 9.8 %collective-permute-start.10 = (f32[128,256]{1,0:T(8,128)S(1)}, f32[128,256]{1,0:T(8,128)S(1)}, u32[]{:S(2)}, u32[]{:S(2)}) collective-permute-start(f32[128,256]{1,0:T(8,128)S(1)} %get-tuple-element.44), channel_id=1, source_target_pairs={{0,24},{4,28},{8,16},{12,20},{16,8},{20,12},{24,0},{28,4},{1,25},{... | collective-permute-start | bytes 393224 | tf_op jit(solution)/shard_map/ppermute | solution.py:234
  32.9 10.5 %collective-permute-start.8 = (f32[128,256]{1,0:T(8,128)S(1)}, f32[128,256]{1,0:T(8,128)S(1)}, u32[]{:S(2)}, u32[]{:S(2)}) collective-permute-start(f32[128,256]{1,0:T(8,128)S(1)} %get-tuple-element.44), channel_id=1, source_target_pairs={{0,8},{4,12},{8,0},{12,4},{16,24},{20,28},{24,16},{28,20},{1,9},{5... | collective-permute-start | bytes 393224 | tf_op jit(solution)/shard_map/ppermute | solution.py:234
  33.2 10.3 %collective-permute-start.9 = (f32[128,256]{1,0:T(8,128)S(1)}, f32[128,256]{1,0:T(8,128)S(1)}, u32[]{:S(2)}, u32[]{:S(2)}) collective-permute-start(f32[128,256]{1,0:T(8,128)S(1)} %get-tuple-element.44), channel_id=1, source_target_pairs={{0,16},{4,20},{8,24},{12,28},{16,0},{20,4},{24,8},{28,12},{1,17},{... | collective-permute-start | bytes 393224 | tf_op jit(solution)/shard_map/ppermute | solution.py:234
  43.5 1.5 %copy-start.1 = (f32[256,256]{1,0:T(8,128)S(1)}, f32[256,256]{1,0:T(8,128)}, u32[]{:S(2)}) copy-start(f32[256,256]{1,0:T(8,128)} %copy-done) | copy-start | bytes 786436
  43.5 3.6 %collective-permute-start.15 = (f32[256,256]{1,0:T(8,128)S(1)}, f32[256,256]{1,0:T(8,128)S(1)}, u32[]{:S(2)}, u32[]{:S(2)}) collective-permute-start(f32[256,256]{1,0:T(8,128)S(1)} %pad_maximum_fusion.5.mine_ref.refs_0_), channel_id=1, source_target_pairs={{0,4},{4,0},{8,12},{12,8},{16,20},{20,16},{24,28},{28,24},{1,5},{5... | collective-permute-start | bytes 786440 | tf_op jit(solution)/shard_map/ppermute | solution.py:234
  45.0 8.7 %collective-permute-start.14 = (f32[256,256]{1,0:T(8,128)S(1)}, f32[256,256]{1,0:T(8,128)S(1)}, u32[]{:S(2)}, u32[]{:S(2)}) collective-permute-start(f32[256,256]{1,0:T(8,128)S(1)} %copy-done.1), channel_id=1, source_target_pairs={{2,3},{6,7},{10,11},{14,15},{18,19},{22,23},{26,27},{30,31}} | collective-permute-start | bytes 786440 | tf_op jit(solution)/shard_map/ppermute | solution.py:299
  45.9 7.9 %collective-permute-start.16 = (f32[256,256]{1,0:T(8,128)S(1)}, f32[256,256]{1,0:T(8,128)S(1)}, u32[]{:S(2)}, u32[]{:S(2)}) collective-permute-start(f32[256,256]{1,0:T(8,128)S(1)} %pad_maximum_fusion.4), channel_id=1, source_target_pairs={{0,24},{4,28},{8,16},{12,20},{16,8},{20,12},{24,0},{28,4},{1,25},{... | collective-permute-start | bytes 786440 | tf_op jit(solution)/shard_map/ppermute | solution.py:234
  53.9 4.5 %collective-permute-start.17 = (f32[512,256]{1,0:T(8,128)S(1)}, f32[512,256]{1,0:T(8,128)S(1)}, u32[]{:S(2)}, u32[]{:S(2)}) collective-permute-start(f32[512,256]{1,0:T(8,128)S(1)} %pad_maximum_fusion.2.refs_2_), channel_id=1, source_target_pairs={{0,4},{4,0},{8,12},{12,8},{16,20},{20,16},{24,28},{28,24},{1,5},{5... | collective-permute-start | bytes 1572872 | tf_op jit(solution)/shard_map/ppermute | solution.py:234
  55.7 16.7 %collective-permute-start.18 = (f32[256,256]{1,0:T(8,128)S(1)}, f32[256,256]{1,0:T(8,128)S(1)}, u32[]{:S(2)}, u32[]{:S(2)}) collective-permute-start(f32[256,256]{1,0:T(8,128)S(1)} %bitcast.37), channel_id=1, source_target_pairs={{0,8},{4,12},{8,0},{12,4},{16,24},{20,28},{24,16},{28,20},{1,9},{5... | collective-permute-start | bytes 786440 | tf_op jit(solution)/shard_map/ppermute | solution.py:234
  57.0 15.5 %collective-permute-start.19 = (f32[256,256]{1,0:T(8,128)S(1)}, f32[256,256]{1,0:T(8,128)S(1)}, u32[]{:S(2)}, u32[]{:S(2)}) collective-permute-start(f32[256,256]{1,0:T(8,128)S(1)} %bitcast.38), channel_id=1, source_target_pairs={{0,16},{4,20},{8,24},{12,28},{16,0},{20,4},{24,8},{28,12},{1,17},{... | collective-permute-start | bytes 786440 | tf_op jit(solution)/shard_map/ppermute | solution.py:234
  57.2 15.2 %collective-permute-start.20 = (f32[256,256]{1,0:T(8,128)S(1)}, f32[256,256]{1,0:T(8,128)S(1)}, u32[]{:S(2)}, u32[]{:S(2)}) collective-permute-start(f32[256,256]{1,0:T(8,128)S(1)} %bitcast.39), channel_id=1, source_target_pairs={{0,24},{4,28},{8,16},{12,20},{16,8},{20,12},{24,0},{28,4},{1,25},{... | collective-permute-start | bytes 786440 | tf_op jit(solution)/shard_map/ppermute | solution.py:234
  72.6 2.5 %collective-permute-start.21 = (f32[512,256]{1,0:T(8,128)S(1)}, f32[512,256]{1,0:T(8,128)S(1)}, u32[]{:S(2)}, u32[]{:S(2)}) collective-permute-start(f32[512,256]{1,0:T(8,128)S(1)} %pad_maximum_fusion.3.refs_2_), channel_id=1, source_target_pairs={{0,4},{4,0},{8,12},{12,8},{16,20},{20,16},{24,28},{28,24},{1,5},{5... | collective-permute-start | bytes 1572872 | tf_op jit(solution)/shard_map/ppermute | solution.py:234

commit v7 on v6

--- a/solution.py
+++ b/solution.py
@@ -243,6 +243,15 @@
     return [value, swap(value, "row", 2), swap(value, "row", 4), far]
 
 
+def launch_beyond(value):
+    n_row, n_col = lax.axis_size("row"), lax.axis_size("col")
+    far, x, y = [
+        lax.ppermute(value, ("row", "col"), [
+            (r * n_col + k, (r ^ bit) * n_col + k) for r in range(n_row) for k in range(PANELS, n_col)])
+        for bit in (6, 2, 4)]
+    return [value, x, y, far]
+
+
 def land(came, p, *others):
     n_row = lax.axis_size("row")
     came = lax.optimization_barrier((*came, *others))
@@ -357,7 +366,7 @@
     w0 = call(first_kernel, "first", square, chain, 6.5, *one)
     blocks[0] = finish(last, w0)
     two = cross(*land(two, p, w0, blocks[0]))
-    top_own = launch(after(own, w0))
+    top_own = launch_beyond(after(own, w0))
     inverses, upper = call(
         rest_kernel, "rest",
         (jax.ShapeDtypeStruct((2, nb, nb), f32), jax.ShapeDtypeStruct((PANELS, nb, nb), f32)),

time: 79.6 us -> 82.6 us (1.038)
  the two profiles are of different devices: /device:TPU:13 before, /device:TPU:29 now
where the time goes in v7:
time: 82.6 us; the launch traced here: 82.3 us
  starting transfers between devices  27.8 us (34%)
  Pallas kernels  25.3 us (31%)
  waiting for transfers between devices  24.8 us (30%)
  local copies, waits for them, and re-layouts  2.25 us (3%)
  other arithmetic  1.81 us (2%)
    pallas_call x3, Pallas kernels, call(): pl.pallas_call(body, out_shape=outs, in_specs=[smem] + [vmem] * len(opera...  25.3 us
    ppermute x14, starting transfers between devices, swap(): return lax.ppermute(value, axis, [(i, i ^ bit) for i in range(n)])  14.1 us
    ppermute x14, waiting for transfers between devices, swap(): return lax.ppermute(value, axis, [(i, i ^ bit) for i in range(n)])  12.5 us
    ppermute x2, waiting for transfers between devices, along_col(): came = [lax.ppermute(value, 'col', steps_right(s, n_col))]  12.3 us
    ppermute x3, starting transfers between devices, launch_beyond(): lax.ppermute(value, ('row', 'col'), [(r * n_col + k, (r ^ bit) * n_col +...  8.54 us
    ppermute x2, starting transfers between devices, along_col(): came = [lax.ppermute(value, 'col', steps_right(s, n_col))]  2.57 us
  transfers between devices with their start and end apart: 22, of which 9 were waited for; matrix products, arithmetic and copies ran while one was open for 2% of the time, Pallas kernels for 25%

profile of v7, /device:TPU:29, one launch (start us, length us, event | category | flops | bytes accessed | tf_op | source)
XLA Modules:
  0.0 82.3 jit_solution(6159152509930234358)
XLA Ops:
  0.0 1.6 %fusion.1 = (f32[1,256,1,256]{3,2,1,0:T(1,128)S(1)}, f32[1,256,1,256]{3,2,1,0:T(1,128)S(1)}) fusion(f32[1,256,2,256]{3,2,1,0:T(2,128)} %param.1), kind=kLoop, calls=%fused_computation.30 | loop fusion | bytes 1048576 | tf_op jit(solution)/shard_map/slice | solution.py:329
  1.7 1.3 %collective-permute-start = (f32[256,256]{1,0:T(8,128)S(1)}, f32[256,256]{1,0:T(8,128)S(1)}, u32[]{:S(2)}, u32[]{:S(2)}) collective-permute-start(f32[256,256]{1,0:T(8,128)S(1)} %bitcast.35), channel_id=1, source_target_pairs={{0,1},{1,2},{2,3},{4,5},{5,6},{6,7},{8,9},{9,10},{10,11},{12,13},{... | collective-permute-start | bytes 786440 | tf_op jit(solution)/shard_map/ppermute | solution.py:282
  3.0 0.7 collective-permute-start.1
  3.7 1.3 %collective-permute-start.2 = (f32[256,256]{1,0:T(8,128)S(1)}, f32[256,256]{1,0:T(8,128)S(1)}, u32[]{:S(2)}, u32[]{:S(2)}) collective-permute-start(f32[256,256]{1,0:T(8,128)S(1)} %bitcast.42), channel_id=1, source_target_pairs={{0,8},{4,12},{8,0},{12,4},{16,24},{20,28},{24,16},{28,20},{1,9},{5... | collective-permute-start | bytes 786440 | tf_op jit(solution)/shard_map/ppermute | solution.py:234
  5.2 5.6 %collective-permute-done = f32[256,256]{1,0:T(8,128)S(1)} collective-permute-done((f32[256,256]{1,0:T(8,128)S(1)}, f32[256,256]{1,0:T(8,128)S(1)}, u32[]{:S(2)}, u32[]{:S(2)}) %collective-permute-start) | collective-permute-done | bytes 262176 | tf_op jit(solution)/shard_map/ppermute | solution.py:282
  10.9 0.9 %collective-permute-done.3 = f32[256,256]{1,0:T(8,128)S(1)} collective-permute-done((f32[256,256]{1,0:T(8,128)S(1)}, f32[256,256]{1,0:T(8,128)S(1)}, u32[]{:S(2)}, u32[]{:S(2)}) %collective-permute-start.3) | collective-permute-done | bytes 262176 | tf_op jit(solution)/shard_map/ppermute | solution.py:234
  11.8 1.3 %collective-permute-start.4 = (f32[256,256]{1,0:T(8,128)S(1)}, f32[256,256]{1,0:T(8,128)S(1)}, u32[]{:S(2)}, u32[]{:S(2)}) collective-permute-start(f32[256,256]{1,0:T(8,128)S(1)} %collective-permute-done), channel_id=1, source_target_pairs={{1,2},{2,3},{5,6},{6,7},{9,10},{10,11},{13,14},{14,15},{17,18},{18... | collective-permute-start | bytes 786440 | tf_op jit(solution)/shard_map/ppermute | solution.py:282
  13.1 0.7 collective-permute-start.5
  13.8 0.4 collective-permute-start.6
  14.2 6.7 %collective-permute-done.4 = f32[256,256]{1,0:T(8,128)S(1)} collective-permute-done((f32[256,256]{1,0:T(8,128)S(1)}, f32[256,256]{1,0:T(8,128)S(1)}, u32[]{:S(2)}, u32[]{:S(2)}) %collective-permute-start.4) | collective-permute-done | bytes 262176 | tf_op jit(solution)/shard_map/ppermute | solution.py:282
  21.1 0.6 copy-done
  21.7 3.0 %collective-permute-start.7 = (f32[3,128,256]{2,1,0:T(8,128)S(1)}, f32[3,128,256]{2,1,0:T(8,128)S(1)}, u32[]{:S(2)}, u32[]{:S(2)}) collective-permute-start(f32[3,128,256]{2,1,0:T(8,128)S(1)} %select_bitcast_fusion), channel_id=1, source_target_pairs={{0,4},{4,0},{8,12},{12,8},{16,20},{20,16},{24,28},{28,24},{1,5},{5... | collective-permute-start | bytes 1179656 | tf_op jit(solution)/shard_map/ppermute | solution.py:234
  24.8 1.0 %select_select_fusion.5 = (f32[256,256]{1,0:T(8,128)S(1)}, f32[256,256]{1,0:T(8,128)S(1)}) fusion(f32[256,256]{1,0:T(8,128)S(1)} %bitcast.44, f32[256,256]{1,0:T(8,128)S(1)} %collective-permute-done.2, f32[256,256]{1,0:T(8,128)S(1)} %collective-permute-done.3, f32[256,256]{1,0:T(8,128)} %collective-permute-done.6, pred[]{:T(512)S(6)} %eq.38, pred[]{:T(512)S(6)} %eq.37, ...), kind=kLoop, calls=%fused_computation.15 | loop fusion | flops 393216 | bytes 1572870 | tf_op jit(solution)/shard_map/jit(_where)/select_n | solution.py:261
  26.3 0.3 collective-permute-start.12
  26.6 0.6 collective-permute-start.13
  27.3 1.7 %collective-permute-start.10 = (f32[128,256]{1,0:T(8,128)S(1)}, f32[128,256]{1,0:T(8,128)S(1)}, u32[]{:S(2)}, u32[]{:S(2)}) collective-permute-start(f32[128,256]{1,0:T(8,128)S(1)} %get-tuple-element.44), channel_id=1, source_target_pairs={{0,24},{4,28},{8,16},{12,20},{16,8},{20,12},{24,0},{28,4},{1,25},{... | collective-permute-start | bytes 393224 | tf_op jit(solution)/shard_map/ppermute | solution.py:234
  29.0 0.3 collective-permute-start.8
  29.3 0.6 collective-permute-start.9
  29.9 6.7 %collective-permute-done.10 = f32[128,256]{1,0:T(8,128)S(1)} collective-permute-done((f32[128,256]{1,0:T(8,128)S(1)}, f32[128,256]{1,0:T(8,128)S(1)}, u32[]{:S(2)}, u32[]{:S(2)}) %collective-permute-start.10) | collective-permute-done | bytes 131104 | tf_op jit(solution)/shard_map/ppermute | solution.py:234
  36.7 2.9 %collective-permute-done.8 = f32[128,256]{1,0:T(8,128)S(1)} collective-permute-done((f32[128,256]{1,0:T(8,128)S(1)}, f32[128,256]{1,0:T(8,128)S(1)}, u32[]{:S(2)}, u32[]{:S(2)}) %collective-permute-start.8) | collective-permute-done | bytes 131104 | tf_op jit(solution)/shard_map/ppermute | solution.py:234
  39.6 1.5 %collective-permute-start.15 = (f32[256,256]{1,0:T(8,128)S(1)}, f32[256,256]{1,0:T(8,128)S(1)}, u32[]{:S(2)}, u32[]{:S(2)}) collective-permute-start(f32[256,256]{1,0:T(8,128)S(1)} %pad_maximum_fusion.5.mine_ref.refs_0_), channel_id=1, source_target_pairs={{0,4},{4,0},{8,12},{12,8},{16,20},{20,16},{24,28},{28,24},{1,5},{5... | collective-permute-start | bytes 786440 | tf_op jit(solution)/shard_map/ppermute | solution.py:234
  41.1 1.3 %collective-permute-start.14 = (f32[256,256]{1,0:T(8,128)S(1)}, f32[256,256]{1,0:T(8,128)S(1)}, u32[]{:S(2)}, u32[]{:S(2)}) collective-permute-start(f32[256,256]{1,0:T(8,128)S(1)} %copy-done.1), channel_id=1, source_target_pairs={{2,3},{6,7},{10,11},{14,15},{18,19},{22,23},{26,27},{30,31}} | collective-permute-start | bytes 786440 | tf_op jit(solution)/shard_map/ppermute | solution.py:308
  42.4 1.2 %collective-permute-start.16 = (f32[256,256]{1,0:T(8,128)S(1)}, f32[256,256]{1,0:T(8,128)S(1)}, u32[]{:S(2)}, u32[]{:S(2)}) collective-permute-start(f32[256,256]{1,0:T(8,128)S(1)} %pad_maximum_fusion.4), channel_id=1, source_target_pairs={{0,24},{4,28},{8,16},{12,20},{16,8},{20,12},{24,0},{28,4},{1,25},{... | collective-permute-start | bytes 786440 | tf_op jit(solution)/shard_map/ppermute | solution.py:234
  43.7 6.5 %first.1.w0_ref = f32[256,256]{1,0:T(8,128)S(1)} custom-call(s32[2]{0:T(128)S(1)} %pad_add_fusion.place, f32[256,256]{1,0:T(8,128)S(1)} %pad_maximum_fusion.5.mine_ref.refs_0_, f32[256,256]{1,0:T(8,128)S(1)} %collective-permute-done.15.other_ref.refs_1_), custom_call_target="tpu_custom_call" | custom-call | bytes 22750000 | tf_op jit(solution)/shard_map/first/pallas_call | solution.py:337
  50.5 1.8 %collective-permute-start.17 = (f32[512,256]{1,0:T(8,128)S(1)}, f32[512,256]{1,0:T(8,128)S(1)}, u32[]{:S(2)}, u32[]{:S(2)}) collective-permute-start(f32[512,256]{1,0:T(8,128)S(1)} %pad_maximum_fusion.2.refs_2_), channel_id=1, source_target_pairs={{0,4},{4,0},{8,12},{12,8},{16,20},{20,16},{24,28},{28,24},{1,5},{5... | collective-permute-start | bytes 1572872 | tf_op jit(solution)/shard_map/ppermute | solution.py:234
  52.3 3.1 %collective-permute-start.18 = (f32[256,256]{1,0:T(8,128)S(1)}, f32[256,256]{1,0:T(8,128)S(1)}, u32[]{:S(2)}, u32[]{:S(2)}) collective-permute-start(f32[256,256]{1,0:T(8,128)S(1)} %bitcast.37), channel_id=1, source_target_pairs={{3,11},{7,15},{11,3},{15,7},{19,27},{23,31},{27,19},{31,23}} | collective-permute-start | bytes 786440 | tf_op jit(solution)/shard_map/ppermute | solution.py:249
  55.4 2.1 %collective-permute-start.19 = (f32[256,256]{1,0:T(8,128)S(1)}, f32[256,256]{1,0:T(8,128)S(1)}, u32[]{:S(2)}, u32[]{:S(2)}) collective-permute-start(f32[256,256]{1,0:T(8,128)S(1)} %bitcast.38), channel_id=1, source_target_pairs={{3,19},{7,23},{11,27},{15,31},{19,3},{23,7},{27,11},{31,15}} | collective-permute-start | bytes 786440 | tf_op jit(solution)/shard_map/ppermute | solution.py:249
  57.5 3.3 %collective-permute-start.20 = (f32[256,256]{1,0:T(8,128)S(1)}, f32[256,256]{1,0:T(8,128)S(1)}, u32[]{:S(2)}, u32[]{:S(2)}) collective-permute-start(f32[256,256]{1,0:T(8,128)S(1)} %bitcast.39), channel_id=1, source_target_pairs={{3,27},{7,31},{11,19},{15,23},{19,11},{23,15},{27,3},{31,7}} | collective-permute-start | bytes 786440 | tf_op jit(solution)/shard_map/ppermute | solution.py:249
  60.9 13.8 %rest.1 = (f32[2,256,256]{2,1,0:T(8,128)S(1)}, f32[3,256,256]{2,1,0:T(8,128)S(1)}) custom-call(s32[2]{0:T(128)S(1)} %pad_add_fusion.place, f32[256,256]{1,0:T(8,128)S(1)} %first.1.w0_ref, f32[256,256]{1,0:T(8,128)S(1)} %pad_maximum_fusion.5.mine_ref.refs_0_, f32[256,256]{1,0:T(8,128)S(1)} %collective-permute-done.15.other_ref.refs_1_, ...), custom_call_target="tpu_custom_call" | custom-call | bytes 52500000 | tf_op jit(solution)/shard_map/rest/pallas_call | solution.py:337
  74.8 0.9 %collective-permute-start.21 = (f32[512,256]{1,0:T(8,128)S(1)}, f32[512,256]{1,0:T(8,128)S(1)}, u32[]{:S(2)}, u32[]{:S(2)}) collective-permute-start(f32[512,256]{1,0:T(8,128)S(1)} %pad_maximum_fusion.3.refs_2_), channel_id=1, source_target_pairs={{0,4},{4,0},{8,12},{12,8},{16,20},{20,16},{24,28},{28,24},{1,5},{5... | collective-permute-start | bytes 1572872 | tf_op jit(solution)/shard_map/ppermute | solution.py:234
  75.7 1.5 %collective-permute-done.21.refs_3_ = f32[512,256]{1,0:T(8,128)S(1)} collective-permute-done((f32[512,256]{1,0:T(8,128)S(1)}, f32[512,256]{1,0:T(8,128)S(1)}, u32[]{:S(2)}, u32[]{:S(2)}) %collective-permute-start.21) | collective-permute-done | bytes 524320 | tf_op jit(solution)/shard_map/ppermute | solution.py:234
  77.3 5.0 %apply.1 = f32[1,256,2,256]{3,2,1,0:T(2,128)} custom-call(s32[2]{0:T(128)S(1)} %pad_add_fusion.place, f32[256,256]{1,0:T(8,128)S(1)} %bitcast.41, f32[256,256]{1,0:T(8,128)S(1)} %bitcast.45, f32[256,256]{1,0:T(8,128)S(1)} %broadcast_select_fusion.1.b0_ref, f32[256,256]{1,0:T(8,128)S(1)} %get-tuple-element.65.b1_ref, ...), custom_call_target="tpu_custom_call" | custom-call | bytes 21000000 | tf_op jit(solution)/shard_map/apply/pallas_call | solution.py:337
  (38 shorter events, 1.7 us)
Async XLA Ops:
  1.7 9.1 %collective-permute-start = (f32[256,256]{1,0:T(8,128)S(1)}, f32[256,256]{1,0:T(8,128)S(1)}, u32[]{:S(2)}, u32[]{:S(2)}) collective-permute-start(f32[256,256]{1,0:T(8,128)S(1)} %bitcast.35), channel_id=1, source_target_pairs={{0,1},{1,2},{2,3},{4,5},{5,6},{6,7},{8,9},{9,10},{10,11},{12,13},{... | collective-permute-start | bytes 786440 | tf_op jit(solution)/shard_map/ppermute | solution.py:282
  3.0 7.8 %collective-permute-start.1 = (f32[256,256]{1,0:T(8,128)S(1)}, f32[256,256]{1,0:T(8,128)S(1)}, u32[]{:S(2)}, u32[]{:S(2)}) collective-permute-start(f32[256,256]{1,0:T(8,128)S(1)} %bitcast.36), channel_id=1, source_target_pairs={{1,0},{2,1},{5,4},{6,5},{9,8},{10,9},{13,12},{14,13},{17,16},{18,1... | collective-permute-start | bytes 786440 | tf_op jit(solution)/shard_map/ppermute | solution.py:287
  3.7 7.2 %collective-permute-start.2 = (f32[256,256]{1,0:T(8,128)S(1)}, f32[256,256]{1,0:T(8,128)S(1)}, u32[]{:S(2)}, u32[]{:S(2)}) collective-permute-start(f32[256,256]{1,0:T(8,128)S(1)} %bitcast.42), channel_id=1, source_target_pairs={{0,8},{4,12},{8,0},{12,4},{16,24},{20,28},{24,16},{28,20},{1,9},{5... | collective-permute-start | bytes 786440 | tf_op jit(solution)/shard_map/ppermute | solution.py:234
  5.0 6.9 %collective-permute-start.3 = (f32[256,256]{1,0:T(8,128)S(1)}, f32[256,256]{1,0:T(8,128)S(1)}, u32[]{:S(2)}, u32[]{:S(2)}) collective-permute-start(f32[256,256]{1,0:T(8,128)S(1)} %bitcast.43), channel_id=1, source_target_pairs={{0,16},{4,20},{8,24},{12,28},{16,0},{20,4},{24,8},{28,12},{1,17},{... | collective-permute-start | bytes 786440 | tf_op jit(solution)/shard_map/ppermute | solution.py:234
  11.8 9.1 %collective-permute-start.4 = (f32[256,256]{1,0:T(8,128)S(1)}, f32[256,256]{1,0:T(8,128)S(1)}, u32[]{:S(2)}, u32[]{:S(2)}) collective-permute-start(f32[256,256]{1,0:T(8,128)S(1)} %collective-permute-done), channel_id=1, source_target_pairs={{1,2},{2,3},{5,6},{6,7},{9,10},{10,11},{13,14},{14,15},{17,18},{18... | collective-permute-start | bytes 786440 | tf_op jit(solution)/shard_map/ppermute | solution.py:282
  13.1 7.8 %collective-permute-start.5 = (f32[256,256]{1,0:T(8,128)S(1)}, f32[256,256]{1,0:T(8,128)S(1)}, u32[]{:S(2)}, u32[]{:S(2)}) collective-permute-start(f32[256,256]{1,0:T(8,128)S(1)} %collective-permute-done.1), channel_id=1, source_target_pairs={{1,0},{5,4},{9,8},{13,12},{17,16},{21,20},{25,24},{29,28}} | collective-permute-start | bytes 786440 | tf_op jit(solution)/shard_map/ppermute | solution.py:287
  13.8 7.1 %collective-permute-start.6 = (f32[256,256]{1,0:T(8,128)S(1)}, f32[256,256]{1,0:T(8,128)}, u32[]{:S(2)}, u32[]{:S(2)}) collective-permute-start(f32[256,256]{1,0:T(8,128)S(1)} %collective-permute-done.3), channel_id=1, source_target_pairs={{0,8},{4,12},{8,0},{12,4},{16,24},{20,28},{24,16},{28,20},{1,9},{5... | collective-permute-start | bytes 786440 | tf_op jit(solution)/shard_map/ppermute | solution.py:234
  20.9 0.7 copy-start
  21.7 4.4 %collective-permute-start.7 = (f32[3,128,256]{2,1,0:T(8,128)S(1)}, f32[3,128,256]{2,1,0:T(8,128)S(1)}, u32[]{:S(2)}, u32[]{:S(2)}) collective-permute-start(f32[3,128,256]{2,1,0:T(8,128)S(1)} %select_bitcast_fusion), channel_id=1, source_target_pairs={{0,4},{4,0},{8,12},{12,8},{16,20},{20,16},{24,28},{28,24},{1,5},{5... | collective-permute-start | bytes 1179656 | tf_op jit(solution)/shard_map/ppermute | solution.py:234
  25.8 3.4 %collective-permute-start.11 = (f32[512,256]{1,0:T(8,128)S(1)}, f32[512,256]{1,0:T(8,128)S(1)}, u32[]{:S(2)}, u32[]{:S(2)}) collective-permute-start(f32[512,256]{1,0:T(8,128)S(1)} %pad_maximum_fusion.1.refs_0_), channel_id=1, source_target_pairs={{0,4},{4,0},{8,12},{12,8},{16,20},{20,16},{24,28},{28,24},{1,5},{5... | collective-permute-start | bytes 1572872 | tf_op jit(solution)/shard_map/ppermute | solution.py:234
  26.3 13.3 %collective-permute-start.12 = (f32[256,256]{1,0:T(8,128)S(1)}, f32[256,256]{1,0:T(8,128)S(1)}, u32[]{:S(2)}, u32[]{:S(2)}) collective-permute-start(f32[256,256]{1,0:T(8,128)S(1)} %pad_maximum_fusion.4), channel_id=1, source_target_pairs={{0,8},{4,12},{8,0},{12,4},{16,24},{20,28},{24,16},{28,20},{1,9},{5... | collective-permute-start | bytes 786440 | tf_op jit(solution)/shard_map/ppermute | solution.py:234
  26.6 12.9 %collective-permute-start.13 = (f32[256,256]{1,0:T(8,128)S(1)}, f32[256,256]{1,0:T(8,128)S(1)}, u32[]{:S(2)}, u32[]{:S(2)}) collective-permute-start(f32[256,256]{1,0:T(8,128)S(1)} %pad_maximum_fusion.4), channel_id=1, source_target_pairs={{0,16},{4,20},{8,24},{12,28},{16,0},{20,4},{24,8},{28,12},{1,17},{... | collective-permute-start | bytes 786440 | tf_op jit(solution)/shard_map/ppermute | solution.py:234
  27.3 9.4 %collective-permute-start.10 = (f32[128,256]{1,0:T(8,128)S(1)}, f32[128,256]{1,0:T(8,128)S(1)}, u32[]{:S(2)}, u32[]{:S(2)}) collective-permute-start(f32[128,256]{1,0:T(8,128)S(1)} %get-tuple-element.44), channel_id=1, source_target_pairs={{0,24},{4,28},{8,16},{12,20},{16,8},{20,12},{24,0},{28,4},{1,25},{... | collective-permute-start | bytes 393224 | tf_op jit(solution)/shard_map/ppermute | solution.py:234
  29.0 10.5 %collective-permute-start.8 = (f32[128,256]{1,0:T(8,128)S(1)}, f32[128,256]{1,0:T(8,128)S(1)}, u32[]{:S(2)}, u32[]{:S(2)}) collective-permute-start(f32[128,256]{1,0:T(8,128)S(1)} %get-tuple-element.44), channel_id=1, source_target_pairs={{0,8},{4,12},{8,0},{12,4},{16,24},{20,28},{24,16},{28,20},{1,9},{5... | collective-permute-start | bytes 393224 | tf_op jit(solution)/shard_map/ppermute | solution.py:234
  29.3 10.2 %collective-permute-start.9 = (f32[128,256]{1,0:T(8,128)S(1)}, f32[128,256]{1,0:T(8,128)S(1)}, u32[]{:S(2)}, u32[]{:S(2)}) collective-permute-start(f32[128,256]{1,0:T(8,128)S(1)} %get-tuple-element.44), channel_id=1, source_target_pairs={{0,16},{4,20},{8,24},{12,28},{16,0},{20,4},{24,8},{28,12},{1,17},{... | collective-permute-start | bytes 393224 | tf_op jit(solution)/shard_map/ppermute | solution.py:234
  39.6 1.5 %copy-start.1 = (f32[256,256]{1,0:T(8,128)S(1)}, f32[256,256]{1,0:T(8,128)}, u32[]{:S(2)}) copy-start(f32[256,256]{1,0:T(8,128)} %copy-done) | copy-start | bytes 786436
  39.6 4.1 %collective-permute-start.15 = (f32[256,256]{1,0:T(8,128)S(1)}, f32[256,256]{1,0:T(8,128)S(1)}, u32[]{:S(2)}, u32[]{:S(2)}) collective-permute-start(f32[256,256]{1,0:T(8,128)S(1)} %pad_maximum_fusion.5.mine_ref.refs_0_), channel_id=1, source_target_pairs={{0,4},{4,0},{8,12},{12,8},{16,20},{20,16},{24,28},{28,24},{1,5},{5... | collective-permute-start | bytes 786440 | tf_op jit(solution)/shard_map/ppermute | solution.py:234
  41.1 9.1 %collective-permute-start.14 = (f32[256,256]{1,0:T(8,128)S(1)}, f32[256,256]{1,0:T(8,128)S(1)}, u32[]{:S(2)}, u32[]{:S(2)}) collective-permute-start(f32[256,256]{1,0:T(8,128)S(1)} %copy-done.1), channel_id=1, source_target_pairs={{2,3},{6,7},{10,11},{14,15},{18,19},{22,23},{26,27},{30,31}} | collective-permute-start | bytes 786440 | tf_op jit(solution)/shard_map/ppermute | solution.py:308
  42.4 7.9 %collective-permute-start.16 = (f32[256,256]{1,0:T(8,128)S(1)}, f32[256,256]{1,0:T(8,128)S(1)}, u32[]{:S(2)}, u32[]{:S(2)}) collective-permute-start(f32[256,256]{1,0:T(8,128)S(1)} %pad_maximum_fusion.4), channel_id=1, source_target_pairs={{0,24},{4,28},{8,16},{12,20},{16,8},{20,12},{24,0},{28,4},{1,25},{... | collective-permute-start | bytes 786440 | tf_op jit(solution)/shard_map/ppermute | solution.py:234
  50.5 10.4 %collective-permute-start.17 = (f32[512,256]{1,0:T(8,128)S(1)}, f32[512,256]{1,0:T(8,128)S(1)}, u32[]{:S(2)}, u32[]{:S(2)}) collective-permute-start(f32[512,256]{1,0:T(8,128)S(1)} %pad_maximum_fusion.2.refs_2_), channel_id=1, source_target_pairs={{0,4},{4,0},{8,12},{12,8},{16,20},{20,16},{24,28},{28,24},{1,5},{5... | collective-permute-start | bytes 1572872 | tf_op jit(solution)/shard_map/ppermute | solution.py:234
  52.3 22.4 %collective-permute-start.18 = (f32[256,256]{1,0:T(8,128)S(1)}, f32[256,256]{1,0:T(8,128)S(1)}, u32[]{:S(2)}, u32[]{:S(2)}) collective-permute-start(f32[256,256]{1,0:T(8,128)S(1)} %bitcast.37), channel_id=1, source_target_pairs={{3,11},{7,15},{11,3},{15,7},{19,27},{23,31},{27,19},{31,23}} | collective-permute-start | bytes 786440 | tf_op jit(solution)/shard_map/ppermute | solution.py:249
  55.4 19.3 %collective-permute-start.19 = (f32[256,256]{1,0:T(8,128)S(1)}, f32[256,256]{1,0:T(8,128)S(1)}, u32[]{:S(2)}, u32[]{:S(2)}) collective-permute-start(f32[256,256]{1,0:T(8,128)S(1)} %bitcast.38), channel_id=1, source_target_pairs={{3,19},{7,23},{11,27},{15,31},{19,3},{23,7},{27,11},{31,15}} | collective-permute-start | bytes 786440 | tf_op jit(solution)/shard_map/ppermute | solution.py:249
  57.5 17.2 %collective-permute-start.20 = (f32[256,256]{1,0:T(8,128)S(1)}, f32[256,256]{1,0:T(8,128)S(1)}, u32[]{:S(2)}, u32[]{:S(2)}) collective-permute-start(f32[256,256]{1,0:T(8,128)S(1)} %bitcast.39), channel_id=1, source_target_pairs={{3,27},{7,31},{11,19},{15,23},{19,11},{23,15},{27,3},{31,7}} | collective-permute-start | bytes 786440 | tf_op jit(solution)/shard_map/ppermute | solution.py:249
  74.8 2.5 %collective-permute-start.21 = (f32[512,256]{1,0:T(8,128)S(1)}, f32[512,256]{1,0:T(8,128)S(1)}, u32[]{:S(2)}, u32[]{:S(2)}) collective-permute-start(f32[512,256]{1,0:T(8,128)S(1)} %pad_maximum_fusion.3.refs_2_), channel_id=1, source_target_pairs={{0,4},{4,0},{8,12},{12,8},{16,20},{20,16},{24,28},{28,24},{1,5},{5... | collective-permute-start | bytes 1572872 | tf_op jit(solution)/shard_map/ppermute | solution.py:234
